TPU v7x, 32 devices: a whole 2x2x4 slice. The times are simulated.
32 devices in a mesh: bulk: 8 (over z, y), rep: 4 (over x, core).
Axes of the slice: x: 2, y: 2, z: 4, core: 2. Of those that a mesh axis runs over, the one named last changes fastest.
Arguments:
- orbitals: float32 [1024, 2048], P('rep', 'bulk'), may hold values from -6 to 6
- triangles: float32 [1024, 1024], P('rep', 'bulk'), may hold values from -0.09375 to 0.09375
- coupling: float32 [1024, 1024], P('rep', 'bulk'), may hold values from -0.09375 to 0.09375
- diagonals: float32 [2, 1024], P(None, 'bulk'), may hold values from 1 to 2
Outputs:
- solved: float32 [1024, 2048], P(('rep', 'bulk'))
All inputs are finite; a program needn't handle non-finite values.
Results may differ from a plain program's by a relative error of at most 0.000084.
Values sent between devices are 32-bit elements; how exact they have to be, the bound alone decides.
No kernel may reach another device: no remote copies, remote signals or barrier semaphores. Data moves between devices by JAX's collectives and lax.ppermute only.
A program may use at most 64 MiB of HBM per device.

v0:
```python
import jax
import jax.numpy as jnp
from jax import lax
from jax.experimental import pallas as pl
from jax.experimental.pallas import tpu as pltpu
from jax.sharding import PartitionSpec as P

F32 = jnp.float32
BF16 = jnp.bfloat16
NN = (((1,), (0,)), ((), ()))
NT = (((1,), (1,)), ((), ()))


def unpack(triangles, diagonals):
    first_block = jnp.tril(triangles, -1) + jnp.diag(diagonals[0])
    second_block = jnp.tril(triangles.T, -1) + jnp.diag(diagonals[1])
    return (first_block, second_block)


def per_device_any(orbitals, triangles, coupling, diagonals):
    tri_rows, couple_rows = (
        lax.all_gather(triangles, "rep", axis=0, tiled=True),
        lax.all_gather(coupling, "rep", axis=0, tiled=True),
    )
    tri_whole, couple_whole, diag_whole = (
        lax.all_gather(tri_rows, "bulk", axis=1, tiled=True),
        lax.all_gather(couple_rows, "bulk", axis=1, tiled=True),
        lax.all_gather(diagonals, "bulk", axis=1, tiled=True),
    )
    first_block, second_block = unpack(tri_whole, diag_whole)
    panel = first_block.shape[0]
    groups = lax.axis_size("bulk")
    local_rows = orbitals.shape[0] // groups
    blocks = orbitals.reshape(groups, local_rows, orbitals.shape[1])
    received = lax.all_to_all(blocks, "bulk", split_axis=0, concat_axis=2, tiled=True)
    rows_now = received.reshape(local_rows, received.shape[2])
    left_part = rows_now[:, :panel]
    right_part = rows_now[:, panel:]
    solved_one = jax.scipy.linalg.solve_triangular(first_block, left_part.T, lower=True).T
    update = jnp.dot(
        solved_one,
        couple_whole.T,
        precision=lax.Precision.HIGHEST,
        preferred_element_type=jnp.float32,
    )
    solved_two = jax.scipy.linalg.solve_triangular(
        second_block, (right_part - update).T, lower=True
    ).T
    return jnp.concatenate([solved_one, solved_two], axis=1)


def dot(a, b, dims=NN):
    return lax.dot_general(a, b, dims, preferred_element_type=F32)


def dot_exact(a, b):
    return lax.dot_general(a, b, NN, precision=lax.Precision.HIGHEST, preferred_element_type=F32)


def split(x):
    high = x.astype(BF16)
    return high, (x - high.astype(F32)).astype(BF16)


def mul(x, b, dims=NN):
    xh, xl = split(x)
    bh, bl = b
    m = x.shape[0]
    both = dot(jnp.concatenate([xh, xl], axis=0), bh, dims)
    return (both[:m] + both[m:]) + dot(xh, bl, dims)


def mul3(a, b):
    (ah, al), (bh, bl) = split(a), split(b)
    return dot(ah, bh) + (dot(al, bh) + dot(ah, bl))


def iotas(n):
    return lax.broadcasted_iota(jnp.int32, (n, n), 0), lax.broadcasted_iota(jnp.int32, (n, n), 1)


def invert_kernel(place_ref, tri_ref, diag_ref, t_ref):
    rep, bulk = place_ref[0], place_ref[1]
    rows, n = tri_ref.shape
    inv = 1.0 / diag_ref[...]
    t_ref[0:rows, :] = tri_ref[...]
    t_ref[rows : rows + 8, :] = jnp.concatenate([inv, jnp.zeros((6, n), F32)], axis=0)

    @pl.when(rep == bulk // 2)
    def _():
        start = pl.multiple_of((bulk % 2) * n, n)
        block = tri_ref[pl.ds(start, n), :]
        i, j = iotas(n)
        eye = i == j
        ans = []
        for which in range(2):
            row, col = (i, j) if which == 0 else (j, i)
            along = inv[which : which + 1, :]
            d = jnp.where(eye, along, 0.0)
            down = jnp.sum(d, axis=1, keepdims=True)
            part = (row >> 1 == col >> 1) & (row > col)
            ans.append(d - jnp.where(part, block * along * down, 0.0))
        level = 1
        while (1 << level) < n:
            for which in range(2):
                row, col = (i, j) if which == 0 else (j, i)
                part = (row >> (level + 1) == col >> (level + 1)) & (row >> level > col >> level)
                t = ans[which]
                ans[which] = t - mul3(mul3(t, jnp.where(part, block, 0.0)), t)
            level += 1
        t_ref[pl.ds(start, n), :] = jnp.where(i >= j, ans[0], ans[1])


def leave_kernel(place_ref, orb, out):
    y = place_ref[1] & 1
    for k in range(4):
        out[k] = orb[k, 1 - y]


def spread_kernel(place_ref, orb, came, b1, b2, b3):
    z, y = place_ref[1] >> 1, place_ref[1] & 1
    for m, ref in ((1, b1), (2, b2), (3, b3)):
        ref[0] = orb[z ^ m, y]
        ref[1] = came[z ^ m]


def rows_kernel(place_ref, orb, came, b1, b2, b3, left, both):
    z, y = place_ref[1] >> 1, place_ref[1] & 1

    def put(m, dy, value):
        k = 2 * (z ^ m) + (y ^ dy)
        both[k >> 2, :, pl.ds(pl.multiple_of((k & 3) * 256, 256), 256)] = value

    put(0, 0, orb[z, y])
    put(0, 1, came[z])
    for m, ref in ((1, b1), (2, b2), (3, b3)):
        put(m, 0, ref[0])
        put(m, 1, ref[1])
    left[...] = both[0]


def origin(place_ref, crossed, first, second, m):
    rep, bulk = place_ref[0], place_ref[1]
    if m < 2:
        dx, dy = second, first
    else:
        core = (rep & 1) ^ crossed
        dx = jnp.where(core == 0, first, second)
        dy = jnp.where(core == 0, second, first)
    return rep ^ (2 * dx + crossed), bulk ^ (2 * m + dy)


def pieces(bufs):
    found = []
    for crossed in range(2):
        for m in range(4):
            for second in range(2):
                for first in range(2):
                    buf = bufs[8 * crossed + 4 * (m // 2) + 2 * second + first]
                    found.append((buf.at[m % 2], (crossed, first, second, m)))
    return found


def offset(index, size):
    return pl.ds(pl.multiple_of(index * size, size), size)


def place_pieces(place_ref, bufs, upper, high, low, diag):
    for piece, args in pieces(bufs):
        rep, bulk = origin(place_ref, *args)

        @pl.when((rep <= bulk // 2) if upper else (rep >= bulk // 2))
        def _():
            h, l = split(piece[0:256, :])
            high[offset(rep, 256), offset(bulk, 128)] = h
            low[offset(rep, 256), offset(bulk, 128)] = l

        @pl.when(rep == bulk // 2)
        def _():
            diag[bulk, 0:128, :] = piece[pl.ds(pl.multiple_of((bulk % 2) * 128, 128), 128), :]
            diag[bulk, 128:136, :] = piece[256:264, :]


def mul_pairs(a, b):
    (ah, al), (bh, bl) = a, b
    return dot(ah, bh) + (dot(al, bh) + dot(ah, bl))


def pair_of(high, low, r, c, size):
    rows, cols = slice(r, r + size), slice(c, c + size)
    return high[rows, cols], low[rows, cols]


def join(a, b, c, d):
    return jnp.concatenate([jnp.concatenate([a, b], axis=1), jnp.concatenate([c, d], axis=1)], axis=0)


def first_kernel(place_ref, pair, other_pair, *refs):
    bufs, (x_ref, high, low, diag) = refs[:16], refs[16:]
    place_pieces(place_ref, bufs, False, high, low, diag)
    n = 128
    i, j = iotas(n)

    def block(k):
        return jnp.where(i > j, diag[k, 0:n, :], 0.0) + jnp.where(i == j, diag[k, n : n + 1, :], 0.0)

    zero = jnp.zeros((n, n), F32)
    inverses = []
    for k in range(4):
        ta, tb = block(2 * k), block(2 * k + 1)
        pa, pb = split(ta), split(tb)
        off = -mul_pairs(split(mul_pairs(pb, pair_of(high, low, 256 * k + n, 256 * k, n))), pa)
        inverses.append(split(join(ta, zero, off, tb)))

    rest = jnp.concatenate([pair[0], pair[1], other_pair[0], other_pair[1]], axis=0)
    for k in range(4):
        x = mul(rest[:, :256], inverses[k], NT)
        x_ref[:, k * 256 : (k + 1) * 256] = x
        if k < 3:
            rows, cols = slice((k + 1) * 256, 1024), slice(k * 256, (k + 1) * 256)
            rest = rest[:, 256:] - mul(x, (high[rows, cols], low[rows, cols]), NT)


def update_kernel(place_ref, x_ref, *refs):
    held, outs, (high, low) = refs[:4], refs[4:8], refs[8:]
    bulk = place_ref[1]
    for dy in range(2):
        for m in range(4):
            h, l = split(held[2 * dy + m // 2][m % 2])
            high[:, offset(bulk ^ (2 * m + dy), 128)] = h
            low[:, offset(bulk ^ (2 * m + dy), 128)] = l
    upd = mul(x_ref[...], (high[...], low[...]), NT)
    for k, out in enumerate(outs):
        out[...] = upd[32 * k : 32 * (k + 1)]


def second_factor_kernel(place_ref, *refs):
    bufs, (high, low, diag) = refs[:16], refs[16:]
    place_pieces(place_ref, bufs, True, high, low, diag)
    n = 128
    i, j = iotas(n)

    def block(k):
        return jnp.where(i < j, diag[k, 0:n, :], 0.0) + jnp.where(i == j, diag[k, n + 1 : n + 2, :], 0.0)

    zero = jnp.zeros((n, n), F32)
    inverses = []
    for k in range(4):
        ta, tb = block(2 * k), block(2 * k + 1)
        pa, pb = split(ta), split(tb)
        off = -mul_pairs(split(mul_pairs(pa, pair_of(high, low, 256 * k, 256 * k + n, n))), pb)
        inverses.append(split(join(ta, off, zero, tb)))

    def put(r, c, value):
        high[r : r + 256, c : c + 256], low[r : r + 256, c : c + 256] = value

    for k in range(2):
        at = 512 * k
        pa, pb = inverses[2 * k], inverses[2 * k + 1]
        off = -mul_pairs(split(mul_pairs(pa, pair_of(high, low, at, at + 256, 256))), pb)
        put(at, at, pa)
        put(at + 256, at + 256, pb)
        put(at, at + 256, split(off))
        put(at + 256, at, (jnp.zeros((256, 256), BF16),) * 2)


def second_kernel(place_ref, x_ref, both_ref, uh_ref, ul_ref, mine, from_x, from_core, from_both, out_ref):
    x = x_ref[0:32, :]
    out_ref[:, 0:1024] = x
    parts = []
    for k in range(4):
        way = place_ref[0] ^ k
        upd = jnp.where(
            way == 0,
            mine[...],
            jnp.where(way == 2, from_x[...], jnp.where(way == 1, from_core[...], from_both[...])),
        )
        parts.append(both_ref[1, :, k * 256 : (k + 1) * 256] - upd)
    ra = jnp.concatenate(parts[:2], axis=1)
    rb = jnp.concatenate(parts[2:], axis=1)

    def u(r, c):
        rows, cols = slice(r * 512, r * 512 + 512), slice(c * 512, c * 512 + 512)
        return uh_ref[rows, cols], ul_ref[rows, cols]

    xa = mul(ra, u(0, 0))
    xb = mul(rb - mul(xa, u(0, 1)), u(1, 1))
    out_ref[:, 1024:1536] = xa
    out_ref[:, 1536:2048] = xb


BOTH = ("bulk", "rep")

SPREAD, INVERT, LEAVE, ROWS, FIRST, SECOND = 1_000_000_000, 3_500_000_000, 500_000_000, 1_000_000_000, 200_000_000, 3_000_000_000


def swap_z(x, m):
    return lax.ppermute(x, "bulk", [(k, k ^ (2 * m)) for k in range(8)])


def swap_y(x):
    return lax.ppermute(x, "bulk", [(k, k ^ 1) for k in range(8)])


def swap_rep(x, bits):
    return lax.ppermute(x, "rep", [(k, k ^ bits) for k in range(4)])


def cross(x, stage):
    pairs = []
    for rep in range(4):
        for bulk in range(8):
            to = (rep ^ 2, bulk) if (rep & 1) == stage else (rep, bulk ^ 1)
            pairs.append((bulk * 4 + rep, to[1] * 4 + to[0]))
    return lax.ppermute(x, BOTH, pairs)


def after(x, *deps):
    return lax.optimization_barrier((x,) + deps)[0]


ANY = pl.BlockSpec(memory_space=pl.ANY)
VMEM = pl.BlockSpec(memory_space=pltpu.VMEM)
SMEM = pl.BlockSpec(memory_space=pltpu.SMEM)


def call(kernel, out, specs, outs, scratch, flops, size, name):
    return pl.pallas_call(
        kernel,
        out_shape=out,
        in_specs=specs,
        out_specs=outs,
        scratch_shapes=scratch,
        compiler_params=pltpu.CompilerParams(vmem_limit_bytes=size << 20),
        cost_estimate=pl.CostEstimate(flops=flops, bytes_accessed=2 << 20, transcendentals=0),
        name=name,
    )


def shape(*dims, dtype=F32):
    return jax.ShapeDtypeStruct(dims, dtype)


def per_device(orbitals, triangles, coupling, diagonals):
    rep, bulk = lax.axis_index("rep"), lax.axis_index("bulk")
    place = jnp.stack([rep, bulk]).astype(jnp.int32)
    blocks = orbitals.reshape(4, 2, 32, 256)

    t = call(invert_kernel, shape(264, 128), [SMEM, VMEM, VMEM], VMEM, [], INVERT, 4, "invert")(
        place, triangles, diagonals
    )
    coup = after(coupling, t)

    near = jnp.stack([t, swap_z(t, 1)])
    far = swap_z(near, 2)
    near0 = swap_y(near)
    near1 = swap_rep(near, 2)
    near01 = swap_rep(near0, 2)

    leave = call(leave_kernel, shape(4, 32, 256), [SMEM, VMEM], VMEM, [], LEAVE, 4, "leave")(place, blocks)
    came = swap_y(after(leave, t))
    c_near = jnp.stack([coupling, swap_z(coup, 1)])
    c_near_got = swap_y(c_near)

    far_now = after(far, near0, near1, came)
    far0 = cross(far_now, 0)
    far1 = cross(far_now, 1)
    b_out = call(spread_kernel, [shape(2, 32, 256)] * 3, [SMEM, VMEM, VMEM], [VMEM] * 3, [], SPREAD, 4, "spread")(
        place, blocks, came
    )
    b_z = [swap_z(after(b, far), m + 1) for m, b in enumerate(b_out)]
    c_far = swap_z(after(c_near, far), 2)
    c_far_got = swap_y(c_far)
    far01 = cross(after(far0, far1, near01), 1)

    left, both = call(
        rows_kernel,
        [shape(32, 1024), shape(2, 32, 1024)],
        [SMEM] + [VMEM] * 5,
        [VMEM] * 2,
        [],
        ROWS,
        4,
        "rows",
    )(place, blocks, came, *b_z)
    pair = jnp.stack([left, swap_rep(after(left, c_far), 2)])
    other_pair = swap_rep(after(pair, c_far), 1)
    bufs = [near, near0, near1, near01, far, far0, far1, far01]
    bufs += [swap_rep(b, 1) for b in bufs[:7]] + [swap_rep(after(far01, far1), 1)]

    scratch = [pltpu.VMEM((8, 136, 128), F32)]
    halves = [shape(1024, 1024, dtype=BF16)] * 2
    x = call(
        first_kernel,
        shape(128, 1024),
        [SMEM] + [VMEM] * 18,
        VMEM,
        [pltpu.VMEM((1024, 1024), BF16)] * 2 + scratch,
        FIRST,
        24,
        "first_panel",
    )(place, pair, after(other_pair, c_near_got), *bufs)

    mine, to_x, to_core, to_both = call(
        update_kernel,
        [shape(32, 256)] * 4,
        [SMEM] + [VMEM] * 5,
        [VMEM] * 4,
        [pltpu.VMEM((256, 1024), BF16)] * 2,
        2_000_000_000,
        24,
        "update",
    )(place, x, c_near, c_far, c_near_got, c_far_got)
    back = [swap_rep(to_x, 2), swap_rep(to_core, 1), swap_rep(to_both, 3)]

    uh, ul = call(
        second_factor_kernel, halves, [SMEM] + [VMEM] * 16, [VMEM] * 2, scratch, SECOND, 24, "second_factor"
    )(after(place, mine), *bufs)

    return call(second_kernel, shape(32, 2048), [SMEM] + [VMEM] * 8, VMEM, [], 2_500_000_000, 24, "second_panel")(
        place, x, both, uh, ul, mine, *back
    )


def solution(mesh):
    special = mesh.shape["bulk"] == 8 and mesh.shape["rep"] == 4

    def run(orbitals, triangles, coupling, diagonals):
        fits = orbitals.shape == (1024, 2048) and triangles.shape == (1024, 1024)
        body = per_device if special and fits else per_device_any
        return jax.shard_map(
            body,
            mesh=mesh,
            in_specs=(P("rep", "bulk"), P("rep", "bulk"), P("rep", "bulk"), P(None, "bulk")),
            out_specs=P(("rep", "bulk"), None),
            check_vma=False,
        )(orbitals, triangles, coupling, diagonals)

    return run
```

profile of v0, /device:TPU:0, one launch (start us, length us, event | category | flops | bytes accessed | tf_op | source)
XLA Modules:
  0.0 72.2 jit_solution(12144374031723534530)
XLA Ops:
  0.1 0.9 %copy-done.1 = f32[256,128]{1,0:T(8,128)S(1)} copy-done((f32[256,128]{1,0:T(8,128)S(1)}, f32[256,128]{1,0:T(8,128)}, u32[]{:S(2)}) %copy-start.1) | copy-done | bytes 131096
  1.0 0.7 copy-done.2
  1.7 2.6 %invert.1 = f32[264,128]{1,0:T(8,128)S(1)} custom-call(s32[2]{0:T(128)S(1)} %pad_add_fusion.place_ref, f32[256,128]{1,0:T(8,128)S(1)} %copy-done.1, f32[2,128]{1,0:T(2,128)S(1)} %copy-done.2), custom_call_target="tpu_custom_call" | custom-call | flops 3500000000 | bytes 2097152 | tf_op jit(solution)/shard_map/invert/pallas_call | solution.py:349
  4.2 1.1 %collective-permute-start.1 = (f32[264,128]{1,0:T(8,128)S(1)}, f32[264,128]{1,0:T(8,128)S(1)}, u32[]{:S(2)}, u32[]{:S(2)}) collective-permute-start(f32[264,128]{1,0:T(8,128)S(1)} %invert.1), channel_id=1, source_target_pairs={{0,8},{4,12},{8,0},{12,4},{16,24},{20,28},{24,16},{28,20},{1,9},{5... | collective-permute-start | bytes 405512 | tf_op jit(solution)/shard_map/ppermute | solution.py:298
  5.3 5.3 %collective-permute-done.1 = f32[264,128]{1,0:T(8,128)S(1)} collective-permute-done((f32[264,128]{1,0:T(8,128)S(1)}, f32[264,128]{1,0:T(8,128)S(1)}, u32[]{:S(2)}, u32[]{:S(2)}) %collective-permute-start.1) | collective-permute-done | bytes 135200 | tf_op jit(solution)/shard_map/ppermute | solution.py:298
  10.6 1.9 %collective-permute-start.11 = (f32[2,264,128]{2,1,0:T(8,128)S(1)}, f32[2,264,128]{2,1,0:T(8,128)S(1)}, u32[]{:S(2)}, u32[]{:S(2)}) collective-permute-start(f32[2,264,128]{2,1,0:T(8,128)S(1)} %pad_maximum_fusion.refs_0_), channel_id=1, source_target_pairs={{0,4},{4,0},{8,12},{12,8},{16,20},{20,16},{24,28},{28,24},{1,5},{5... | collective-permute-start | bytes 811016 | tf_op jit(solution)/shard_map/ppermute | solution.py:302
  12.5 4.1 %collective-permute-start.2 = (f32[2,264,128]{2,1,0:T(8,128)S(1)}, f32[2,264,128]{2,1,0:T(8,128)S(1)}, u32[]{:S(2)}, u32[]{:S(2)}) collective-permute-start(f32[2,264,128]{2,1,0:T(8,128)S(1)} %pad_maximum_fusion.refs_0_), channel_id=1, source_target_pairs={{0,16},{4,20},{8,24},{12,28},{16,0},{20,4},{24,8},{28,12},{1,17},{... | collective-permute-start | bytes 811016 | tf_op jit(solution)/shard_map/ppermute | solution.py:298
  17.7 0.9 %collective-permute-start.6 = (f32[256,128]{1,0:T(8,128)S(1)}, f32[256,128]{1,0:T(8,128)S(1)}, u32[]{:S(2)}, u32[]{:S(2)}) collective-permute-start(f32[256,128]{1,0:T(8,128)S(1)} %copy-done.3), channel_id=1, source_target_pairs={{0,8},{4,12},{8,0},{12,4},{16,24},{20,28},{24,16},{28,20},{1,9},{5... | collective-permute-start | bytes 393224 | tf_op jit(solution)/shard_map/ppermute | solution.py:298
  18.7 1.3 %collective-permute-done.11.refs_1_ = f32[2,264,128]{2,1,0:T(8,128)S(1)} collective-permute-done((f32[2,264,128]{2,1,0:T(8,128)S(1)}, f32[2,264,128]{2,1,0:T(8,128)S(1)}, u32[]{:S(2)}, u32[]{:S(2)}) %collective-permute-start.11) | collective-permute-done | bytes 270368 | tf_op jit(solution)/shard_map/ppermute | solution.py:302
  20.0 2.2 %collective-permute-done.came = f32[4,32,256]{2,1,0:T(8,128)S(1)} collective-permute-done((f32[4,32,256]{2,1,0:T(8,128)S(1)}, f32[4,32,256]{2,1,0:T(8,128)S(1)}, u32[]{:S(2)}, u32[]{:S(2)}) %collective-permute-start) | collective-permute-done | bytes 131104 | tf_op jit(solution)/shard_map/ppermute | solution.py:302
  22.2 5.2 %collective-permute-done.2.refs_4_ = f32[2,264,128]{2,1,0:T(8,128)S(1)} collective-permute-done((f32[2,264,128]{2,1,0:T(8,128)S(1)}, f32[2,264,128]{2,1,0:T(8,128)S(1)}, u32[]{:S(2)}, u32[]{:S(2)}) %collective-permute-start.2) | collective-permute-done | bytes 270368 | tf_op jit(solution)/shard_map/ppermute | solution.py:298
  28.0 1.4 %collective-permute-start.14 = (f32[2,264,128]{2,1,0:T(8,128)S(1)}, f32[2,264,128]{2,1,0:T(8,128)S(1)}, u32[]{:S(2)}, u32[]{:S(2)}) collective-permute-start(f32[2,264,128]{2,1,0:T(8,128)S(1)} %collective-permute-done.2.refs_4_), channel_id=1, source_target_pairs={{0,2},{4,6},{8,10},{12,14},{16,18},{20,22},{24,26},{28,30},{1,5},{... | collective-permute-start | bytes 811016 | tf_op jit(solution)/shard_map/ppermute | solution.py:315
  30.1 3.0 %collective-permute-start.3 = (f32[2,32,256]{2,1,0:T(8,128)S(1)}, f32[2,32,256]{2,1,0:T(8,128)S(1)}, u32[]{:S(2)}, u32[]{:S(2)}) collective-permute-start(f32[2,32,256]{2,1,0:T(8,128)S(1)} %get-tuple-element.31), channel_id=1, source_target_pairs={{0,8},{4,12},{8,0},{12,4},{16,24},{20,28},{24,16},{28,20},{1,9},{5... | collective-permute-start | bytes 196616 | tf_op jit(solution)/shard_map/ppermute | solution.py:298
  33.1 2.0 %collective-permute-done.15.refs_6_ = f32[2,264,128]{2,1,0:T(8,128)S(1)} collective-permute-done((f32[2,264,128]{2,1,0:T(8,128)S(1)}, f32[2,264,128]{2,1,0:T(8,128)S(1)}, u32[]{:S(2)}, u32[]{:S(2)}) %collective-permute-start.15) | collective-permute-done | bytes 270368 | tf_op jit(solution)/shard_map/ppermute | solution.py:315
  35.1 4.2 %collective-permute-start.5 = (f32[2,32,256]{2,1,0:T(8,128)S(1)}, f32[2,32,256]{2,1,0:T(8,128)S(1)}, u32[]{:S(2)}, u32[]{:S(2)}) collective-permute-start(f32[2,32,256]{2,1,0:T(8,128)S(1)} %get-tuple-element.35), channel_id=1, source_target_pairs={{0,24},{4,28},{8,16},{12,20},{16,8},{20,12},{24,0},{28,4},{1,25},{... | collective-permute-start | bytes 196616 | tf_op jit(solution)/shard_map/ppermute | solution.py:298
  39.9 1.5 %collective-permute-start.16 = (f32[2,264,128]{2,1,0:T(8,128)S(1)}, f32[2,264,128]{2,1,0:T(8,128)S(1)}, u32[]{:S(2)}, u32[]{:S(2)}) collective-permute-start(f32[2,264,128]{2,1,0:T(8,128)S(1)} %collective-permute-done.14.refs_5_), channel_id=1, source_target_pairs={{0,4},{4,0},{8,12},{12,8},{16,20},{20,16},{24,28},{28,24},{1,3},{5... | collective-permute-start | bytes 811016 | tf_op jit(solution)/shard_map/ppermute | solution.py:315
  41.4 6.4 %collective-permute-done.4.b2 = f32[2,32,256]{2,1,0:T(8,128)S(1)} collective-permute-done((f32[2,32,256]{2,1,0:T(8,128)S(1)}, f32[2,32,256]{2,1,0:T(8,128)S(1)}, u32[]{:S(2)}, u32[]{:S(2)}) %collective-permute-start.4) | collective-permute-done | bytes 65568 | tf_op jit(solution)/shard_map/ppermute | solution.py:298
  49.4 4.0 %collective-permute-done.8 = f32[32,1024]{1,0:T(8,128)S(1)} collective-permute-done((f32[32,1024]{1,0:T(8,128)S(1)}, f32[32,1024]{1,0:T(8,128)S(1)}, u32[]{:S(2)}, u32[]{:S(2)}) %collective-permute-start.8) | collective-permute-done | bytes 131104 | tf_op jit(solution)/shard_map/ppermute | solution.py:306
  56.9 3.6 %first_panel.1.x_ref = f32[128,1024]{1,0:T(8,128)S(1)} custom-call(s32[2]{0:T(128)S(1)} %pad_add_fusion.place_ref, f32[2,32,1024]{2,1,0:T(8,128)S(1)} %pad_maximum_fusion.2.pair, f32[2,32,1024]{2,1,0:T(8,128)S(1)} %collective-permute-done.9.other_pair, f32[2,264,128]{2,1,0:T(8,128)S(1)} %pad_maximum_fusion.refs_0_, ...), custom_call_target="tpu_custom_call" | custom-call | flops 200000000 | bytes 2097152 | tf_op jit(solution)/shard_map/first_panel/pallas_call | solution.py:393
  60.5 3.3 %collective-permute-done.25.refs_3_ = f32[2,256,128]{2,1,0:T(8,128)S(1)} collective-permute-done((f32[2,256,128]{2,1,0:T(8,128)S(1)}, f32[2,256,128]{2,1,0:T(8,128)S(1)}, u32[]{:S(2)}, u32[]{:S(2)}) %collective-permute-start.25) | collective-permute-done | bytes 262176 | tf_op jit(solution)/shard_map/ppermute | solution.py:302
  63.7 1.3 %update.1 = (f32[32,256]{1,0:T(8,128)S(1)}, f32[32,256]{1,0:T(8,128)S(1)}, f32[32,256]{1,0:T(8,128)S(1)}, f32[32,256]{1,0:T(8,128)S(1)}) custom-call(s32[2]{0:T(128)S(1)} %pad_add_fusion.place_ref, f32[128,1024]{1,0:T(8,128)S(1)} %first_panel.1.x_ref, f32[2,256,128]{2,1,0:T(8,128)S(1)} %pad_maximum_fusion.1.refs_0_, ...), custom_call_target="tpu_custom_call" | custom-call | flops 2000000000 | bytes 2097152 | tf_op jit(solution)/shard_map/update/pallas_call | solution.py:404
  65.6 1.7 %collective-permute-start.28 = (f32[32,256]{1,0:T(8,128)S(1)}, f32[32,256]{1,0:T(8,128)S(1)}, u32[]{:S(2)}, u32[]{:S(2)}) collective-permute-start(f32[32,256]{1,0:T(8,128)S(1)} %get-tuple-element.52), channel_id=1, source_target_pairs={{0,3},{1,2},{2,1},{3,0},{4,7},{5,6},{6,5},{7,4},{8,11},{9,10},{10,... | collective-permute-start | bytes 98312 | tf_op jit(solution)/shard_map/ppermute | solution.py:306
  67.2 2.9 %second_factor.1 = (bf16[1024,1024]{1,0:T(8,128)(2,1)S(1)}, bf16[1024,1024]{1,0:T(8,128)(2,1)S(1)}) custom-call(s32[2]{0:T(128)S(1)} %pad_add_fusion.place_ref, f32[2,264,128]{2,1,0:T(8,128)S(1)} %pad_maximum_fusion.refs_0_, f32[2,264,128]{2,1,0:T(8,128)S(1)} %collective-permute-done.11.refs_1_, f32[2,264,128]{2,1,0:T(8,128)S(1)} %collective-permute-done.12.refs_2_, ...), custom_call_target="tpu_custom_call" | custom-call | flops 3000000000 | bytes 2097152 | tf_op jit(solution)/shard_map/second_factor/pallas_call | solution.py:416
  70.1 2.1 %second_panel.1 = f32[32,2048]{1,0:T(8,128)} custom-call(s32[2]{0:T(128)S(1)} %pad_add_fusion.place_ref, f32[128,1024]{1,0:T(8,128)S(1)} %first_panel.1.x_ref, f32[2,32,1024]{2,1,0:T(8,128)S(1)} %get-tuple-element.45.both_ref, bf16[1024,1024]{1,0:T(8,128)(2,1)S(1)} %get-tuple-element.48.uh_ref, bf16[1024,1024]{1,0:T(8,128)(2,1)S(1)} %get-tuple-element.49.ul_ref, ...), custom_call_target="tpu_custom_call" | custom-call | flops 2500000000 | bytes 2097152 | tf_op jit(solution)/shard_map/second_panel/pallas_call | solution.py:420
  (54 shorter events, 8.7 us)
Async XLA Ops:
  4.2 6.4 %collective-permute-start.1 = (f32[264,128]{1,0:T(8,128)S(1)}, f32[264,128]{1,0:T(8,128)S(1)}, u32[]{:S(2)}, u32[]{:S(2)}) collective-permute-start(f32[264,128]{1,0:T(8,128)S(1)} %invert.1), channel_id=1, source_target_pairs={{0,8},{4,12},{8,0},{12,4},{16,24},{20,28},{24,16},{28,20},{1,9},{5... | collective-permute-start | bytes 405512 | tf_op jit(solution)/shard_map/ppermute | solution.py:298
  10.6 9.4 %collective-permute-start.11 = (f32[2,264,128]{2,1,0:T(8,128)S(1)}, f32[2,264,128]{2,1,0:T(8,128)S(1)}, u32[]{:S(2)}, u32[]{:S(2)}) collective-permute-start(f32[2,264,128]{2,1,0:T(8,128)S(1)} %pad_maximum_fusion.refs_0_), channel_id=1, source_target_pairs={{0,4},{4,0},{8,12},{12,8},{16,20},{20,16},{24,28},{28,24},{1,5},{5... | collective-permute-start | bytes 811016 | tf_op jit(solution)/shard_map/ppermute | solution.py:302
  12.5 9.7 %collective-permute-start.12 = (f32[2,264,128]{2,1,0:T(8,128)S(1)}, f32[2,264,128]{2,1,0:T(8,128)S(1)}, u32[]{:S(2)}, u32[]{:S(2)}) collective-permute-start(f32[2,264,128]{2,1,0:T(8,128)S(1)} %pad_maximum_fusion.refs_0_), channel_id=1, source_target_pairs={{0,2},{1,3},{2,0},{3,1},{4,6},{5,7},{6,4},{7,5},{8,10},{9,11},{10,... | collective-permute-start | bytes 811016 | tf_op jit(solution)/shard_map/ppermute | solution.py:306
  12.5 14.9 %collective-permute-start.2 = (f32[2,264,128]{2,1,0:T(8,128)S(1)}, f32[2,264,128]{2,1,0:T(8,128)S(1)}, u32[]{:S(2)}, u32[]{:S(2)}) collective-permute-start(f32[2,264,128]{2,1,0:T(8,128)S(1)} %pad_maximum_fusion.refs_0_), channel_id=1, source_target_pairs={{0,16},{4,20},{8,24},{12,28},{16,0},{20,4},{24,8},{28,12},{1,17},{... | collective-permute-start | bytes 811016 | tf_op jit(solution)/shard_map/ppermute | solution.py:298
  17.2 5.0 %collective-permute-start = (f32[4,32,256]{2,1,0:T(8,128)S(1)}, f32[4,32,256]{2,1,0:T(8,128)S(1)}, u32[]{:S(2)}, u32[]{:S(2)}) collective-permute-start(f32[4,32,256]{2,1,0:T(8,128)S(1)} %leave.1), channel_id=1, source_target_pairs={{0,4},{4,0},{8,12},{12,8},{16,20},{20,16},{24,28},{28,24},{1,5},{5... | collective-permute-start | bytes 393224 | tf_op jit(solution)/shard_map/ppermute | solution.py:302
  17.7 11.7 %collective-permute-start.6 = (f32[256,128]{1,0:T(8,128)S(1)}, f32[256,128]{1,0:T(8,128)S(1)}, u32[]{:S(2)}, u32[]{:S(2)}) collective-permute-start(f32[256,128]{1,0:T(8,128)S(1)} %copy-done.3), channel_id=1, source_target_pairs={{0,8},{4,12},{8,0},{12,4},{16,24},{20,28},{24,16},{28,20},{1,9},{5... | collective-permute-start | bytes 393224 | tf_op jit(solution)/shard_map/ppermute | solution.py:298
  20.0 13.0 %collective-permute-start.13 = (f32[2,264,128]{2,1,0:T(8,128)S(1)}, f32[2,264,128]{2,1,0:T(8,128)S(1)}, u32[]{:S(2)}, u32[]{:S(2)}) collective-permute-start(f32[2,264,128]{2,1,0:T(8,128)S(1)} %collective-permute-done.11.refs_1_), channel_id=1, source_target_pairs={{0,2},{1,3},{2,0},{3,1},{4,6},{5,7},{6,4},{7,5},{8,10},{9,11},{10,... | collective-permute-start | bytes 811016 | tf_op jit(solution)/shard_map/ppermute | solution.py:306
  27.4 7.7 %collective-permute-start.15 = (f32[2,264,128]{2,1,0:T(8,128)S(1)}, f32[2,264,128]{2,1,0:T(8,128)S(1)}, u32[]{:S(2)}, u32[]{:S(2)}) collective-permute-start(f32[2,264,128]{2,1,0:T(8,128)S(1)} %collective-permute-done.2.refs_4_), channel_id=1, source_target_pairs={{0,4},{4,0},{8,12},{12,8},{16,20},{20,16},{24,28},{28,24},{1,3},{5... | collective-permute-start | bytes 811016 | tf_op jit(solution)/shard_map/ppermute | solution.py:315
  28.0 11.3 %collective-permute-start.14 = (f32[2,264,128]{2,1,0:T(8,128)S(1)}, f32[2,264,128]{2,1,0:T(8,128)S(1)}, u32[]{:S(2)}, u32[]{:S(2)}) collective-permute-start(f32[2,264,128]{2,1,0:T(8,128)S(1)} %collective-permute-done.2.refs_4_), channel_id=1, source_target_pairs={{0,2},{4,6},{8,10},{12,14},{16,18},{20,22},{24,26},{28,30},{1,5},{... | collective-permute-start | bytes 811016 | tf_op jit(solution)/shard_map/ppermute | solution.py:315
  29.4 18.9 %collective-permute-start.7 = (f32[2,256,128]{2,1,0:T(8,128)S(1)}, f32[2,256,128]{2,1,0:T(8,128)S(1)}, u32[]{:S(2)}, u32[]{:S(2)}) collective-permute-start(f32[2,256,128]{2,1,0:T(8,128)S(1)} %pad_maximum_fusion.1.refs_0_), channel_id=1, source_target_pairs={{0,16},{4,20},{8,24},{12,28},{16,0},{20,4},{24,8},{28,12},{1,17},{... | collective-permute-start | bytes 786440 | tf_op jit(solution)/shard_map/ppermute | solution.py:298
  30.1 9.8 %collective-permute-start.3 = (f32[2,32,256]{2,1,0:T(8,128)S(1)}, f32[2,32,256]{2,1,0:T(8,128)S(1)}, u32[]{:S(2)}, u32[]{:S(2)}) collective-permute-start(f32[2,32,256]{2,1,0:T(8,128)S(1)} %get-tuple-element.31), channel_id=1, source_target_pairs={{0,8},{4,12},{8,0},{12,4},{16,24},{20,28},{24,16},{28,20},{1,9},{5... | collective-permute-start | bytes 196616 | tf_op jit(solution)/shard_map/ppermute | solution.py:298
  33.0 14.7 %collective-permute-start.4 = (f32[2,32,256]{2,1,0:T(8,128)S(1)}, f32[2,32,256]{2,1,0:T(8,128)S(1)}, u32[]{:S(2)}, u32[]{:S(2)}) collective-permute-start(f32[2,32,256]{2,1,0:T(8,128)S(1)} %get-tuple-element.33), channel_id=1, source_target_pairs={{0,16},{4,20},{8,24},{12,28},{16,0},{20,4},{24,8},{28,12},{1,17},{... | collective-permute-start | bytes 196616 | tf_op jit(solution)/shard_map/ppermute | solution.py:298
  35.1 12.6 %collective-permute-start.5 = (f32[2,32,256]{2,1,0:T(8,128)S(1)}, f32[2,32,256]{2,1,0:T(8,128)S(1)}, u32[]{:S(2)}, u32[]{:S(2)}) collective-permute-start(f32[2,32,256]{2,1,0:T(8,128)S(1)} %get-tuple-element.35), channel_id=1, source_target_pairs={{0,24},{4,28},{8,16},{12,20},{16,8},{20,12},{24,0},{28,4},{1,25},{... | collective-permute-start | bytes 196616 | tf_op jit(solution)/shard_map/ppermute | solution.py:298
  39.4 10.0 %collective-permute-start.10 = (f32[2,256,128]{2,1,0:T(8,128)S(1)}, f32[2,256,128]{2,1,0:T(8,128)S(1)}, u32[]{:S(2)}, u32[]{:S(2)}) collective-permute-start(f32[2,256,128]{2,1,0:T(8,128)S(1)} %pad_maximum_fusion.1.refs_0_), channel_id=1, source_target_pairs={{0,4},{4,0},{8,12},{12,8},{16,20},{20,16},{24,28},{28,24},{1,5},{5... | collective-permute-start | bytes 786440 | tf_op jit(solution)/shard_map/ppermute | solution.py:302
  39.9 13.5 %collective-permute-start.16 = (f32[2,264,128]{2,1,0:T(8,128)S(1)}, f32[2,264,128]{2,1,0:T(8,128)S(1)}, u32[]{:S(2)}, u32[]{:S(2)}) collective-permute-start(f32[2,264,128]{2,1,0:T(8,128)S(1)} %collective-permute-done.14.refs_5_), channel_id=1, source_target_pairs={{0,4},{4,0},{8,12},{12,8},{16,20},{20,16},{24,28},{28,24},{1,3},{5... | collective-permute-start | bytes 811016 | tf_op jit(solution)/shard_map/ppermute | solution.py:315
  48.4 5.0 %collective-permute-start.8 = (f32[32,1024]{1,0:T(8,128)S(1)}, f32[32,1024]{1,0:T(8,128)S(1)}, u32[]{:S(2)}, u32[]{:S(2)}) collective-permute-start(f32[32,1024]{1,0:T(8,128)S(1)} %get-tuple-element.39), channel_id=1, source_target_pairs={{0,2},{1,3},{2,0},{3,1},{4,6},{5,7},{6,4},{7,5},{8,10},{9,11},{10,... | collective-permute-start | bytes 393224 | tf_op jit(solution)/shard_map/ppermute | solution.py:306
  48.9 5.1 %collective-permute-start.17 = (f32[2,264,128]{2,1,0:T(8,128)S(1)}, f32[2,264,128]{2,1,0:T(8,128)S(1)}, u32[]{:S(2)}, u32[]{:S(2)}) collective-permute-start(f32[2,264,128]{2,1,0:T(8,128)S(1)} %pad_maximum_fusion.refs_0_), channel_id=1, source_target_pairs={{0,1},{1,0},{2,3},{3,2},{4,5},{5,4},{6,7},{7,6},{8,9},{9,8},{10,11... | collective-permute-start | bytes 811016 | tf_op jit(solution)/shard_map/ppermute | solution.py:306
  48.9 5.2 %collective-permute-start.19 = (f32[2,264,128]{2,1,0:T(8,128)S(1)}, f32[2,264,128]{2,1,0:T(8,128)S(1)}, u32[]{:S(2)}, u32[]{:S(2)}) collective-permute-start(f32[2,264,128]{2,1,0:T(8,128)S(1)} %collective-permute-done.12.refs_2_), channel_id=1, source_target_pairs={{0,1},{1,0},{2,3},{3,2},{4,5},{5,4},{6,7},{7,6},{8,9},{9,8},{10,11... | collective-permute-start | bytes 811016 | tf_op jit(solution)/shard_map/ppermute | solution.py:306
  49.4 5.1 %collective-permute-start.18 = (f32[2,264,128]{2,1,0:T(8,128)S(1)}, f32[2,264,128]{2,1,0:T(8,128)S(1)}, u32[]{:S(2)}, u32[]{:S(2)}) collective-permute-start(f32[2,264,128]{2,1,0:T(8,128)S(1)} %collective-permute-done.11.refs_1_), channel_id=1, source_target_pairs={{0,1},{1,0},{2,3},{3,2},{4,5},{5,4},{6,7},{7,6},{8,9},{9,8},{10,11... | collective-permute-start | bytes 811016 | tf_op jit(solution)/shard_map/ppermute | solution.py:306
  54.1 2.0 %collective-permute-start.23 = (f32[2,264,128]{2,1,0:T(8,128)S(1)}, f32[2,264,128]{2,1,0:T(8,128)S(1)}, u32[]{:S(2)}, u32[]{:S(2)}) collective-permute-start(f32[2,264,128]{2,1,0:T(8,128)S(1)} %collective-permute-done.15.refs_6_), channel_id=1, source_target_pairs={{0,1},{1,0},{2,3},{3,2},{4,5},{5,4},{6,7},{7,6},{8,9},{9,8},{10,11... | collective-permute-start | bytes 811016 | tf_op jit(solution)/shard_map/ppermute | solution.py:306
  55.3 8.4 %collective-permute-start.25 = (f32[2,256,128]{2,1,0:T(8,128)S(1)}, f32[2,256,128]{2,1,0:T(8,128)S(1)}, u32[]{:S(2)}, u32[]{:S(2)}) collective-permute-start(f32[2,256,128]{2,1,0:T(8,128)S(1)} %collective-permute-done.7.refs_1_), channel_id=1, source_target_pairs={{0,4},{4,0},{8,12},{12,8},{16,20},{20,16},{24,28},{28,24},{1,5},{5... | collective-permute-start | bytes 786440 | tf_op jit(solution)/shard_map/ppermute | solution.py:302
  65.0 5.1 %collective-permute-start.26 = (f32[32,256]{1,0:T(8,128)S(1)}, f32[32,256]{1,0:T(8,128)S(1)}, u32[]{:S(2)}, u32[]{:S(2)}) collective-permute-start(f32[32,256]{1,0:T(8,128)S(1)} %get-tuple-element.50), channel_id=1, source_target_pairs={{0,2},{1,3},{2,0},{3,1},{4,6},{5,7},{6,4},{7,5},{8,10},{9,11},{10,... | collective-permute-start | bytes 98312 | tf_op jit(solution)/shard_map/ppermute | solution.py:306
  65.5 4.6 %collective-permute-start.27 = (f32[32,256]{1,0:T(8,128)S(1)}, f32[32,256]{1,0:T(8,128)S(1)}, u32[]{:S(2)}, u32[]{:S(2)}) collective-permute-start(f32[32,256]{1,0:T(8,128)S(1)} %get-tuple-element.51), channel_id=1, source_target_pairs={{0,1},{1,0},{2,3},{3,2},{4,5},{5,4},{6,7},{7,6},{8,9},{9,8},{10,11... | collective-permute-start | bytes 98312 | tf_op jit(solution)/shard_map/ppermute | solution.py:306
  65.6 4.6 %collective-permute-start.28 = (f32[32,256]{1,0:T(8,128)S(1)}, f32[32,256]{1,0:T(8,128)S(1)}, u32[]{:S(2)}, u32[]{:S(2)}) collective-permute-start(f32[32,256]{1,0:T(8,128)S(1)} %get-tuple-element.52), channel_id=1, source_target_pairs={{0,3},{1,2},{2,1},{3,0},{4,7},{5,6},{6,5},{7,4},{8,11},{9,10},{10,... | collective-permute-start | bytes 98312 | tf_op jit(solution)/shard_map/ppermute | solution.py:306
  (9 other events, 39.1 us)
where the time goes:
time: 72.4 us; the launch traced here: 72.2 us
  waiting for transfers between devices  31.3 us (43%)
  starting transfers between devices  24.9 us (34%)
  Pallas kernels  14 us (19%)
  local copies, waits for them, and re-layouts  1.59 us (2%)
    ppermute x7, waiting for transfers between devices, swap_z(): return lax.ppermute(x, 'bulk', [(k, k ^ 2 * m) for k in range(8)])  16.9 us
    ppermute x7, starting transfers between devices, swap_z(): return lax.ppermute(x, 'bulk', [(k, k ^ 2 * m) for k in range(8)])  13.5 us
    ppermute x4, waiting for transfers between devices, swap_y(): return lax.ppermute(x, 'bulk', [(k, k ^ 1) for k in range(8)])  6.81 us
    ppermute x15, waiting for transfers between devices, swap_rep(): return lax.ppermute(x, 'rep', [(k, k ^ bits) for k in range(4)])  5.68 us
    ppermute x15, starting transfers between devices, swap_rep(): return lax.ppermute(x, 'rep', [(k, k ^ bits) for k in range(4)])  4.55 us
    pallas_call x1, Pallas kernels, per_device(): call(first_kernel, shape(128, 1024), [SMEM] + [VMEM] * 18, VMEM, [pltpu.V...  3.58 us
    ppermute x3, starting transfers between devices, cross(): return lax.ppermute(x, BOTH, pairs)  3.5 us
    ppermute x4, starting transfers between devices, swap_y(): return lax.ppermute(x, 'bulk', [(k, k ^ 1) for k in range(8)])  3.41 us
  transfers between devices with their start and end apart: 29, of which 13 were waited for; matrix products, arithmetic and copies ran while one was open for 0% of the time, Pallas kernels for 11%

commit v1 on v0

--- a/solution.py
+++ b/solution.py
@@ -362,16 +362,16 @@
     c_near = jnp.stack([coupling, swap_z(coup, 1)])
     c_near_got = swap_y(c_near)
 
-    far_now = after(far, near0, near1, came)
+    far_now = after(far, near0, near1, came, c_near)
     far0 = cross(far_now, 0)
     far1 = cross(far_now, 1)
     b_out = call(spread_kernel, [shape(2, 32, 256)] * 3, [SMEM, VMEM, VMEM], [VMEM] * 3, [], SPREAD, 4, "spread")(
         place, blocks, came
     )
-    b_z = [swap_z(after(b, far), m + 1) for m, b in enumerate(b_out)]
-    c_far = swap_z(after(c_near, far), 2)
+    b_z = [swap_z(after(b, far, near01), m + 1) for m, b in enumerate(b_out)]
+    c_far = swap_z(after(c_near, far, b_z[0]), 2)
     c_far_got = swap_y(c_far)
-    far01 = cross(after(far0, far1, near01), 1)
+    far01 = cross(after(far0, far1), 1)
 
     left, both = call(
         rows_kernel,
@@ -383,7 +383,7 @@
         4,
         "rows",
     )(place, blocks, came, *b_z)
-    pair = jnp.stack([left, swap_rep(after(left, c_far), 2)])
+    pair = jnp.stack([left, swap_rep(after(left, came), 2)])
     other_pair = swap_rep(after(pair, c_far), 1)
     bufs = [near, near0, near1, near01, far, far0, far1, far01]
     bufs += [swap_rep(b, 1) for b in bufs[:7]] + [swap_rep(after(far01, far1), 1)]

time: 72.4 us -> 69 us (0.953)
  waiting for transfers between devices: 31.3 us -> 27.2 us
    ppermute x7, waiting for transfers between devices: 16.9 us -> 20.2 us  [swap_z(): return lax.ppermute(x, 'bulk', [(k, k ^ 2 * m) for k in range(8)])]
    ppermute x4, waiting for transfers between devices: 6.81 us -> 3.81 us  [swap_y(): return lax.ppermute(x, 'bulk', [(k, k ^ 1) for k in range(8)])]
    ppermute x15, waiting for transfers between devices: 5.68 us -> 3.21 us  [swap_rep(): return lax.ppermute(x, 'rep', [(k, k ^ bits) for k in range(4)])]
    ppermute x3, waiting for transfers between devices: 1.99 us -> 0.01 us  [cross(): return lax.ppermute(x, BOTH, pairs)]
    ppermute x15, starting transfers between devices: 4.55 us -> 6.23 us  [swap_rep(): return lax.ppermute(x, 'rep', [(k, k ^ bits) for k in range(4)])]
    ppermute x7, starting transfers between devices: 13.5 us -> 12 us  [swap_z(): return lax.ppermute(x, 'bulk', [(k, k ^ 2 * m) for k in range(8)])]
    ppermute x4, starting transfers between devices: 3.41 us -> 4.86 us  [swap_y(): return lax.ppermute(x, 'bulk', [(k, k ^ 1) for k in range(8)])]
    ppermute x3, starting transfers between devices: 3.5 us -> 2.57 us  [cross(): return lax.ppermute(x, BOTH, pairs)]
  transfers between devices with their start and end apart: 29 -> 29, of which waited for: 13 -> 11; matrix products, arithmetic and copies ran while one was open for 0% -> 0% of each run, Pallas kernels for 11% -> 12%
where the time goes in v1:
time: 69 us; the launch traced here: 68.8 us
  waiting for transfers between devices  27.2 us (39%)
  starting transfers between devices  25.6 us (37%)
  Pallas kernels  14 us (20%)
  local copies, waits for them, and re-layouts  1.59 us (2%)
    ppermute x7, waiting for transfers between devices, swap_z(): return lax.ppermute(x, 'bulk', [(k, k ^ 2 * m) for k in range(8)])  20.2 us
    ppermute x7, starting transfers between devices, swap_z(): return lax.ppermute(x, 'bulk', [(k, k ^ 2 * m) for k in range(8)])  12 us
    ppermute x15, starting transfers between devices, swap_rep(): return lax.ppermute(x, 'rep', [(k, k ^ bits) for k in range(4)])  6.23 us
    ppermute x4, starting transfers between devices, swap_y(): return lax.ppermute(x, 'bulk', [(k, k ^ 1) for k in range(8)])  4.86 us
    ppermute x4, waiting for transfers between devices, swap_y(): return lax.ppermute(x, 'bulk', [(k, k ^ 1) for k in range(8)])  3.81 us
    pallas_call x1, Pallas kernels, per_device(): call(first_kernel, shape(128, 1024), [SMEM] + [VMEM] * 18, VMEM, [pltpu.V...  3.58 us
    ppermute x15, waiting for transfers between devices, swap_rep(): return lax.ppermute(x, 'rep', [(k, k ^ bits) for k in range(4)])  3.21 us
    pallas_call x1, Pallas kernels, per_device(): call(second_factor_kernel, halves, [SMEM] + [VMEM] * 16, [VMEM] * 2, scra...  2.86 us
  transfers between devices with their start and end apart: 29, of which 11 were waited for; matrix products, arithmetic and copies ran while one was open for 0% of the time, Pallas kernels for 12%

profile of v1, /device:TPU:0, one launch (start us, length us, event | category | flops | bytes accessed | tf_op | source)
XLA Modules:
  0.0 68.8 jit_solution(4911825445969838144)
XLA Ops:
  1.7 2.6 %invert.1 = f32[264,128]{1,0:T(8,128)S(1)} custom-call(s32[2]{0:T(128)S(1)} %pad_add_fusion.place_ref, f32[256,128]{1,0:T(8,128)S(1)} %copy-done.1, f32[2,128]{1,0:T(2,128)S(1)} %copy-done.2), custom_call_target="tpu_custom_call" | custom-call | flops 3500000000 | bytes 2097152 | tf_op jit(solution)/shard_map/invert/pallas_call | solution.py:349
  4.2 1.1 %collective-permute-start.1 = (f32[264,128]{1,0:T(8,128)S(1)}, f32[264,128]{1,0:T(8,128)S(1)}, u32[]{:S(2)}, u32[]{:S(2)}) collective-permute-start(f32[264,128]{1,0:T(8,128)S(1)} %invert.1), channel_id=1, source_target_pairs={{0,8},{4,12},{8,0},{12,4},{16,24},{20,28},{24,16},{28,20},{1,9},{5... | collective-permute-start | bytes 405512 | tf_op jit(solution)/shard_map/ppermute | solution.py:298
  5.3 5.3 %collective-permute-done.1 = f32[264,128]{1,0:T(8,128)S(1)} collective-permute-done((f32[264,128]{1,0:T(8,128)S(1)}, f32[264,128]{1,0:T(8,128)S(1)}, u32[]{:S(2)}, u32[]{:S(2)}) %collective-permute-start.1) | collective-permute-done | bytes 135200 | tf_op jit(solution)/shard_map/ppermute | solution.py:298
  10.6 1.9 %collective-permute-start.3 = (f32[2,264,128]{2,1,0:T(8,128)S(1)}, f32[2,264,128]{2,1,0:T(8,128)S(1)}, u32[]{:S(2)}, u32[]{:S(2)}) collective-permute-start(f32[2,264,128]{2,1,0:T(8,128)S(1)} %pad_maximum_fusion.refs_0_), channel_id=1, source_target_pairs={{0,4},{4,0},{8,12},{12,8},{16,20},{20,16},{24,28},{28,24},{1,5},{5... | collective-permute-start | bytes 811016 | tf_op jit(solution)/shard_map/ppermute | solution.py:302
  12.5 4.1 %collective-permute-start.2 = (f32[2,264,128]{2,1,0:T(8,128)S(1)}, f32[2,264,128]{2,1,0:T(8,128)S(1)}, u32[]{:S(2)}, u32[]{:S(2)}) collective-permute-start(f32[2,264,128]{2,1,0:T(8,128)S(1)} %pad_maximum_fusion.refs_0_), channel_id=1, source_target_pairs={{0,16},{4,20},{8,24},{12,28},{16,0},{20,4},{24,8},{28,12},{1,17},{... | collective-permute-start | bytes 811016 | tf_op jit(solution)/shard_map/ppermute | solution.py:298
  16.6 0.9 %collective-permute-start.9 = (f32[256,128]{1,0:T(8,128)S(1)}, f32[256,128]{1,0:T(8,128)S(1)}, u32[]{:S(2)}, u32[]{:S(2)}) collective-permute-start(f32[256,128]{1,0:T(8,128)S(1)} %copy-done.3), channel_id=1, source_target_pairs={{0,8},{4,12},{8,0},{12,4},{16,24},{20,28},{24,16},{28,20},{1,9},{5... | collective-permute-start | bytes 393224 | tf_op jit(solution)/shard_map/ppermute | solution.py:298
  19.2 4.5 %collective-permute-done.9 = f32[256,128]{1,0:T(8,128)S(1)} collective-permute-done((f32[256,128]{1,0:T(8,128)S(1)}, f32[256,128]{1,0:T(8,128)S(1)}, u32[]{:S(2)}, u32[]{:S(2)}) %collective-permute-start.9) | collective-permute-done | bytes 131104 | tf_op jit(solution)/shard_map/ppermute | solution.py:298
  23.8 3.6 %collective-permute-done.2.refs_4_ = f32[2,264,128]{2,1,0:T(8,128)S(1)} collective-permute-done((f32[2,264,128]{2,1,0:T(8,128)S(1)}, f32[2,264,128]{2,1,0:T(8,128)S(1)}, u32[]{:S(2)}, u32[]{:S(2)}) %collective-permute-start.2) | collective-permute-done | bytes 270368 | tf_op jit(solution)/shard_map/ppermute | solution.py:298
  27.9 1.5 %collective-permute-start.14 = (f32[2,264,128]{2,1,0:T(8,128)S(1)}, f32[2,264,128]{2,1,0:T(8,128)S(1)}, u32[]{:S(2)}, u32[]{:S(2)}) collective-permute-start(f32[2,264,128]{2,1,0:T(8,128)S(1)} %collective-permute-done.2.refs_4_), channel_id=1, source_target_pairs={{0,2},{4,6},{8,10},{12,14},{16,18},{20,22},{24,26},{28,30},{1,5},{... | collective-permute-start | bytes 811016 | tf_op jit(solution)/shard_map/ppermute | solution.py:315
  30.0 2.9 %collective-permute-start.6 = (f32[2,32,256]{2,1,0:T(8,128)S(1)}, f32[2,32,256]{2,1,0:T(8,128)S(1)}, u32[]{:S(2)}, u32[]{:S(2)}) collective-permute-start(f32[2,32,256]{2,1,0:T(8,128)S(1)} %get-tuple-element.33), channel_id=1, source_target_pairs={{0,16},{4,20},{8,24},{12,28},{16,0},{20,4},{24,8},{28,12},{1,17},{... | collective-permute-start | bytes 196616 | tf_op jit(solution)/shard_map/ppermute | solution.py:298
  32.9 1.5 %collective-permute-start.7 = (f32[2,32,256]{2,1,0:T(8,128)S(1)}, f32[2,32,256]{2,1,0:T(8,128)S(1)}, u32[]{:S(2)}, u32[]{:S(2)}) collective-permute-start(f32[2,32,256]{2,1,0:T(8,128)S(1)} %get-tuple-element.35), channel_id=1, source_target_pairs={{0,24},{4,28},{8,16},{12,20},{16,8},{20,12},{24,0},{28,4},{1,25},{... | collective-permute-start | bytes 196616 | tf_op jit(solution)/shard_map/ppermute | solution.py:298
  34.4 1.0 %collective-permute-start.12 = (f32[2,256,128]{2,1,0:T(8,128)S(1)}, f32[2,256,128]{2,1,0:T(8,128)S(1)}, u32[]{:S(2)}, u32[]{:S(2)}) collective-permute-start(f32[2,256,128]{2,1,0:T(8,128)S(1)} %pad_maximum_fusion.2.refs_0_), channel_id=1, source_target_pairs={{0,4},{4,0},{8,12},{12,8},{16,20},{20,16},{24,28},{28,24},{1,5},{5... | collective-permute-start | bytes 786440 | tf_op jit(solution)/shard_map/ppermute | solution.py:302
  35.5 1.4 %collective-permute-start.10 = (f32[2,256,128]{2,1,0:T(8,128)S(1)}, f32[2,256,128]{2,1,0:T(8,128)S(1)}, u32[]{:S(2)}, u32[]{:S(2)}) collective-permute-start(f32[2,256,128]{2,1,0:T(8,128)S(1)} %pad_maximum_fusion.2.refs_0_), channel_id=1, source_target_pairs={{0,16},{4,20},{8,24},{12,28},{16,0},{20,4},{24,8},{28,12},{1,17},{... | collective-permute-start | bytes 786440 | tf_op jit(solution)/shard_map/ppermute | solution.py:298
  37.5 1.9 %collective-permute-done.7.b3 = f32[2,32,256]{2,1,0:T(8,128)S(1)} collective-permute-done((f32[2,32,256]{2,1,0:T(8,128)S(1)}, f32[2,32,256]{2,1,0:T(8,128)S(1)}, u32[]{:S(2)}, u32[]{:S(2)}) %collective-permute-start.7) | collective-permute-done | bytes 65568 | tf_op jit(solution)/shard_map/ppermute | solution.py:298
  40.0 2.2 %collective-permute-start.8 = (f32[32,1024]{1,0:T(8,128)S(1)}, f32[32,1024]{1,0:T(8,128)S(1)}, u32[]{:S(2)}, u32[]{:S(2)}) collective-permute-start(f32[32,1024]{1,0:T(8,128)S(1)} %get-tuple-element.37), channel_id=1, source_target_pairs={{0,2},{1,3},{2,0},{3,1},{4,6},{5,7},{6,4},{7,5},{8,10},{9,11},{10,... | collective-permute-start | bytes 393224 | tf_op jit(solution)/shard_map/ppermute | solution.py:306
  42.7 2.4 %collective-permute-done.8 = f32[32,1024]{1,0:T(8,128)S(1)} collective-permute-done((f32[32,1024]{1,0:T(8,128)S(1)}, f32[32,1024]{1,0:T(8,128)S(1)}, u32[]{:S(2)}, u32[]{:S(2)}) %collective-permute-start.8) | collective-permute-done | bytes 131104 | tf_op jit(solution)/shard_map/ppermute | solution.py:306
  45.1 4.9 %collective-permute-done.10.refs_1_ = f32[2,256,128]{2,1,0:T(8,128)S(1)} collective-permute-done((f32[2,256,128]{2,1,0:T(8,128)S(1)}, f32[2,256,128]{2,1,0:T(8,128)S(1)}, u32[]{:S(2)}, u32[]{:S(2)}) %collective-permute-start.10) | collective-permute-done | bytes 262176 | tf_op jit(solution)/shard_map/ppermute | solution.py:298
  51.9 1.4 %collective-permute-start.25 = (f32[2,256,128]{2,1,0:T(8,128)S(1)}, f32[2,256,128]{2,1,0:T(8,128)S(1)}, u32[]{:S(2)}, u32[]{:S(2)}) collective-permute-start(f32[2,256,128]{2,1,0:T(8,128)S(1)} %collective-permute-done.10.refs_1_), channel_id=1, source_target_pairs={{0,4},{4,0},{8,12},{12,8},{16,20},{20,16},{24,28},{28,24},{1,5},{5... | collective-permute-start | bytes 786440 | tf_op jit(solution)/shard_map/ppermute | solution.py:302
  53.5 3.6 %first_panel.1.x_ref = f32[128,1024]{1,0:T(8,128)S(1)} custom-call(s32[2]{0:T(128)S(1)} %pad_add_fusion.place_ref, f32[2,32,1024]{2,1,0:T(8,128)S(1)} %pad_maximum_fusion.1.pair, f32[2,32,1024]{2,1,0:T(8,128)S(1)} %collective-permute-done.11.other_pair, f32[2,264,128]{2,1,0:T(8,128)S(1)} %pad_maximum_fusion.refs_0_, ...), custom_call_target="tpu_custom_call" | custom-call | flops 200000000 | bytes 2097152 | tf_op jit(solution)/shard_map/first_panel/pallas_call | solution.py:393
  57.0 3.3 %collective-permute-done.25.refs_3_ = f32[2,256,128]{2,1,0:T(8,128)S(1)} collective-permute-done((f32[2,256,128]{2,1,0:T(8,128)S(1)}, f32[2,256,128]{2,1,0:T(8,128)S(1)}, u32[]{:S(2)}, u32[]{:S(2)}) %collective-permute-start.25) | collective-permute-done | bytes 262176 | tf_op jit(solution)/shard_map/ppermute | solution.py:302
  60.3 1.3 %update.1 = (f32[32,256]{1,0:T(8,128)S(1)}, f32[32,256]{1,0:T(8,128)S(1)}, f32[32,256]{1,0:T(8,128)S(1)}, f32[32,256]{1,0:T(8,128)S(1)}) custom-call(s32[2]{0:T(128)S(1)} %pad_add_fusion.place_ref, f32[128,1024]{1,0:T(8,128)S(1)} %first_panel.1.x_ref, f32[2,256,128]{2,1,0:T(8,128)S(1)} %pad_maximum_fusion.2.refs_0_, ...), custom_call_target="tpu_custom_call" | custom-call | flops 2000000000 | bytes 2097152 | tf_op jit(solution)/shard_map/update/pallas_call | solution.py:404
  61.6 1.6 %collective-permute-start.26 = (f32[32,256]{1,0:T(8,128)S(1)}, f32[32,256]{1,0:T(8,128)S(1)}, u32[]{:S(2)}, u32[]{:S(2)}) collective-permute-start(f32[32,256]{1,0:T(8,128)S(1)} %get-tuple-element.50), channel_id=1, source_target_pairs={{0,2},{1,3},{2,0},{3,1},{4,6},{5,7},{6,4},{7,5},{8,10},{9,11},{10,... | collective-permute-start | bytes 98312 | tf_op jit(solution)/shard_map/ppermute | solution.py:306
  63.8 2.9 %second_factor.1 = (bf16[1024,1024]{1,0:T(8,128)(2,1)S(1)}, bf16[1024,1024]{1,0:T(8,128)(2,1)S(1)}) custom-call(s32[2]{0:T(128)S(1)} %pad_add_fusion.place_ref, f32[2,264,128]{2,1,0:T(8,128)S(1)} %pad_maximum_fusion.refs_0_, f32[2,264,128]{2,1,0:T(8,128)S(1)} %collective-permute-done.3.refs_1_, f32[2,264,128]{2,1,0:T(8,128)S(1)} %collective-permute-done.13.refs_2_, ...), custom_call_target="tpu_custom_call" | custom-call | flops 3000000000 | bytes 2097152 | tf_op jit(solution)/shard_map/second_factor/pallas_call | solution.py:416
  66.7 2.1 %second_panel.1 = f32[32,2048]{1,0:T(8,128)} custom-call(s32[2]{0:T(128)S(1)} %pad_add_fusion.place_ref, f32[128,1024]{1,0:T(8,128)S(1)} %first_panel.1.x_ref, f32[2,32,1024]{2,1,0:T(8,128)S(1)} %get-tuple-element.45.both_ref, bf16[1024,1024]{1,0:T(8,128)(2,1)S(1)} %get-tuple-element.48.uh_ref, bf16[1024,1024]{1,0:T(8,128)(2,1)S(1)} %get-tuple-element.49.ul_ref, ...), custom_call_target="tpu_custom_call" | custom-call | flops 2500000000 | bytes 2097152 | tf_op jit(solution)/shard_map/second_panel/pallas_call | solution.py:420
  (54 shorter events, 8.9 us)
Async XLA Ops:
  4.2 6.4 %collective-permute-start.1 = (f32[264,128]{1,0:T(8,128)S(1)}, f32[264,128]{1,0:T(8,128)S(1)}, u32[]{:S(2)}, u32[]{:S(2)}) collective-permute-start(f32[264,128]{1,0:T(8,128)S(1)} %invert.1), channel_id=1, source_target_pairs={{0,8},{4,12},{8,0},{12,4},{16,24},{20,28},{24,16},{28,20},{1,9},{5... | collective-permute-start | bytes 405512 | tf_op jit(solution)/shard_map/ppermute | solution.py:298
  10.6 8.6 %collective-permute-start.3 = (f32[2,264,128]{2,1,0:T(8,128)S(1)}, f32[2,264,128]{2,1,0:T(8,128)S(1)}, u32[]{:S(2)}, u32[]{:S(2)}) collective-permute-start(f32[2,264,128]{2,1,0:T(8,128)S(1)} %pad_maximum_fusion.refs_0_), channel_id=1, source_target_pairs={{0,4},{4,0},{8,12},{12,8},{16,20},{20,16},{24,28},{28,24},{1,5},{5... | collective-permute-start | bytes 811016 | tf_op jit(solution)/shard_map/ppermute | solution.py:302
  12.5 11.3 %collective-permute-start.13 = (f32[2,264,128]{2,1,0:T(8,128)S(1)}, f32[2,264,128]{2,1,0:T(8,128)S(1)}, u32[]{:S(2)}, u32[]{:S(2)}) collective-permute-start(f32[2,264,128]{2,1,0:T(8,128)S(1)} %pad_maximum_fusion.refs_0_), channel_id=1, source_target_pairs={{0,2},{1,3},{2,0},{3,1},{4,6},{5,7},{6,4},{7,5},{8,10},{9,11},{10,... | collective-permute-start | bytes 811016 | tf_op jit(solution)/shard_map/ppermute | solution.py:306
  12.5 14.9 %collective-permute-start.2 = (f32[2,264,128]{2,1,0:T(8,128)S(1)}, f32[2,264,128]{2,1,0:T(8,128)S(1)}, u32[]{:S(2)}, u32[]{:S(2)}) collective-permute-start(f32[2,264,128]{2,1,0:T(8,128)S(1)} %pad_maximum_fusion.refs_0_), channel_id=1, source_target_pairs={{0,16},{4,20},{8,24},{12,28},{16,0},{20,4},{24,8},{28,12},{1,17},{... | collective-permute-start | bytes 811016 | tf_op jit(solution)/shard_map/ppermute | solution.py:298
  16.6 7.1 %collective-permute-start.9 = (f32[256,128]{1,0:T(8,128)S(1)}, f32[256,128]{1,0:T(8,128)S(1)}, u32[]{:S(2)}, u32[]{:S(2)}) collective-permute-start(f32[256,128]{1,0:T(8,128)S(1)} %copy-done.3), channel_id=1, source_target_pairs={{0,8},{4,12},{8,0},{12,4},{16,24},{20,28},{24,16},{28,20},{1,9},{5... | collective-permute-start | bytes 393224 | tf_op jit(solution)/shard_map/ppermute | solution.py:298
  18.1 5.6 %collective-permute-start = (f32[4,32,256]{2,1,0:T(8,128)S(1)}, f32[4,32,256]{2,1,0:T(8,128)S(1)}, u32[]{:S(2)}, u32[]{:S(2)}) collective-permute-start(f32[4,32,256]{2,1,0:T(8,128)S(1)} %leave.1), channel_id=1, source_target_pairs={{0,4},{4,0},{8,12},{12,8},{16,20},{20,16},{24,28},{28,24},{1,5},{5... | collective-permute-start | bytes 393224 | tf_op jit(solution)/shard_map/ppermute | solution.py:302
  19.2 10.8 %collective-permute-start.4 = (f32[2,264,128]{2,1,0:T(8,128)S(1)}, f32[2,264,128]{2,1,0:T(8,128)S(1)}, u32[]{:S(2)}, u32[]{:S(2)}) collective-permute-start(f32[2,264,128]{2,1,0:T(8,128)S(1)} %collective-permute-done.3.refs_1_), channel_id=1, source_target_pairs={{0,2},{1,3},{2,0},{3,1},{4,6},{5,7},{6,4},{7,5},{8,10},{9,11},{10,... | collective-permute-start | bytes 811016 | tf_op jit(solution)/shard_map/ppermute | solution.py:306
  27.4 8.0 %collective-permute-start.15 = (f32[2,264,128]{2,1,0:T(8,128)S(1)}, f32[2,264,128]{2,1,0:T(8,128)S(1)}, u32[]{:S(2)}, u32[]{:S(2)}) collective-permute-start(f32[2,264,128]{2,1,0:T(8,128)S(1)} %collective-permute-done.2.refs_4_), channel_id=1, source_target_pairs={{0,4},{4,0},{8,12},{12,8},{16,20},{20,16},{24,28},{28,24},{1,3},{5... | collective-permute-start | bytes 811016 | tf_op jit(solution)/shard_map/ppermute | solution.py:315
  27.9 9.0 %collective-permute-start.14 = (f32[2,264,128]{2,1,0:T(8,128)S(1)}, f32[2,264,128]{2,1,0:T(8,128)S(1)}, u32[]{:S(2)}, u32[]{:S(2)}) collective-permute-start(f32[2,264,128]{2,1,0:T(8,128)S(1)} %collective-permute-done.2.refs_4_), channel_id=1, source_target_pairs={{0,2},{4,6},{8,10},{12,14},{16,18},{20,22},{24,26},{28,30},{1,5},{... | collective-permute-start | bytes 811016 | tf_op jit(solution)/shard_map/ppermute | solution.py:315
  29.9 4.5 %collective-permute-start.5 = (f32[2,32,256]{2,1,0:T(8,128)S(1)}, f32[2,32,256]{2,1,0:T(8,128)S(1)}, u32[]{:S(2)}, u32[]{:S(2)}) collective-permute-start(f32[2,32,256]{2,1,0:T(8,128)S(1)} %get-tuple-element.31), channel_id=1, source_target_pairs={{0,8},{4,12},{8,0},{12,4},{16,24},{20,28},{24,16},{28,20},{1,9},{5... | collective-permute-start | bytes 196616 | tf_op jit(solution)/shard_map/ppermute | solution.py:298
  30.0 7.5 %collective-permute-start.6 = (f32[2,32,256]{2,1,0:T(8,128)S(1)}, f32[2,32,256]{2,1,0:T(8,128)S(1)}, u32[]{:S(2)}, u32[]{:S(2)}) collective-permute-start(f32[2,32,256]{2,1,0:T(8,128)S(1)} %get-tuple-element.33), channel_id=1, source_target_pairs={{0,16},{4,20},{8,24},{12,28},{16,0},{20,4},{24,8},{28,12},{1,17},{... | collective-permute-start | bytes 196616 | tf_op jit(solution)/shard_map/ppermute | solution.py:298
  32.9 6.5 %collective-permute-start.7 = (f32[2,32,256]{2,1,0:T(8,128)S(1)}, f32[2,32,256]{2,1,0:T(8,128)S(1)}, u32[]{:S(2)}, u32[]{:S(2)}) collective-permute-start(f32[2,32,256]{2,1,0:T(8,128)S(1)} %get-tuple-element.35), channel_id=1, source_target_pairs={{0,24},{4,28},{8,16},{12,20},{16,8},{20,12},{24,0},{28,4},{1,25},{... | collective-permute-start | bytes 196616 | tf_op jit(solution)/shard_map/ppermute | solution.py:298
  34.4 7.8 %collective-permute-start.12 = (f32[2,256,128]{2,1,0:T(8,128)S(1)}, f32[2,256,128]{2,1,0:T(8,128)S(1)}, u32[]{:S(2)}, u32[]{:S(2)}) collective-permute-start(f32[2,256,128]{2,1,0:T(8,128)S(1)} %pad_maximum_fusion.2.refs_0_), channel_id=1, source_target_pairs={{0,4},{4,0},{8,12},{12,8},{16,20},{20,16},{24,28},{28,24},{1,5},{5... | collective-permute-start | bytes 786440 | tf_op jit(solution)/shard_map/ppermute | solution.py:302
  35.5 14.5 %collective-permute-start.10 = (f32[2,256,128]{2,1,0:T(8,128)S(1)}, f32[2,256,128]{2,1,0:T(8,128)S(1)}, u32[]{:S(2)}, u32[]{:S(2)}) collective-permute-start(f32[2,256,128]{2,1,0:T(8,128)S(1)} %pad_maximum_fusion.2.refs_0_), channel_id=1, source_target_pairs={{0,16},{4,20},{8,24},{12,28},{16,0},{20,4},{24,8},{28,12},{1,17},{... | collective-permute-start | bytes 786440 | tf_op jit(solution)/shard_map/ppermute | solution.py:298
  36.9 13.1 %collective-permute-start.16 = (f32[2,264,128]{2,1,0:T(8,128)S(1)}, f32[2,264,128]{2,1,0:T(8,128)S(1)}, u32[]{:S(2)}, u32[]{:S(2)}) collective-permute-start(f32[2,264,128]{2,1,0:T(8,128)S(1)} %collective-permute-done.14.refs_5_), channel_id=1, source_target_pairs={{0,4},{4,0},{8,12},{12,8},{16,20},{20,16},{24,28},{28,24},{1,3},{5... | collective-permute-start | bytes 811016 | tf_op jit(solution)/shard_map/ppermute | solution.py:315
  40.0 5.1 %collective-permute-start.8 = (f32[32,1024]{1,0:T(8,128)S(1)}, f32[32,1024]{1,0:T(8,128)S(1)}, u32[]{:S(2)}, u32[]{:S(2)}) collective-permute-start(f32[32,1024]{1,0:T(8,128)S(1)} %get-tuple-element.37), channel_id=1, source_target_pairs={{0,2},{1,3},{2,0},{3,1},{4,6},{5,7},{6,4},{7,5},{8,10},{9,11},{10,... | collective-permute-start | bytes 393224 | tf_op jit(solution)/shard_map/ppermute | solution.py:306
  42.2 8.4 %collective-permute-start.17 = (f32[2,264,128]{2,1,0:T(8,128)S(1)}, f32[2,264,128]{2,1,0:T(8,128)S(1)}, u32[]{:S(2)}, u32[]{:S(2)}) collective-permute-start(f32[2,264,128]{2,1,0:T(8,128)S(1)} %pad_maximum_fusion.refs_0_), channel_id=1, source_target_pairs={{0,1},{1,0},{2,3},{3,2},{4,5},{5,4},{6,7},{7,6},{8,9},{9,8},{10,11... | collective-permute-start | bytes 811016 | tf_op jit(solution)/shard_map/ppermute | solution.py:306
  42.2 8.5 %collective-permute-start.19 = (f32[2,264,128]{2,1,0:T(8,128)S(1)}, f32[2,264,128]{2,1,0:T(8,128)S(1)}, u32[]{:S(2)}, u32[]{:S(2)}) collective-permute-start(f32[2,264,128]{2,1,0:T(8,128)S(1)} %collective-permute-done.13.refs_2_), channel_id=1, source_target_pairs={{0,1},{1,0},{2,3},{3,2},{4,5},{5,4},{6,7},{7,6},{8,9},{9,8},{10,11... | collective-permute-start | bytes 811016 | tf_op jit(solution)/shard_map/ppermute | solution.py:306
  45.1 6.0 %collective-permute-start.18 = (f32[2,264,128]{2,1,0:T(8,128)S(1)}, f32[2,264,128]{2,1,0:T(8,128)S(1)}, u32[]{:S(2)}, u32[]{:S(2)}) collective-permute-start(f32[2,264,128]{2,1,0:T(8,128)S(1)} %collective-permute-done.3.refs_1_), channel_id=1, source_target_pairs={{0,1},{1,0},{2,3},{3,2},{4,5},{5,4},{6,7},{7,6},{8,9},{9,8},{10,11... | collective-permute-start | bytes 811016 | tf_op jit(solution)/shard_map/ppermute | solution.py:306
  50.6 2.7 %collective-permute-start.20 = (f32[2,264,128]{2,1,0:T(8,128)S(1)}, f32[2,264,128]{2,1,0:T(8,128)S(1)}, u32[]{:S(2)}, u32[]{:S(2)}) collective-permute-start(f32[2,264,128]{2,1,0:T(8,128)S(1)} %collective-permute-done.4.refs_3_), channel_id=1, source_target_pairs={{0,1},{1,0},{2,3},{3,2},{4,5},{5,4},{6,7},{7,6},{8,9},{9,8},{10,11... | collective-permute-start | bytes 811016 | tf_op jit(solution)/shard_map/ppermute | solution.py:306
  51.9 8.4 %collective-permute-start.25 = (f32[2,256,128]{2,1,0:T(8,128)S(1)}, f32[2,256,128]{2,1,0:T(8,128)S(1)}, u32[]{:S(2)}, u32[]{:S(2)}) collective-permute-start(f32[2,256,128]{2,1,0:T(8,128)S(1)} %collective-permute-done.10.refs_1_), channel_id=1, source_target_pairs={{0,4},{4,0},{8,12},{12,8},{16,20},{20,16},{24,28},{28,24},{1,5},{5... | collective-permute-start | bytes 786440 | tf_op jit(solution)/shard_map/ppermute | solution.py:302
  61.6 5.1 %collective-permute-start.26 = (f32[32,256]{1,0:T(8,128)S(1)}, f32[32,256]{1,0:T(8,128)S(1)}, u32[]{:S(2)}, u32[]{:S(2)}) collective-permute-start(f32[32,256]{1,0:T(8,128)S(1)} %get-tuple-element.50), channel_id=1, source_target_pairs={{0,2},{1,3},{2,0},{3,1},{4,6},{5,7},{6,4},{7,5},{8,10},{9,11},{10,... | collective-permute-start | bytes 98312 | tf_op jit(solution)/shard_map/ppermute | solution.py:306
  63.3 3.4 %collective-permute-start.27 = (f32[32,256]{1,0:T(8,128)S(1)}, f32[32,256]{1,0:T(8,128)S(1)}, u32[]{:S(2)}, u32[]{:S(2)}) collective-permute-start(f32[32,256]{1,0:T(8,128)S(1)} %get-tuple-element.51), channel_id=1, source_target_pairs={{0,1},{1,0},{2,3},{3,2},{4,5},{5,4},{6,7},{7,6},{8,9},{9,8},{10,11... | collective-permute-start | bytes 98312 | tf_op jit(solution)/shard_map/ppermute | solution.py:306
  63.3 3.4 %collective-permute-start.28 = (f32[32,256]{1,0:T(8,128)S(1)}, f32[32,256]{1,0:T(8,128)S(1)}, u32[]{:S(2)}, u32[]{:S(2)}) collective-permute-start(f32[32,256]{1,0:T(8,128)S(1)} %get-tuple-element.52), channel_id=1, source_target_pairs={{0,3},{1,2},{2,1},{3,0},{4,7},{5,6},{6,5},{7,4},{8,11},{9,10},{10,... | collective-permute-start | bytes 98312 | tf_op jit(solution)/shard_map/ppermute | solution.py:306
  (9 other events, 42.5 us)

commit v2 on v1

--- a/solution.py
+++ b/solution.py
@@ -141,7 +141,7 @@
 
 def origin(place_ref, crossed, first, second, m):
     rep, bulk = place_ref[0], place_ref[1]
-    if m < 2:
+    if m % 2 == 0:
         dx, dy = second, first
     else:
         core = (rep & 1) ^ crossed
@@ -156,8 +156,8 @@
         for m in range(4):
             for second in range(2):
                 for first in range(2):
-                    buf = bufs[8 * crossed + 4 * (m // 2) + 2 * second + first]
-                    found.append((buf.at[m % 2], (crossed, first, second, m)))
+                    buf = bufs[8 * crossed + 4 * (m % 2) + 2 * second + first]
+                    found.append((buf.at[m // 2], (crossed, first, second, m)))
     return found
 
 
@@ -226,7 +226,7 @@
     bulk = place_ref[1]
     for dy in range(2):
         for m in range(4):
-            h, l = split(held[2 * dy + m // 2][m % 2])
+            h, l = split(held[2 * dy + m % 2][m // 2])
             high[:, offset(bulk ^ (2 * m + dy), 128)] = h
             low[:, offset(bulk ^ (2 * m + dy), 128)] = l
     upd = mul(x_ref[...], (high[...], low[...]), NT)
@@ -351,15 +351,15 @@
     )
     coup = after(coupling, t)
 
-    near = jnp.stack([t, swap_z(t, 1)])
-    far = swap_z(near, 2)
+    near = jnp.stack([t, swap_z(t, 2)])
+    far = swap_z(near, 1)
     near0 = swap_y(near)
     near1 = swap_rep(near, 2)
     near01 = swap_rep(near0, 2)
 
     leave = call(leave_kernel, shape(4, 32, 256), [SMEM, VMEM], VMEM, [], LEAVE, 4, "leave")(place, blocks)
     came = swap_y(after(leave, t))
-    c_near = jnp.stack([coupling, swap_z(coup, 1)])
+    c_near = jnp.stack([coupling, swap_z(after(coup, near), 2)])
     c_near_got = swap_y(c_near)
 
     far_now = after(far, near0, near1, came, c_near)
@@ -368,10 +368,10 @@
     b_out = call(spread_kernel, [shape(2, 32, 256)] * 3, [SMEM, VMEM, VMEM], [VMEM] * 3, [], SPREAD, 4, "spread")(
         place, blocks, came
     )
-    b_z = [swap_z(after(b, far, near01), m + 1) for m, b in enumerate(b_out)]
-    c_far = swap_z(after(c_near, far, b_z[0]), 2)
+    b_z = [swap_z(after(b, far), m + 1) for m, b in enumerate(b_out)]
+    c_far = swap_z(after(c_near, far, b_z[0]), 1)
     c_far_got = swap_y(c_far)
-    far01 = cross(after(far0, far1), 1)
+    far01 = cross(after(far0, far1, near01), 1)
 
     left, both = call(
         rows_kernel,

time: 69 us -> 66.6 us (0.965)
  waiting for transfers between devices: 27.2 us -> 23.6 us
  starting transfers between devices: 25.6 us -> 26.9 us
    ppermute x7, waiting for transfers between devices: 20.2 us -> 14.7 us  [swap_z(): return lax.ppermute(x, 'bulk', [(k, k ^ 2 * m) for k in range(8)])]
    ppermute x4, waiting for transfers between devices: 3.81 us -> 5.03 us  [swap_y(): return lax.ppermute(x, 'bulk', [(k, k ^ 1) for k in range(8)])]
    ppermute x7, starting transfers between devices: 12 us -> 12.8 us  [swap_z(): return lax.ppermute(x, 'bulk', [(k, k ^ 2 * m) for k in range(8)])]
  transfers between devices with their start and end apart: 29 -> 29, of which waited for: 11 -> 10; matrix products, arithmetic and copies ran while one was open for 0% -> 0% of each run, Pallas kernels for 12% -> 12%
where the time goes in v2:
time: 66.6 us; the launch traced here: 66.4 us
  starting transfers between devices  26.9 us (40%)
  waiting for transfers between devices  23.6 us (35%)
  Pallas kernels  14 us (21%)
  local copies, waits for them, and re-layouts  1.59 us (2%)
    ppermute x7, waiting for transfers between devices, swap_z(): return lax.ppermute(x, 'bulk', [(k, k ^ 2 * m) for k in range(8)])  14.7 us
    ppermute x7, starting transfers between devices, swap_z(): return lax.ppermute(x, 'bulk', [(k, k ^ 2 * m) for k in range(8)])  12.8 us
    ppermute x15, starting transfers between devices, swap_rep(): return lax.ppermute(x, 'rep', [(k, k ^ bits) for k in range(4)])  6.6 us
    ppermute x4, starting transfers between devices, swap_y(): return lax.ppermute(x, 'bulk', [(k, k ^ 1) for k in range(8)])  5.34 us
    ppermute x4, waiting for transfers between devices, swap_y(): return lax.ppermute(x, 'bulk', [(k, k ^ 1) for k in range(8)])  5.03 us
    ppermute x15, waiting for transfers between devices, swap_rep(): return lax.ppermute(x, 'rep', [(k, k ^ bits) for k in range(4)])  3.89 us
    pallas_call x1, Pallas kernels, per_device(): call(first_kernel, shape(128, 1024), [SMEM] + [VMEM] * 18, VMEM, [pltpu.V...  3.58 us
    pallas_call x1, Pallas kernels, per_device(): call(second_factor_kernel, halves, [SMEM] + [VMEM] * 16, [VMEM] * 2, scra...  2.86 us
  transfers between devices with their start and end apart: 29, of which 10 were waited for; matrix products, arithmetic and copies ran while one was open for 0% of the time, Pallas kernels for 12%

profile of v2, /device:TPU:0, one launch (start us, length us, event | category | flops | bytes accessed | tf_op | source)
XLA Modules:
  0.0 66.4 jit_solution(2554826772049439652)
XLA Ops:
  1.7 2.6 %invert.1 = f32[264,128]{1,0:T(8,128)S(1)} custom-call(s32[2]{0:T(128)S(1)} %pad_add_fusion.place_ref, f32[256,128]{1,0:T(8,128)S(1)} %copy-done.1, f32[2,128]{1,0:T(2,128)S(1)} %copy-done.2), custom_call_target="tpu_custom_call" | custom-call | flops 3500000000 | bytes 2097152 | tf_op jit(solution)/shard_map/invert/pallas_call | solution.py:349
  4.2 2.1 %collective-permute-start.1 = (f32[264,128]{1,0:T(8,128)S(1)}, f32[264,128]{1,0:T(8,128)S(1)}, u32[]{:S(2)}, u32[]{:S(2)}) collective-permute-start(f32[264,128]{1,0:T(8,128)S(1)} %invert.1), channel_id=1, source_target_pairs={{0,16},{4,20},{8,24},{12,28},{16,0},{20,4},{24,8},{28,12},{1,17},{... | collective-permute-start | bytes 405512 | tf_op jit(solution)/shard_map/ppermute | solution.py:298
  6.3 6.8 %collective-permute-done.1 = f32[264,128]{1,0:T(8,128)S(1)} collective-permute-done((f32[264,128]{1,0:T(8,128)S(1)}, f32[264,128]{1,0:T(8,128)S(1)}, u32[]{:S(2)}, u32[]{:S(2)}) %collective-permute-start.1) | collective-permute-done | bytes 135200 | tf_op jit(solution)/shard_map/ppermute | solution.py:298
  13.1 2.0 %collective-permute-start.11 = (f32[2,264,128]{2,1,0:T(8,128)S(1)}, f32[2,264,128]{2,1,0:T(8,128)S(1)}, u32[]{:S(2)}, u32[]{:S(2)}) collective-permute-start(f32[2,264,128]{2,1,0:T(8,128)S(1)} %pad_maximum_fusion.refs_0_), channel_id=1, source_target_pairs={{0,4},{4,0},{8,12},{12,8},{16,20},{20,16},{24,28},{28,24},{1,5},{5... | collective-permute-start | bytes 811016 | tf_op jit(solution)/shard_map/ppermute | solution.py:302
  15.2 1.5 %collective-permute-start.12 = (f32[2,264,128]{2,1,0:T(8,128)S(1)}, f32[2,264,128]{2,1,0:T(8,128)S(1)}, u32[]{:S(2)}, u32[]{:S(2)}) collective-permute-start(f32[2,264,128]{2,1,0:T(8,128)S(1)} %pad_maximum_fusion.refs_0_), channel_id=1, source_target_pairs={{0,2},{1,3},{2,0},{3,1},{4,6},{5,7},{6,4},{7,5},{8,10},{9,11},{10,... | collective-permute-start | bytes 811016 | tf_op jit(solution)/shard_map/ppermute | solution.py:306
  16.7 2.7 %collective-permute-start.7 = (f32[256,128]{1,0:T(8,128)S(1)}, f32[256,128]{1,0:T(8,128)S(1)}, u32[]{:S(2)}, u32[]{:S(2)}) collective-permute-start(f32[256,128]{1,0:T(8,128)S(1)} %copy-done.3), channel_id=1, source_target_pairs={{0,16},{4,20},{8,24},{12,28},{16,0},{20,4},{24,8},{28,12},{1,17},{... | collective-permute-start | bytes 393224 | tf_op jit(solution)/shard_map/ppermute | solution.py:298
  20.5 1.2 %collective-permute-start.13 = (f32[2,264,128]{2,1,0:T(8,128)S(1)}, f32[2,264,128]{2,1,0:T(8,128)S(1)}, u32[]{:S(2)}, u32[]{:S(2)}) collective-permute-start(f32[2,264,128]{2,1,0:T(8,128)S(1)} %collective-permute-done.11.refs_1_), channel_id=1, source_target_pairs={{0,2},{1,3},{2,0},{3,1},{4,6},{5,7},{6,4},{7,5},{8,10},{9,11},{10,... | collective-permute-start | bytes 811016 | tf_op jit(solution)/shard_map/ppermute | solution.py:306
  21.7 3.2 %collective-permute-done.7 = f32[256,128]{1,0:T(8,128)S(1)} collective-permute-done((f32[256,128]{1,0:T(8,128)S(1)}, f32[256,128]{1,0:T(8,128)S(1)}, u32[]{:S(2)}, u32[]{:S(2)}) %collective-permute-start.7) | collective-permute-done | bytes 131104 | tf_op jit(solution)/shard_map/ppermute | solution.py:298
  27.2 3.5 %collective-permute-start.3 = (f32[2,32,256]{2,1,0:T(8,128)S(1)}, f32[2,32,256]{2,1,0:T(8,128)S(1)}, u32[]{:S(2)}, u32[]{:S(2)}) collective-permute-start(f32[2,32,256]{2,1,0:T(8,128)S(1)} %get-tuple-element.32), channel_id=1, source_target_pairs={{0,8},{4,12},{8,0},{12,4},{16,24},{20,28},{24,16},{28,20},{1,9},{5... | collective-permute-start | bytes 196616 | tf_op jit(solution)/shard_map/ppermute | solution.py:298
  30.7 1.6 %collective-permute-start.4 = (f32[2,32,256]{2,1,0:T(8,128)S(1)}, f32[2,32,256]{2,1,0:T(8,128)S(1)}, u32[]{:S(2)}, u32[]{:S(2)}) collective-permute-start(f32[2,32,256]{2,1,0:T(8,128)S(1)} %get-tuple-element.34), channel_id=1, source_target_pairs={{0,16},{4,20},{8,24},{12,28},{16,0},{20,4},{24,8},{28,12},{1,17},{... | collective-permute-start | bytes 196616 | tf_op jit(solution)/shard_map/ppermute | solution.py:298
  32.3 1.3 %collective-permute-done.3.b1 = f32[2,32,256]{2,1,0:T(8,128)S(1)} collective-permute-done((f32[2,32,256]{2,1,0:T(8,128)S(1)}, f32[2,32,256]{2,1,0:T(8,128)S(1)}, u32[]{:S(2)}, u32[]{:S(2)}) %collective-permute-start.3) | collective-permute-done | bytes 65568 | tf_op jit(solution)/shard_map/ppermute | solution.py:298
  33.7 2.4 %collective-permute-start.5 = (f32[2,32,256]{2,1,0:T(8,128)S(1)}, f32[2,32,256]{2,1,0:T(8,128)S(1)}, u32[]{:S(2)}, u32[]{:S(2)}) collective-permute-start(f32[2,32,256]{2,1,0:T(8,128)S(1)} %get-tuple-element.36), channel_id=1, source_target_pairs={{0,24},{4,28},{8,16},{12,20},{16,8},{20,12},{24,0},{28,4},{1,25},{... | collective-permute-start | bytes 196616 | tf_op jit(solution)/shard_map/ppermute | solution.py:298
  36.6 1.2 %collective-permute-start.16 = (f32[2,264,128]{2,1,0:T(8,128)S(1)}, f32[2,264,128]{2,1,0:T(8,128)S(1)}, u32[]{:S(2)}, u32[]{:S(2)}) collective-permute-start(f32[2,264,128]{2,1,0:T(8,128)S(1)} %collective-permute-done.14.refs_5_), channel_id=1, source_target_pairs={{0,4},{4,0},{8,12},{12,8},{16,20},{20,16},{24,28},{28,24},{1,3},{5... | collective-permute-start | bytes 811016 | tf_op jit(solution)/shard_map/ppermute | solution.py:315
  37.7 2.7 %collective-permute-done.5.b3 = f32[2,32,256]{2,1,0:T(8,128)S(1)} collective-permute-done((f32[2,32,256]{2,1,0:T(8,128)S(1)}, f32[2,32,256]{2,1,0:T(8,128)S(1)}, u32[]{:S(2)}, u32[]{:S(2)}) %collective-permute-start.5) | collective-permute-done | bytes 65568 | tf_op jit(solution)/shard_map/ppermute | solution.py:298
  41.1 1.5 %collective-permute-start.10 = (f32[2,256,128]{2,1,0:T(8,128)S(1)}, f32[2,256,128]{2,1,0:T(8,128)S(1)}, u32[]{:S(2)}, u32[]{:S(2)}) collective-permute-start(f32[2,256,128]{2,1,0:T(8,128)S(1)} %pad_maximum_fusion.2.refs_0_), channel_id=1, source_target_pairs={{0,4},{4,0},{8,12},{12,8},{16,20},{20,16},{24,28},{28,24},{1,5},{5... | collective-permute-start | bytes 786440 | tf_op jit(solution)/shard_map/ppermute | solution.py:302
  42.7 3.4 %collective-permute-done.6 = f32[32,1024]{1,0:T(8,128)S(1)} collective-permute-done((f32[32,1024]{1,0:T(8,128)S(1)}, f32[32,1024]{1,0:T(8,128)S(1)}, u32[]{:S(2)}, u32[]{:S(2)}) %collective-permute-start.6) | collective-permute-done | bytes 131104 | tf_op jit(solution)/shard_map/ppermute | solution.py:306
  46.7 2.0 %collective-permute-done.10.refs_2_ = f32[2,256,128]{2,1,0:T(8,128)S(1)} collective-permute-done((f32[2,256,128]{2,1,0:T(8,128)S(1)}, f32[2,256,128]{2,1,0:T(8,128)S(1)}, u32[]{:S(2)}, u32[]{:S(2)}) %collective-permute-start.10) | collective-permute-done | bytes 262176 | tf_op jit(solution)/shard_map/ppermute | solution.py:302
  49.7 1.2 %collective-permute-start.25 = (f32[2,256,128]{2,1,0:T(8,128)S(1)}, f32[2,256,128]{2,1,0:T(8,128)S(1)}, u32[]{:S(2)}, u32[]{:S(2)}) collective-permute-start(f32[2,256,128]{2,1,0:T(8,128)S(1)} %collective-permute-done.8.refs_1_), channel_id=1, source_target_pairs={{0,4},{4,0},{8,12},{12,8},{16,20},{20,16},{24,28},{28,24},{1,5},{5... | collective-permute-start | bytes 786440 | tf_op jit(solution)/shard_map/ppermute | solution.py:302
  51.3 3.6 %first_panel.1.x_ref = f32[128,1024]{1,0:T(8,128)S(1)} custom-call(s32[2]{0:T(128)S(1)} %pad_add_fusion.place_ref, f32[2,32,1024]{2,1,0:T(8,128)S(1)} %pad_maximum_fusion.1.pair, f32[2,32,1024]{2,1,0:T(8,128)S(1)} %collective-permute-done.9.other_pair, f32[2,264,128]{2,1,0:T(8,128)S(1)} %pad_maximum_fusion.refs_0_, ...), custom_call_target="tpu_custom_call" | custom-call | flops 200000000 | bytes 2097152 | tf_op jit(solution)/shard_map/first_panel/pallas_call | solution.py:393
  54.9 3.0 %collective-permute-done.25.refs_3_ = f32[2,256,128]{2,1,0:T(8,128)S(1)} collective-permute-done((f32[2,256,128]{2,1,0:T(8,128)S(1)}, f32[2,256,128]{2,1,0:T(8,128)S(1)}, u32[]{:S(2)}, u32[]{:S(2)}) %collective-permute-start.25) | collective-permute-done | bytes 262176 | tf_op jit(solution)/shard_map/ppermute | solution.py:302
  58.0 1.3 %update.1 = (f32[32,256]{1,0:T(8,128)S(1)}, f32[32,256]{1,0:T(8,128)S(1)}, f32[32,256]{1,0:T(8,128)S(1)}, f32[32,256]{1,0:T(8,128)S(1)}) custom-call(s32[2]{0:T(128)S(1)} %pad_add_fusion.place_ref, f32[128,1024]{1,0:T(8,128)S(1)} %first_panel.1.x_ref, f32[2,256,128]{2,1,0:T(8,128)S(1)} %pad_maximum_fusion.2.refs_0_, ...), custom_call_target="tpu_custom_call" | custom-call | flops 2000000000 | bytes 2097152 | tf_op jit(solution)/shard_map/update/pallas_call | solution.py:404
  59.2 1.7 %collective-permute-start.26 = (f32[32,256]{1,0:T(8,128)S(1)}, f32[32,256]{1,0:T(8,128)S(1)}, u32[]{:S(2)}, u32[]{:S(2)}) collective-permute-start(f32[32,256]{1,0:T(8,128)S(1)} %get-tuple-element.52), channel_id=1, source_target_pairs={{0,2},{1,3},{2,0},{3,1},{4,6},{5,7},{6,4},{7,5},{8,10},{9,11},{10,... | collective-permute-start | bytes 98312 | tf_op jit(solution)/shard_map/ppermute | solution.py:306
  61.4 2.9 %second_factor.1 = (bf16[1024,1024]{1,0:T(8,128)(2,1)S(1)}, bf16[1024,1024]{1,0:T(8,128)(2,1)S(1)}) custom-call(s32[2]{0:T(128)S(1)} %pad_add_fusion.place_ref, f32[2,264,128]{2,1,0:T(8,128)S(1)} %pad_maximum_fusion.refs_0_, f32[2,264,128]{2,1,0:T(8,128)S(1)} %collective-permute-done.11.refs_1_, f32[2,264,128]{2,1,0:T(8,128)S(1)} %collective-permute-done.12.refs_2_, ...), custom_call_target="tpu_custom_call" | custom-call | flops 3000000000 | bytes 2097152 | tf_op jit(solution)/shard_map/second_factor/pallas_call | solution.py:416
  64.3 2.1 %second_panel.1 = f32[32,2048]{1,0:T(8,128)} custom-call(s32[2]{0:T(128)S(1)} %pad_add_fusion.place_ref, f32[128,1024]{1,0:T(8,128)S(1)} %first_panel.1.x_ref, f32[2,32,1024]{2,1,0:T(8,128)S(1)} %get-tuple-element.47.both_ref, bf16[1024,1024]{1,0:T(8,128)(2,1)S(1)} %get-tuple-element.50.uh_ref, bf16[1024,1024]{1,0:T(8,128)(2,1)S(1)} %get-tuple-element.51.ul_ref, ...), custom_call_target="tpu_custom_call" | custom-call | flops 2500000000 | bytes 2097152 | tf_op jit(solution)/shard_map/second_panel/pallas_call | solution.py:420
  (54 shorter events, 9.0 us)
Async XLA Ops:
  4.2 8.9 %collective-permute-start.1 = (f32[264,128]{1,0:T(8,128)S(1)}, f32[264,128]{1,0:T(8,128)S(1)}, u32[]{:S(2)}, u32[]{:S(2)}) collective-permute-start(f32[264,128]{1,0:T(8,128)S(1)} %invert.1), channel_id=1, source_target_pairs={{0,16},{4,20},{8,24},{12,28},{16,0},{20,4},{24,8},{28,12},{1,17},{... | collective-permute-start | bytes 405512 | tf_op jit(solution)/shard_map/ppermute | solution.py:298
  13.1 7.4 %collective-permute-start.11 = (f32[2,264,128]{2,1,0:T(8,128)S(1)}, f32[2,264,128]{2,1,0:T(8,128)S(1)}, u32[]{:S(2)}, u32[]{:S(2)}) collective-permute-start(f32[2,264,128]{2,1,0:T(8,128)S(1)} %pad_maximum_fusion.refs_0_), channel_id=1, source_target_pairs={{0,4},{4,0},{8,12},{12,8},{16,20},{20,16},{24,28},{28,24},{1,5},{5... | collective-permute-start | bytes 811016 | tf_op jit(solution)/shard_map/ppermute | solution.py:302
  15.2 9.8 %collective-permute-start.12 = (f32[2,264,128]{2,1,0:T(8,128)S(1)}, f32[2,264,128]{2,1,0:T(8,128)S(1)}, u32[]{:S(2)}, u32[]{:S(2)}) collective-permute-start(f32[2,264,128]{2,1,0:T(8,128)S(1)} %pad_maximum_fusion.refs_0_), channel_id=1, source_target_pairs={{0,2},{1,3},{2,0},{3,1},{4,6},{5,7},{6,4},{7,5},{8,10},{9,11},{10,... | collective-permute-start | bytes 811016 | tf_op jit(solution)/shard_map/ppermute | solution.py:306
  16.7 9.0 %collective-permute-start.2 = (f32[2,264,128]{2,1,0:T(8,128)S(1)}, f32[2,264,128]{2,1,0:T(8,128)S(1)}, u32[]{:S(2)}, u32[]{:S(2)}) collective-permute-start(f32[2,264,128]{2,1,0:T(8,128)S(1)} %pad_maximum_fusion.refs_0_), channel_id=1, source_target_pairs={{0,8},{4,12},{8,0},{12,4},{16,24},{20,28},{24,16},{28,20},{1,9},{5... | collective-permute-start | bytes 811016 | tf_op jit(solution)/shard_map/ppermute | solution.py:298
  16.7 8.2 %collective-permute-start.7 = (f32[256,128]{1,0:T(8,128)S(1)}, f32[256,128]{1,0:T(8,128)S(1)}, u32[]{:S(2)}, u32[]{:S(2)}) collective-permute-start(f32[256,128]{1,0:T(8,128)S(1)} %copy-done.3), channel_id=1, source_target_pairs={{0,16},{4,20},{8,24},{12,28},{16,0},{20,4},{24,8},{28,12},{1,17},{... | collective-permute-start | bytes 393224 | tf_op jit(solution)/shard_map/ppermute | solution.py:298
  19.9 5.0 %collective-permute-start = (f32[4,32,256]{2,1,0:T(8,128)S(1)}, f32[4,32,256]{2,1,0:T(8,128)S(1)}, u32[]{:S(2)}, u32[]{:S(2)}) collective-permute-start(f32[4,32,256]{2,1,0:T(8,128)S(1)} %leave.1), channel_id=1, source_target_pairs={{0,4},{4,0},{8,12},{12,8},{16,20},{20,16},{24,28},{28,24},{1,5},{5... | collective-permute-start | bytes 393224 | tf_op jit(solution)/shard_map/ppermute | solution.py:302
  20.5 15.5 %collective-permute-start.13 = (f32[2,264,128]{2,1,0:T(8,128)S(1)}, f32[2,264,128]{2,1,0:T(8,128)S(1)}, u32[]{:S(2)}, u32[]{:S(2)}) collective-permute-start(f32[2,264,128]{2,1,0:T(8,128)S(1)} %collective-permute-done.11.refs_1_), channel_id=1, source_target_pairs={{0,2},{1,3},{2,0},{3,1},{4,6},{5,7},{6,4},{7,5},{8,10},{9,11},{10,... | collective-permute-start | bytes 811016 | tf_op jit(solution)/shard_map/ppermute | solution.py:306
  25.6 10.4 %collective-permute-start.15 = (f32[2,264,128]{2,1,0:T(8,128)S(1)}, f32[2,264,128]{2,1,0:T(8,128)S(1)}, u32[]{:S(2)}, u32[]{:S(2)}) collective-permute-start(f32[2,264,128]{2,1,0:T(8,128)S(1)} %collective-permute-done.2.refs_4_), channel_id=1, source_target_pairs={{0,4},{4,0},{8,12},{12,8},{16,20},{20,16},{24,28},{28,24},{1,3},{5... | collective-permute-start | bytes 811016 | tf_op jit(solution)/shard_map/ppermute | solution.py:315
  26.1 10.4 %collective-permute-start.14 = (f32[2,264,128]{2,1,0:T(8,128)S(1)}, f32[2,264,128]{2,1,0:T(8,128)S(1)}, u32[]{:S(2)}, u32[]{:S(2)}) collective-permute-start(f32[2,264,128]{2,1,0:T(8,128)S(1)} %collective-permute-done.2.refs_4_), channel_id=1, source_target_pairs={{0,2},{4,6},{8,10},{12,14},{16,18},{20,22},{24,26},{28,30},{1,5},{... | collective-permute-start | bytes 811016 | tf_op jit(solution)/shard_map/ppermute | solution.py:315
  27.2 6.4 %collective-permute-start.3 = (f32[2,32,256]{2,1,0:T(8,128)S(1)}, f32[2,32,256]{2,1,0:T(8,128)S(1)}, u32[]{:S(2)}, u32[]{:S(2)}) collective-permute-start(f32[2,32,256]{2,1,0:T(8,128)S(1)} %get-tuple-element.32), channel_id=1, source_target_pairs={{0,8},{4,12},{8,0},{12,4},{16,24},{20,28},{24,16},{28,20},{1,9},{5... | collective-permute-start | bytes 196616 | tf_op jit(solution)/shard_map/ppermute | solution.py:298
  30.7 7.0 %collective-permute-start.4 = (f32[2,32,256]{2,1,0:T(8,128)S(1)}, f32[2,32,256]{2,1,0:T(8,128)S(1)}, u32[]{:S(2)}, u32[]{:S(2)}) collective-permute-start(f32[2,32,256]{2,1,0:T(8,128)S(1)} %get-tuple-element.34), channel_id=1, source_target_pairs={{0,16},{4,20},{8,24},{12,28},{16,0},{20,4},{24,8},{28,12},{1,17},{... | collective-permute-start | bytes 196616 | tf_op jit(solution)/shard_map/ppermute | solution.py:298
  33.7 6.8 %collective-permute-start.5 = (f32[2,32,256]{2,1,0:T(8,128)S(1)}, f32[2,32,256]{2,1,0:T(8,128)S(1)}, u32[]{:S(2)}, u32[]{:S(2)}) collective-permute-start(f32[2,32,256]{2,1,0:T(8,128)S(1)} %get-tuple-element.36), channel_id=1, source_target_pairs={{0,24},{4,28},{8,16},{12,20},{16,8},{20,12},{24,0},{28,4},{1,25},{... | collective-permute-start | bytes 196616 | tf_op jit(solution)/shard_map/ppermute | solution.py:298
  36.0 6.6 %collective-permute-start.17 = (f32[2,264,128]{2,1,0:T(8,128)S(1)}, f32[2,264,128]{2,1,0:T(8,128)S(1)}, u32[]{:S(2)}, u32[]{:S(2)}) collective-permute-start(f32[2,264,128]{2,1,0:T(8,128)S(1)} %pad_maximum_fusion.refs_0_), channel_id=1, source_target_pairs={{0,1},{1,0},{2,3},{3,2},{4,5},{5,4},{6,7},{7,6},{8,9},{9,8},{10,11... | collective-permute-start | bytes 811016 | tf_op jit(solution)/shard_map/ppermute | solution.py:306
  36.1 10.0 %collective-permute-start.8 = (f32[2,256,128]{2,1,0:T(8,128)S(1)}, f32[2,256,128]{2,1,0:T(8,128)S(1)}, u32[]{:S(2)}, u32[]{:S(2)}) collective-permute-start(f32[2,256,128]{2,1,0:T(8,128)S(1)} %pad_maximum_fusion.2.refs_0_), channel_id=1, source_target_pairs={{0,8},{4,12},{8,0},{12,4},{16,24},{20,28},{24,16},{28,20},{1,9},{5... | collective-permute-start | bytes 786440 | tf_op jit(solution)/shard_map/ppermute | solution.py:298
  36.6 10.0 %collective-permute-start.16 = (f32[2,264,128]{2,1,0:T(8,128)S(1)}, f32[2,264,128]{2,1,0:T(8,128)S(1)}, u32[]{:S(2)}, u32[]{:S(2)}) collective-permute-start(f32[2,264,128]{2,1,0:T(8,128)S(1)} %collective-permute-done.14.refs_5_), channel_id=1, source_target_pairs={{0,4},{4,0},{8,12},{12,8},{16,20},{20,16},{24,28},{28,24},{1,3},{5... | collective-permute-start | bytes 811016 | tf_op jit(solution)/shard_map/ppermute | solution.py:315
  41.0 5.0 %collective-permute-start.6 = (f32[32,1024]{1,0:T(8,128)S(1)}, f32[32,1024]{1,0:T(8,128)S(1)}, u32[]{:S(2)}, u32[]{:S(2)}) collective-permute-start(f32[32,1024]{1,0:T(8,128)S(1)} %get-tuple-element.38), channel_id=1, source_target_pairs={{0,2},{1,3},{2,0},{3,1},{4,6},{5,7},{6,4},{7,5},{8,10},{9,11},{10,... | collective-permute-start | bytes 393224 | tf_op jit(solution)/shard_map/ppermute | solution.py:306
  41.1 7.5 %collective-permute-start.10 = (f32[2,256,128]{2,1,0:T(8,128)S(1)}, f32[2,256,128]{2,1,0:T(8,128)S(1)}, u32[]{:S(2)}, u32[]{:S(2)}) collective-permute-start(f32[2,256,128]{2,1,0:T(8,128)S(1)} %pad_maximum_fusion.2.refs_0_), channel_id=1, source_target_pairs={{0,4},{4,0},{8,12},{12,8},{16,20},{20,16},{24,28},{28,24},{1,5},{5... | collective-permute-start | bytes 786440 | tf_op jit(solution)/shard_map/ppermute | solution.py:302
  42.7 6.0 %collective-permute-start.19 = (f32[2,264,128]{2,1,0:T(8,128)S(1)}, f32[2,264,128]{2,1,0:T(8,128)S(1)}, u32[]{:S(2)}, u32[]{:S(2)}) collective-permute-start(f32[2,264,128]{2,1,0:T(8,128)S(1)} %collective-permute-done.12.refs_2_), channel_id=1, source_target_pairs={{0,1},{1,0},{2,3},{3,2},{4,5},{5,4},{6,7},{7,6},{8,9},{9,8},{10,11... | collective-permute-start | bytes 811016 | tf_op jit(solution)/shard_map/ppermute | solution.py:306
  46.0 3.1 %collective-permute-start.18 = (f32[2,264,128]{2,1,0:T(8,128)S(1)}, f32[2,264,128]{2,1,0:T(8,128)S(1)}, u32[]{:S(2)}, u32[]{:S(2)}) collective-permute-start(f32[2,264,128]{2,1,0:T(8,128)S(1)} %collective-permute-done.11.refs_1_), channel_id=1, source_target_pairs={{0,1},{1,0},{2,3},{3,2},{4,5},{5,4},{6,7},{7,6},{8,9},{9,8},{10,11... | collective-permute-start | bytes 811016 | tf_op jit(solution)/shard_map/ppermute | solution.py:306
  46.1 3.2 %collective-permute-start.21 = (f32[2,264,128]{2,1,0:T(8,128)S(1)}, f32[2,264,128]{2,1,0:T(8,128)S(1)}, u32[]{:S(2)}, u32[]{:S(2)}) collective-permute-start(f32[2,264,128]{2,1,0:T(8,128)S(1)} %collective-permute-done.2.refs_4_), channel_id=1, source_target_pairs={{0,1},{1,0},{2,3},{3,2},{4,5},{5,4},{6,7},{7,6},{8,9},{9,8},{10,11... | collective-permute-start | bytes 811016 | tf_op jit(solution)/shard_map/ppermute | solution.py:306
  49.7 8.3 %collective-permute-start.25 = (f32[2,256,128]{2,1,0:T(8,128)S(1)}, f32[2,256,128]{2,1,0:T(8,128)S(1)}, u32[]{:S(2)}, u32[]{:S(2)}) collective-permute-start(f32[2,256,128]{2,1,0:T(8,128)S(1)} %collective-permute-done.8.refs_1_), channel_id=1, source_target_pairs={{0,4},{4,0},{8,12},{12,8},{16,20},{20,16},{24,28},{28,24},{1,5},{5... | collective-permute-start | bytes 786440 | tf_op jit(solution)/shard_map/ppermute | solution.py:302
  59.2 5.1 %collective-permute-start.26 = (f32[32,256]{1,0:T(8,128)S(1)}, f32[32,256]{1,0:T(8,128)S(1)}, u32[]{:S(2)}, u32[]{:S(2)}) collective-permute-start(f32[32,256]{1,0:T(8,128)S(1)} %get-tuple-element.52), channel_id=1, source_target_pairs={{0,2},{1,3},{2,0},{3,1},{4,6},{5,7},{6,4},{7,5},{8,10},{9,11},{10,... | collective-permute-start | bytes 98312 | tf_op jit(solution)/shard_map/ppermute | solution.py:306
  61.0 3.4 %collective-permute-start.27 = (f32[32,256]{1,0:T(8,128)S(1)}, f32[32,256]{1,0:T(8,128)S(1)}, u32[]{:S(2)}, u32[]{:S(2)}) collective-permute-start(f32[32,256]{1,0:T(8,128)S(1)} %get-tuple-element.53), channel_id=1, source_target_pairs={{0,1},{1,0},{2,3},{3,2},{4,5},{5,4},{6,7},{7,6},{8,9},{9,8},{10,11... | collective-permute-start | bytes 98312 | tf_op jit(solution)/shard_map/ppermute | solution.py:306
  61.0 3.4 %collective-permute-start.28 = (f32[32,256]{1,0:T(8,128)S(1)}, f32[32,256]{1,0:T(8,128)S(1)}, u32[]{:S(2)}, u32[]{:S(2)}) collective-permute-start(f32[32,256]{1,0:T(8,128)S(1)} %get-tuple-element.54), channel_id=1, source_target_pairs={{0,3},{1,2},{2,1},{3,0},{4,7},{5,6},{6,5},{7,4},{8,11},{9,10},{10,... | collective-permute-start | bytes 98312 | tf_op jit(solution)/shard_map/ppermute | solution.py:306
  (9 other events, 45.7 us)

commit v3 on v2

--- a/solution.py
+++ b/solution.py
@@ -139,6 +139,11 @@
     left[...] = both[0]
 
 
+def pair_kernel(left, left_x, later, out):
+    out[0] = left[...]
+    out[1] = left_x[...]
+
+
 def origin(place_ref, crossed, first, second, m):
     rep, bulk = place_ref[0], place_ref[1]
     if m % 2 == 0:
@@ -153,11 +158,15 @@
 def pieces(bufs):
     found = []
     for crossed in range(2):
+        near, far, far01 = bufs[3 * crossed : 3 * crossed + 3]
         for m in range(4):
             for second in range(2):
                 for first in range(2):
-                    buf = bufs[8 * crossed + 4 * (m % 2) + 2 * second + first]
-                    found.append((buf.at[m // 2], (crossed, first, second, m)))
+                    entry = 2 * (2 * second + first) + m // 2
+                    buf = near if m % 2 == 0 else far
+                    if entry > 5 and m % 2 == 1:
+                        buf, entry = far01, m // 2
+                    found.append((buf.at[entry], (crossed, first, second, m)))
     return found
 
 
@@ -196,7 +205,7 @@
 
 
 def first_kernel(place_ref, pair, other_pair, *refs):
-    bufs, (x_ref, high, low, diag) = refs[:16], refs[16:]
+    bufs, (x_ref, high, low, diag) = refs[:6], refs[6:]
     place_pieces(place_ref, bufs, False, high, low, diag)
     n = 128
     i, j = iotas(n)
@@ -235,7 +244,7 @@
 
 
 def second_factor_kernel(place_ref, *refs):
-    bufs, (high, low, diag) = refs[:16], refs[16:]
+    bufs, (high, low, diag) = refs[:6], refs[6:]
     place_pieces(place_ref, bufs, True, high, low, diag)
     n = 128
     i, j = iotas(n)
@@ -291,7 +300,7 @@
 
 BOTH = ("bulk", "rep")
 
-SPREAD, INVERT, LEAVE, ROWS, FIRST, SECOND = 1_000_000_000, 3_500_000_000, 500_000_000, 1_000_000_000, 200_000_000, 3_000_000_000
+SPREAD, INVERT, LEAVE, ROWS, FIRST, SECOND, PAIR = 1_000_000_000, 3_500_000_000, 500_000_000, 1_000_000_000, 200_000_000, 3_000_000_000, 4_000_000_000
 
 
 def swap_z(x, m):
@@ -362,16 +371,16 @@
     c_near = jnp.stack([coupling, swap_z(after(coup, near), 2)])
     c_near_got = swap_y(c_near)
 
-    far_now = after(far, near0, near1, came, c_near)
+    far_now = after(far, near0, near1, came)
     far0 = cross(far_now, 0)
     far1 = cross(far_now, 1)
     b_out = call(spread_kernel, [shape(2, 32, 256)] * 3, [SMEM, VMEM, VMEM], [VMEM] * 3, [], SPREAD, 4, "spread")(
         place, blocks, came
     )
-    b_z = [swap_z(after(b, far), m + 1) for m, b in enumerate(b_out)]
+    b_z = [swap_z(after(b, far, c_near, near01), m + 1) for m, b in enumerate(b_out)]
     c_far = swap_z(after(c_near, far, b_z[0]), 1)
     c_far_got = swap_y(c_far)
-    far01 = cross(after(far0, far1, near01), 1)
+    far01 = cross(after(far0, far1), 1)
 
     left, both = call(
         rows_kernel,
@@ -383,17 +392,20 @@
         4,
         "rows",
     )(place, blocks, came, *b_z)
-    pair = jnp.stack([left, swap_rep(after(left, came), 2)])
-    other_pair = swap_rep(after(pair, c_far), 1)
-    bufs = [near, near0, near1, near01, far, far0, far1, far01]
-    bufs += [swap_rep(b, 1) for b in bufs[:7]] + [swap_rep(after(far01, far1), 1)]
+    left_x = swap_rep(left, 2)
+    pair = call(pair_kernel, shape(2, 32, 1024), [VMEM] * 3, VMEM, [], PAIR, 4, "pair")(left, left_x, c_far)
+    other_pair = swap_rep(pair, 1)
+    near_all = jnp.concatenate([near, near0, near1, near01], axis=0)
+    far_all = jnp.concatenate([far, far0, far1], axis=0)
+    bufs = [near_all, far_all, far01]
+    bufs += [swap_rep(after(near_all, *b_z), 1), swap_rep(after(far_all, far1), 1), swap_rep(after(far01, far1), 1)]
 
     scratch = [pltpu.VMEM((8, 136, 128), F32)]
     halves = [shape(1024, 1024, dtype=BF16)] * 2
     x = call(
         first_kernel,
         shape(128, 1024),
-        [SMEM] + [VMEM] * 18,
+        [SMEM] + [VMEM] * 8,
         VMEM,
         [pltpu.VMEM((1024, 1024), BF16)] * 2 + scratch,
         FIRST,
@@ -414,7 +426,7 @@
     back = [swap_rep(to_x, 2), swap_rep(to_core, 1), swap_rep(to_both, 3)]
 
     uh, ul = call(
-        second_factor_kernel, halves, [SMEM] + [VMEM] * 16, [VMEM] * 2, scratch, SECOND, 24, "second_factor"
+        second_factor_kernel, halves, [SMEM] + [VMEM] * 6, [VMEM] * 2, scratch, SECOND, 24, "second_factor"
     )(after(place, mine), *bufs)
 
     return call(second_kernel, shape(32, 2048), [SMEM] + [VMEM] * 8, VMEM, [], 2_500_000_000, 24, "second_panel")(

time: 66.6 us -> 76.1 us (1.14)
  waiting for transfers between devices: 23.6 us -> 37.3 us
  starting transfers between devices: 26.9 us -> 22.5 us
    ppermute x15 -> x10, waiting for transfers between devices: 3.89 us -> 14.1 us  [swap_rep(): return lax.ppermute(x, 'rep', [(k, k ^ bits) for k in range(4)])]
    ppermute x7, starting transfers between devices: 12.8 us -> 8.78 us  [swap_z(): return lax.ppermute(x, 'bulk', [(k, k ^ 2 * m) for k in range(8)])]
    ppermute x4, waiting for transfers between devices: 5.03 us -> 8.02 us  [swap_y(): return lax.ppermute(x, 'bulk', [(k, k ^ 1) for k in range(8)])]
    ppermute x15 -> x10, starting transfers between devices: 6.6 us -> 8.21 us  [swap_rep(): return lax.ppermute(x, 'rep', [(k, k ^ bits) for k in range(4)])]
    ppermute x4, starting transfers between devices: 5.34 us -> 4.12 us  [swap_y(): return lax.ppermute(x, 'bulk', [(k, k ^ 1) for k in range(8)])]
    ppermute x3, starting transfers between devices: 2.19 us -> 1.37 us  [cross(): return lax.ppermute(x, BOTH, pairs)]
    unnamed x8 -> x14, local copies, waits for them, and re-layouts: 1.59 us -> 1.69 us
    pallas_call x2 -> x3, Pallas kernels: 6.44 us -> 6.51 us  [the longest x1 3.58 us: per_device(): call(first_kernel, shape(128, 1024), [SMEM] + [VMEM] * 8, VMEM, [pltpu.VM...]
  transfers between devices with their start and end apart: 29 -> 24, of which waited for: 10 -> 11; matrix products, arithmetic and copies ran while one was open for 0% -> 0% of each run, Pallas kernels for 12% -> 11%
where the time goes in v3:
time: 76.1 us; the launch traced here: 75.9 us
  waiting for transfers between devices  37.3 us (49%)
  starting transfers between devices  22.5 us (30%)
  Pallas kernels  14.1 us (19%)
  local copies, waits for them, and re-layouts  1.73 us (2%)
    ppermute x7, waiting for transfers between devices, swap_z(): return lax.ppermute(x, 'bulk', [(k, k ^ 2 * m) for k in range(8)])  15.2 us
    ppermute x10, waiting for transfers between devices, swap_rep(): return lax.ppermute(x, 'rep', [(k, k ^ bits) for k in range(4)])  14.1 us
    ppermute x7, starting transfers between devices, swap_z(): return lax.ppermute(x, 'bulk', [(k, k ^ 2 * m) for k in range(8)])  8.78 us
    ppermute x10, starting transfers between devices, swap_rep(): return lax.ppermute(x, 'rep', [(k, k ^ bits) for k in range(4)])  8.21 us
    ppermute x4, waiting for transfers between devices, swap_y(): return lax.ppermute(x, 'bulk', [(k, k ^ 1) for k in range(8)])  8.02 us
    ppermute x4, starting transfers between devices, swap_y(): return lax.ppermute(x, 'bulk', [(k, k ^ 1) for k in range(8)])  4.12 us
    pallas_call x1, Pallas kernels, per_device(): call(first_kernel, shape(128, 1024), [SMEM] + [VMEM] * 8, VMEM, [pltpu.VM...  3.58 us
    pallas_call x1, Pallas kernels, per_device(): call(second_factor_kernel, halves, [SMEM] + [VMEM] * 6, [VMEM] * 2, scrat...  2.91 us
  transfers between devices with their start and end apart: 24, of which 11 were waited for; matrix products, arithmetic and copies ran while one was open for 0% of the time, Pallas kernels for 11%

profile of v3, /device:TPU:0, one launch (start us, length us, event | category | flops | bytes accessed | tf_op | source)
XLA Modules:
  0.0 75.9 jit_solution(10005865458207503900)
XLA Ops:
  0.1 0.9 %copy-done.1 = f32[256,128]{1,0:T(8,128)S(1)} copy-done((f32[256,128]{1,0:T(8,128)S(1)}, f32[256,128]{1,0:T(8,128)}, u32[]{:S(2)}) %copy-start.1) | copy-done | bytes 131096
  1.7 2.6 %invert.1 = f32[264,128]{1,0:T(8,128)S(1)} custom-call(s32[2]{0:T(128)S(1)} %pad_add_fusion.place_ref, f32[256,128]{1,0:T(8,128)S(1)} %copy-done.1, f32[2,128]{1,0:T(2,128)S(1)} %copy-done.2), custom_call_target="tpu_custom_call" | custom-call | flops 3500000000 | bytes 2097152 | tf_op jit(solution)/shard_map/invert/pallas_call | solution.py:358
  4.2 2.1 %collective-permute-start.1 = (f32[264,128]{1,0:T(8,128)S(1)}, f32[264,128]{1,0:T(8,128)S(1)}, u32[]{:S(2)}, u32[]{:S(2)}) collective-permute-start(f32[264,128]{1,0:T(8,128)S(1)} %invert.1), channel_id=1, source_target_pairs={{0,16},{4,20},{8,24},{12,28},{16,0},{20,4},{24,8},{28,12},{1,17},{... | collective-permute-start | bytes 405512 | tf_op jit(solution)/shard_map/ppermute | solution.py:307
  6.9 1.6 %collective-permute-start = (f32[4,32,256]{2,1,0:T(8,128)S(1)}, f32[4,32,256]{2,1,0:T(8,128)S(1)}, u32[]{:S(2)}, u32[]{:S(2)}) collective-permute-start(f32[4,32,256]{2,1,0:T(8,128)S(1)} %leave.1), channel_id=1, source_target_pairs={{0,4},{4,0},{8,12},{12,8},{16,20},{20,16},{24,28},{28,24},{1,5},{5... | collective-permute-start | bytes 393224 | tf_op jit(solution)/shard_map/ppermute | solution.py:311
  8.5 3.4 %collective-permute-done.came = f32[4,32,256]{2,1,0:T(8,128)S(1)} collective-permute-done((f32[4,32,256]{2,1,0:T(8,128)S(1)}, f32[4,32,256]{2,1,0:T(8,128)S(1)}, u32[]{:S(2)}, u32[]{:S(2)}) %collective-permute-start) | collective-permute-done | bytes 131104 | tf_op jit(solution)/shard_map/ppermute | solution.py:311
  13.1 3.0 %collective-permute-start.13 = (f32[2,264,128]{2,1,0:T(8,128)S(1)}, f32[2,264,128]{2,1,0:T(8,128)S(1)}, u32[]{:S(2)}, u32[]{:S(2)}) collective-permute-start(f32[2,264,128]{2,1,0:T(8,128)S(1)} %pad_maximum_fusion), channel_id=1, source_target_pairs={{0,2},{1,3},{2,0},{3,1},{4,6},{5,7},{6,4},{7,5},{8,10},{9,11},{10,... | collective-permute-start | bytes 811016 | tf_op jit(solution)/shard_map/ppermute | solution.py:315
  16.1 1.5 %collective-permute-start.4 = (f32[2,264,128]{2,1,0:T(8,128)S(1)}, f32[2,264,128]{2,1,0:T(8,128)S(1)}, u32[]{:S(2)}, u32[]{:S(2)}) collective-permute-start(f32[2,264,128]{2,1,0:T(8,128)S(1)} %pad_maximum_fusion), channel_id=1, source_target_pairs={{0,4},{4,0},{8,12},{12,8},{16,20},{20,16},{24,28},{28,24},{1,5},{5... | collective-permute-start | bytes 811016 | tf_op jit(solution)/shard_map/ppermute | solution.py:311
  18.1 1.3 %collective-permute-start.3 = (f32[256,128]{1,0:T(8,128)S(1)}, f32[256,128]{1,0:T(8,128)S(1)}, u32[]{:S(2)}, u32[]{:S(2)}) collective-permute-start(f32[256,128]{1,0:T(8,128)S(1)} %copy-done.3), channel_id=1, source_target_pairs={{0,16},{4,20},{8,24},{12,28},{16,0},{20,4},{24,8},{28,12},{1,17},{... | collective-permute-start | bytes 393224 | tf_op jit(solution)/shard_map/ppermute | solution.py:307
  19.4 7.2 %collective-permute-done.3 = f32[256,128]{1,0:T(8,128)S(1)} collective-permute-done((f32[256,128]{1,0:T(8,128)S(1)}, f32[256,128]{1,0:T(8,128)S(1)}, u32[]{:S(2)}, u32[]{:S(2)}) %collective-permute-start.3) | collective-permute-done | bytes 131104 | tf_op jit(solution)/shard_map/ppermute | solution.py:307
  28.2 1.7 %collective-permute-start.5 = (f32[2,264,128]{2,1,0:T(8,128)S(1)}, f32[2,264,128]{2,1,0:T(8,128)S(1)}, u32[]{:S(2)}, u32[]{:S(2)}) collective-permute-start(f32[2,264,128]{2,1,0:T(8,128)S(1)} %collective-permute-done.4), channel_id=1, source_target_pairs={{0,2},{1,3},{2,0},{3,1},{4,6},{5,7},{6,4},{7,5},{8,10},{9,11},{10,... | collective-permute-start | bytes 811016 | tf_op jit(solution)/shard_map/ppermute | solution.py:315
  29.9 9.9 %collective-permute-done.5 = f32[2,264,128]{2,1,0:T(8,128)S(1)} collective-permute-done((f32[2,264,128]{2,1,0:T(8,128)S(1)}, f32[2,264,128]{2,1,0:T(8,128)S(1)}, u32[]{:S(2)}, u32[]{:S(2)}) %collective-permute-start.5) | collective-permute-done | bytes 270368 | tf_op jit(solution)/shard_map/ppermute | solution.py:315
  39.8 2.3 %collective-permute-start.6 = (f32[2,32,256]{2,1,0:T(8,128)S(1)}, f32[2,32,256]{2,1,0:T(8,128)S(1)}, u32[]{:S(2)}, u32[]{:S(2)}) collective-permute-start(f32[2,32,256]{2,1,0:T(8,128)S(1)} %get-tuple-element.34), channel_id=1, source_target_pairs={{0,8},{4,12},{8,0},{12,4},{16,24},{20,28},{24,16},{28,20},{1,9},{5... | collective-permute-start | bytes 196616 | tf_op jit(solution)/shard_map/ppermute | solution.py:307
  42.1 1.7 %collective-permute-start.7 = (f32[2,32,256]{2,1,0:T(8,128)S(1)}, f32[2,32,256]{2,1,0:T(8,128)S(1)}, u32[]{:S(2)}, u32[]{:S(2)}) collective-permute-start(f32[2,32,256]{2,1,0:T(8,128)S(1)} %get-tuple-element.36), channel_id=1, source_target_pairs={{0,16},{4,20},{8,24},{12,28},{16,0},{20,4},{24,8},{28,12},{1,17},{... | collective-permute-start | bytes 196616 | tf_op jit(solution)/shard_map/ppermute | solution.py:307
  45.2 2.8 %collective-permute-done.7.b2 = f32[2,32,256]{2,1,0:T(8,128)S(1)} collective-permute-done((f32[2,32,256]{2,1,0:T(8,128)S(1)}, f32[2,32,256]{2,1,0:T(8,128)S(1)}, u32[]{:S(2)}, u32[]{:S(2)}) %collective-permute-start.7) | collective-permute-done | bytes 65568 | tf_op jit(solution)/shard_map/ppermute | solution.py:307
  47.9 1.9 %collective-permute-done.8.b3 = f32[2,32,256]{2,1,0:T(8,128)S(1)} collective-permute-done((f32[2,32,256]{2,1,0:T(8,128)S(1)}, f32[2,32,256]{2,1,0:T(8,128)S(1)}, u32[]{:S(2)}, u32[]{:S(2)}) %collective-permute-start.8) | collective-permute-done | bytes 65568 | tf_op jit(solution)/shard_map/ppermute | solution.py:307
  52.4 4.2 %collective-permute-done.9.left_x = f32[32,1024]{1,0:T(8,128)S(1)} collective-permute-done((f32[32,1024]{1,0:T(8,128)S(1)}, f32[32,1024]{1,0:T(8,128)S(1)}, u32[]{:S(2)}, u32[]{:S(2)}) %collective-permute-start.9) | collective-permute-done | bytes 131104 | tf_op jit(solution)/shard_map/ppermute | solution.py:315
  56.6 2.0 %collective-permute-done.10.later.refs_1_ = f32[2,256,128]{2,1,0:T(8,128)S(1)} collective-permute-done((f32[2,256,128]{2,1,0:T(8,128)S(1)}, f32[2,256,128]{2,1,0:T(8,128)S(1)}, u32[]{:S(2)}, u32[]{:S(2)}) %collective-permute-start.10) | collective-permute-done | bytes 262176 | tf_op jit(solution)/shard_map/ppermute | solution.py:307
  58.7 1.1 %collective-permute-done.12.refs_2_ = f32[2,256,128]{2,1,0:T(8,128)S(1)} collective-permute-done((f32[2,256,128]{2,1,0:T(8,128)S(1)}, f32[2,256,128]{2,1,0:T(8,128)S(1)}, u32[]{:S(2)}, u32[]{:S(2)}) %collective-permute-start.12) | collective-permute-done | bytes 262176 | tf_op jit(solution)/shard_map/ppermute | solution.py:311
  60.3 3.6 %first_panel.1.x_ref = f32[128,1024]{1,0:T(8,128)S(1)} custom-call(s32[2]{0:T(128)S(1)} %pad_add_fusion.place_ref, f32[2,32,1024]{2,1,0:T(8,128)S(1)} %pair.1, f32[2,32,1024]{2,1,0:T(8,128)S(1)} %collective-permute-done.11.other_pair, f32[8,264,128]{2,1,0:T(8,128)S(1)} %constant_dynamic-update-slice_fusion.refs_0_, ...), custom_call_target="tpu_custom_call" | custom-call | flops 200000000 | bytes 2097152 | tf_op jit(solution)/shard_map/first_panel/pallas_call | solution.py:405
  63.9 3.5 %collective-permute-done.20.refs_3_ = f32[2,256,128]{2,1,0:T(8,128)S(1)} collective-permute-done((f32[2,256,128]{2,1,0:T(8,128)S(1)}, f32[2,256,128]{2,1,0:T(8,128)S(1)}, u32[]{:S(2)}, u32[]{:S(2)}) %collective-permute-start.20) | collective-permute-done | bytes 262176 | tf_op jit(solution)/shard_map/ppermute | solution.py:311
  67.4 1.3 %update.1 = (f32[32,256]{1,0:T(8,128)S(1)}, f32[32,256]{1,0:T(8,128)S(1)}, f32[32,256]{1,0:T(8,128)S(1)}, f32[32,256]{1,0:T(8,128)S(1)}) custom-call(s32[2]{0:T(128)S(1)} %pad_add_fusion.place_ref, f32[128,1024]{1,0:T(8,128)S(1)} %first_panel.1.x_ref, f32[2,256,128]{2,1,0:T(8,128)S(1)} %pad_maximum_fusion.1.refs_0_, ...), custom_call_target="tpu_custom_call" | custom-call | flops 2000000000 | bytes 2097152 | tf_op jit(solution)/shard_map/update/pallas_call | solution.py:416
  69.6 1.4 %collective-permute-start.23 = (f32[32,256]{1,0:T(8,128)S(1)}, f32[32,256]{1,0:T(8,128)S(1)}, u32[]{:S(2)}, u32[]{:S(2)}) collective-permute-start(f32[32,256]{1,0:T(8,128)S(1)} %get-tuple-element.54), channel_id=1, source_target_pairs={{0,3},{1,2},{2,1},{3,0},{4,7},{5,6},{6,5},{7,4},{8,11},{9,10},{10,... | collective-permute-start | bytes 98312 | tf_op jit(solution)/shard_map/ppermute | solution.py:315
  70.9 2.9 %second_factor.1 = (bf16[1024,1024]{1,0:T(8,128)(2,1)S(1)}, bf16[1024,1024]{1,0:T(8,128)(2,1)S(1)}) custom-call(s32[2]{0:T(128)S(1)} %pad_add_fusion.place_ref, f32[8,264,128]{2,1,0:T(8,128)S(1)} %constant_dynamic-update-slice_fusion.refs_0_, f32[6,264,128]{2,1,0:T(8,128)S(1)} %constant_dynamic-update-slice_fusion.5.refs_1_, ...), custom_call_target="tpu_custom_call" | custom-call | flops 3000000000 | bytes 2097152 | tf_op jit(solution)/shard_map/second_factor/pallas_call | solution.py:428
  73.9 2.1 %second_panel.1 = f32[32,2048]{1,0:T(8,128)} custom-call(s32[2]{0:T(128)S(1)} %pad_add_fusion.place_ref, f32[128,1024]{1,0:T(8,128)S(1)} %first_panel.1.x_ref, f32[2,32,1024]{2,1,0:T(8,128)S(1)} %get-tuple-element.47.both_ref, bf16[1024,1024]{1,0:T(8,128)(2,1)S(1)} %get-tuple-element.50.uh_ref, bf16[1024,1024]{1,0:T(8,128)(2,1)S(1)} %get-tuple-element.51.ul_ref, ...), custom_call_target="tpu_custom_call" | custom-call | flops 2500000000 | bytes 2097152 | tf_op jit(solution)/shard_map/second_panel/pallas_call | solution.py:432
  (52 shorter events, 10.0 us)
Async XLA Ops:
  4.2 8.9 %collective-permute-start.1 = (f32[264,128]{1,0:T(8,128)S(1)}, f32[264,128]{1,0:T(8,128)S(1)}, u32[]{:S(2)}, u32[]{:S(2)}) collective-permute-start(f32[264,128]{1,0:T(8,128)S(1)} %invert.1), channel_id=1, source_target_pairs={{0,16},{4,20},{8,24},{12,28},{16,0},{20,4},{24,8},{28,12},{1,17},{... | collective-permute-start | bytes 405512 | tf_op jit(solution)/shard_map/ppermute | solution.py:307
  6.9 5.0 %collective-permute-start = (f32[4,32,256]{2,1,0:T(8,128)S(1)}, f32[4,32,256]{2,1,0:T(8,128)S(1)}, u32[]{:S(2)}, u32[]{:S(2)}) collective-permute-start(f32[4,32,256]{2,1,0:T(8,128)S(1)} %leave.1), channel_id=1, source_target_pairs={{0,4},{4,0},{8,12},{12,8},{16,20},{20,16},{24,28},{28,24},{1,5},{5... | collective-permute-start | bytes 393224 | tf_op jit(solution)/shard_map/ppermute | solution.py:311
  13.1 13.5 %collective-permute-start.13 = (f32[2,264,128]{2,1,0:T(8,128)S(1)}, f32[2,264,128]{2,1,0:T(8,128)S(1)}, u32[]{:S(2)}, u32[]{:S(2)}) collective-permute-start(f32[2,264,128]{2,1,0:T(8,128)S(1)} %pad_maximum_fusion), channel_id=1, source_target_pairs={{0,2},{1,3},{2,0},{3,1},{4,6},{5,7},{6,4},{7,5},{8,10},{9,11},{10,... | collective-permute-start | bytes 811016 | tf_op jit(solution)/shard_map/ppermute | solution.py:315
  16.1 10.5 %collective-permute-start.4 = (f32[2,264,128]{2,1,0:T(8,128)S(1)}, f32[2,264,128]{2,1,0:T(8,128)S(1)}, u32[]{:S(2)}, u32[]{:S(2)}) collective-permute-start(f32[2,264,128]{2,1,0:T(8,128)S(1)} %pad_maximum_fusion), channel_id=1, source_target_pairs={{0,4},{4,0},{8,12},{12,8},{16,20},{20,16},{24,28},{28,24},{1,5},{5... | collective-permute-start | bytes 811016 | tf_op jit(solution)/shard_map/ppermute | solution.py:311
  17.6 9.7 %collective-permute-start.2 = (f32[2,264,128]{2,1,0:T(8,128)S(1)}, f32[2,264,128]{2,1,0:T(8,128)S(1)}, u32[]{:S(2)}, u32[]{:S(2)}) collective-permute-start(f32[2,264,128]{2,1,0:T(8,128)S(1)} %pad_maximum_fusion), channel_id=1, source_target_pairs={{0,8},{4,12},{8,0},{12,4},{16,24},{20,28},{24,16},{28,20},{1,9},{5... | collective-permute-start | bytes 811016 | tf_op jit(solution)/shard_map/ppermute | solution.py:307
  18.1 8.5 %collective-permute-start.3 = (f32[256,128]{1,0:T(8,128)S(1)}, f32[256,128]{1,0:T(8,128)S(1)}, u32[]{:S(2)}, u32[]{:S(2)}) collective-permute-start(f32[256,128]{1,0:T(8,128)S(1)} %copy-done.3), channel_id=1, source_target_pairs={{0,16},{4,20},{8,24},{12,28},{16,0},{20,4},{24,8},{28,12},{1,17},{... | collective-permute-start | bytes 393224 | tf_op jit(solution)/shard_map/ppermute | solution.py:307
  27.3 17.3 %collective-permute-start.15 = (f32[2,264,128]{2,1,0:T(8,128)S(1)}, f32[2,264,128]{2,1,0:T(8,128)S(1)}, u32[]{:S(2)}, u32[]{:S(2)}) collective-permute-start(f32[2,264,128]{2,1,0:T(8,128)S(1)} %collective-permute-done.2), channel_id=1, source_target_pairs={{0,4},{4,0},{8,12},{12,8},{16,20},{20,16},{24,28},{28,24},{1,3},{5... | collective-permute-start | bytes 811016 | tf_op jit(solution)/shard_map/ppermute | solution.py:324
  27.8 16.8 %collective-permute-start.14 = (f32[2,264,128]{2,1,0:T(8,128)S(1)}, f32[2,264,128]{2,1,0:T(8,128)S(1)}, u32[]{:S(2)}, u32[]{:S(2)}) collective-permute-start(f32[2,264,128]{2,1,0:T(8,128)S(1)} %collective-permute-done.2), channel_id=1, source_target_pairs={{0,2},{4,6},{8,10},{12,14},{16,18},{20,22},{24,26},{28,30},{1,5},{... | collective-permute-start | bytes 811016 | tf_op jit(solution)/shard_map/ppermute | solution.py:324
  28.2 11.6 %collective-permute-start.5 = (f32[2,264,128]{2,1,0:T(8,128)S(1)}, f32[2,264,128]{2,1,0:T(8,128)S(1)}, u32[]{:S(2)}, u32[]{:S(2)}) collective-permute-start(f32[2,264,128]{2,1,0:T(8,128)S(1)} %collective-permute-done.4), channel_id=1, source_target_pairs={{0,2},{1,3},{2,0},{3,1},{4,6},{5,7},{6,4},{7,5},{8,10},{9,11},{10,... | collective-permute-start | bytes 811016 | tf_op jit(solution)/shard_map/ppermute | solution.py:315
  39.8 5.4 %collective-permute-start.6 = (f32[2,32,256]{2,1,0:T(8,128)S(1)}, f32[2,32,256]{2,1,0:T(8,128)S(1)}, u32[]{:S(2)}, u32[]{:S(2)}) collective-permute-start(f32[2,32,256]{2,1,0:T(8,128)S(1)} %get-tuple-element.34), channel_id=1, source_target_pairs={{0,8},{4,12},{8,0},{12,4},{16,24},{20,28},{24,16},{28,20},{1,9},{5... | collective-permute-start | bytes 196616 | tf_op jit(solution)/shard_map/ppermute | solution.py:307
  42.1 5.9 %collective-permute-start.7 = (f32[2,32,256]{2,1,0:T(8,128)S(1)}, f32[2,32,256]{2,1,0:T(8,128)S(1)}, u32[]{:S(2)}, u32[]{:S(2)}) collective-permute-start(f32[2,32,256]{2,1,0:T(8,128)S(1)} %get-tuple-element.36), channel_id=1, source_target_pairs={{0,16},{4,20},{8,24},{12,28},{16,0},{20,4},{24,8},{28,12},{1,17},{... | collective-permute-start | bytes 196616 | tf_op jit(solution)/shard_map/ppermute | solution.py:307
  43.8 6.1 %collective-permute-start.8 = (f32[2,32,256]{2,1,0:T(8,128)S(1)}, f32[2,32,256]{2,1,0:T(8,128)S(1)}, u32[]{:S(2)}, u32[]{:S(2)}) collective-permute-start(f32[2,32,256]{2,1,0:T(8,128)S(1)} %get-tuple-element.38), channel_id=1, source_target_pairs={{0,24},{4,28},{8,16},{12,20},{16,8},{20,12},{24,0},{28,4},{1,25},{... | collective-permute-start | bytes 196616 | tf_op jit(solution)/shard_map/ppermute | solution.py:307
  44.6 7.2 %collective-permute-start.16 = (f32[2,264,128]{2,1,0:T(8,128)S(1)}, f32[2,264,128]{2,1,0:T(8,128)S(1)}, u32[]{:S(2)}, u32[]{:S(2)}) collective-permute-start(f32[2,264,128]{2,1,0:T(8,128)S(1)} %collective-permute-done.14), channel_id=1, source_target_pairs={{0,4},{4,0},{8,12},{12,8},{16,20},{20,16},{24,28},{28,24},{1,3},{5... | collective-permute-start | bytes 811016 | tf_op jit(solution)/shard_map/ppermute | solution.py:324
  49.8 10.5 %collective-permute-start.17 = (f32[8,264,128]{2,1,0:T(8,128)S(1)}, f32[8,264,128]{2,1,0:T(8,128)S(1)}, u32[]{:S(2)}, u32[]{:S(2)}) collective-permute-start(f32[8,264,128]{2,1,0:T(8,128)S(1)} %constant_dynamic-update-slice_fusion.refs_0_), channel_id=1, source_target_pairs={{0,1},{1,0},{2,3},{3,2},{4,5},{5,4},{6,7},{7,6},{8,9},{9,8},{10,11... | collective-permute-start | bytes 3244040 | tf_op jit(solution)/shard_map/ppermute | solution.py:315
  49.8 8.8 %collective-permute-start.10 = (f32[2,256,128]{2,1,0:T(8,128)S(1)}, f32[2,256,128]{2,1,0:T(8,128)S(1)}, u32[]{:S(2)}, u32[]{:S(2)}) collective-permute-start(f32[2,256,128]{2,1,0:T(8,128)S(1)} %pad_maximum_fusion.1.refs_0_), channel_id=1, source_target_pairs={{0,8},{4,12},{8,0},{12,4},{16,24},{20,28},{24,16},{28,20},{1,9},{5... | collective-permute-start | bytes 786440 | tf_op jit(solution)/shard_map/ppermute | solution.py:307
  50.0 10.4 %collective-permute-start.18 = (f32[6,264,128]{2,1,0:T(8,128)S(1)}, f32[6,264,128]{2,1,0:T(8,128)S(1)}, u32[]{:S(2)}, u32[]{:S(2)}) collective-permute-start(f32[6,264,128]{2,1,0:T(8,128)S(1)} %constant_dynamic-update-slice_fusion.5.refs_1_), channel_id=1, source_target_pairs={{0,1},{1,0},{2,3},{3,2},{4,5},{5,4},{6,7},{7,6},{8,9},{9,8},{10,11... | collective-permute-start | bytes 2433032 | tf_op jit(solution)/shard_map/ppermute | solution.py:315
  51.1 5.5 %collective-permute-start.9 = (f32[32,1024]{1,0:T(8,128)S(1)}, f32[32,1024]{1,0:T(8,128)S(1)}, u32[]{:S(2)}, u32[]{:S(2)}) collective-permute-start(f32[32,1024]{1,0:T(8,128)S(1)} %get-tuple-element.39.left), channel_id=1, source_target_pairs={{0,2},{1,3},{2,0},{3,1},{4,6},{5,7},{6,4},{7,5},{8,10},{9,11},{10,... | collective-permute-start | bytes 393224 | tf_op jit(solution)/shard_map/ppermute | solution.py:315
  51.9 7.9 %collective-permute-start.12 = (f32[2,256,128]{2,1,0:T(8,128)S(1)}, f32[2,256,128]{2,1,0:T(8,128)S(1)}, u32[]{:S(2)}, u32[]{:S(2)}) collective-permute-start(f32[2,256,128]{2,1,0:T(8,128)S(1)} %pad_maximum_fusion.1.refs_0_), channel_id=1, source_target_pairs={{0,4},{4,0},{8,12},{12,8},{16,20},{20,16},{24,28},{28,24},{1,5},{5... | collective-permute-start | bytes 786440 | tf_op jit(solution)/shard_map/ppermute | solution.py:311
  56.6 3.7 %collective-permute-start.19 = (f32[2,264,128]{2,1,0:T(8,128)S(1)}, f32[2,264,128]{2,1,0:T(8,128)S(1)}, u32[]{:S(2)}, u32[]{:S(2)}) collective-permute-start(f32[2,264,128]{2,1,0:T(8,128)S(1)} %collective-permute-done.16.refs_2_), channel_id=1, source_target_pairs={{0,1},{1,0},{2,3},{3,2},{4,5},{5,4},{6,7},{7,6},{8,9},{9,8},{10,11... | collective-permute-start | bytes 811016 | tf_op jit(solution)/shard_map/ppermute | solution.py:315
  58.6 1.7 %collective-permute-start.11 = (f32[2,32,1024]{2,1,0:T(8,128)S(1)}, f32[2,32,1024]{2,1,0:T(8,128)S(1)}, u32[]{:S(2)}, u32[]{:S(2)}) collective-permute-start(f32[2,32,1024]{2,1,0:T(8,128)S(1)} %pair.1), channel_id=1, source_target_pairs={{0,1},{1,0},{2,3},{3,2},{4,5},{5,4},{6,7},{7,6},{8,9},{9,8},{10,11... | collective-permute-start | bytes 786440 | tf_op jit(solution)/shard_map/ppermute | solution.py:315
  59.8 7.6 %collective-permute-start.20 = (f32[2,256,128]{2,1,0:T(8,128)S(1)}, f32[2,256,128]{2,1,0:T(8,128)S(1)}, u32[]{:S(2)}, u32[]{:S(2)}) collective-permute-start(f32[2,256,128]{2,1,0:T(8,128)S(1)} %collective-permute-done.10.later.refs_1_), channel_id=1, source_target_pairs={{0,4},{4,0},{8,12},{12,8},{16,20},{20,16},{24,28},{28,24},{1,5},{5... | collective-permute-start | bytes 786440 | tf_op jit(solution)/shard_map/ppermute | solution.py:311
  68.7 5.1 %collective-permute-start.21 = (f32[32,256]{1,0:T(8,128)S(1)}, f32[32,256]{1,0:T(8,128)S(1)}, u32[]{:S(2)}, u32[]{:S(2)}) collective-permute-start(f32[32,256]{1,0:T(8,128)S(1)} %get-tuple-element.52), channel_id=1, source_target_pairs={{0,2},{1,3},{2,0},{3,1},{4,6},{5,7},{6,4},{7,5},{8,10},{9,11},{10,... | collective-permute-start | bytes 98312 | tf_op jit(solution)/shard_map/ppermute | solution.py:315
  69.6 4.3 %collective-permute-start.22 = (f32[32,256]{1,0:T(8,128)S(1)}, f32[32,256]{1,0:T(8,128)S(1)}, u32[]{:S(2)}, u32[]{:S(2)}) collective-permute-start(f32[32,256]{1,0:T(8,128)S(1)} %get-tuple-element.53), channel_id=1, source_target_pairs={{0,1},{1,0},{2,3},{3,2},{4,5},{5,4},{6,7},{7,6},{8,9},{9,8},{10,11... | collective-permute-start | bytes 98312 | tf_op jit(solution)/shard_map/ppermute | solution.py:315
  69.6 4.3 %collective-permute-start.23 = (f32[32,256]{1,0:T(8,128)S(1)}, f32[32,256]{1,0:T(8,128)S(1)}, u32[]{:S(2)}, u32[]{:S(2)}) collective-permute-start(f32[32,256]{1,0:T(8,128)S(1)} %get-tuple-element.54), channel_id=1, source_target_pairs={{0,3},{1,2},{2,1},{3,0},{4,7},{5,6},{6,5},{7,4},{8,11},{9,10},{10,... | collective-permute-start | bytes 98312 | tf_op jit(solution)/shard_map/ppermute | solution.py:315
  (4 other events, 15.8 us)

commit v4 on v2

--- a/solution.py
+++ b/solution.py
@@ -369,7 +369,7 @@
         place, blocks, came
     )
     b_z = [swap_z(after(b, far), m + 1) for m, b in enumerate(b_out)]
-    c_far = swap_z(after(c_near, far, b_z[0]), 1)
+    c_far = swap_z(after(c_near, far0), 1)
     c_far_got = swap_y(c_far)
     far01 = cross(after(far0, far1, near01), 1)
 
@@ -386,7 +386,7 @@
     pair = jnp.stack([left, swap_rep(after(left, came), 2)])
     other_pair = swap_rep(after(pair, c_far), 1)
     bufs = [near, near0, near1, near01, far, far0, far1, far01]
-    bufs += [swap_rep(b, 1) for b in bufs[:7]] + [swap_rep(after(far01, far1), 1)]
+    bufs += [swap_rep(after(b, b_z[2], far0), 1) for b in bufs[:7]] + [swap_rep(after(far01, far1), 1)]
 
     scratch = [pltpu.VMEM((8, 136, 128), F32)]
     halves = [shape(1024, 1024, dtype=BF16)] * 2

time: 66.6 us -> 63.7 us (0.956)
  waiting for transfers between devices: 23.6 us -> 18.3 us
  starting transfers between devices: 26.9 us -> 29.3 us
    ppermute x7, waiting for transfers between devices: 14.7 us -> 10.7 us  [swap_z(): return lax.ppermute(x, 'bulk', [(k, k ^ 2 * m) for k in range(8)])]
    ppermute x4, waiting for transfers between devices: 5.03 us -> 3.2 us  [swap_y(): return lax.ppermute(x, 'bulk', [(k, k ^ 1) for k in range(8)])]
    ppermute x15, starting transfers between devices: 6.6 us -> 8.21 us  [swap_rep(): return lax.ppermute(x, 'rep', [(k, k ^ bits) for k in range(4)])]
    ppermute x7, starting transfers between devices: 12.8 us -> 13.9 us  [swap_z(): return lax.ppermute(x, 'bulk', [(k, k ^ 2 * m) for k in range(8)])]
  transfers between devices with their start and end apart: 29 -> 29, of which waited for: 10 -> 9; matrix products, arithmetic and copies ran while one was open for 0% -> 0% of each run, Pallas kernels for 12% -> 13%
where the time goes in v4:
time: 63.7 us; the launch traced here: 63.5 us
  starting transfers between devices  29.3 us (46%)
  waiting for transfers between devices  18.3 us (29%)
  Pallas kernels  14 us (22%)
  local copies, waits for them, and re-layouts  1.59 us (2%)
    ppermute x7, starting transfers between devices, swap_z(): return lax.ppermute(x, 'bulk', [(k, k ^ 2 * m) for k in range(8)])  13.9 us
    ppermute x7, waiting for transfers between devices, swap_z(): return lax.ppermute(x, 'bulk', [(k, k ^ 2 * m) for k in range(8)])  10.7 us
    ppermute x15, starting transfers between devices, swap_rep(): return lax.ppermute(x, 'rep', [(k, k ^ bits) for k in range(4)])  8.21 us
    ppermute x4, starting transfers between devices, swap_y(): return lax.ppermute(x, 'bulk', [(k, k ^ 1) for k in range(8)])  5.72 us
    ppermute x15, waiting for transfers between devices, swap_rep(): return lax.ppermute(x, 'rep', [(k, k ^ bits) for k in range(4)])  3.97 us
    pallas_call x1, Pallas kernels, per_device(): call(first_kernel, shape(128, 1024), [SMEM] + [VMEM] * 18, VMEM, [pltpu.V...  3.59 us
    ppermute x4, waiting for transfers between devices, swap_y(): return lax.ppermute(x, 'bulk', [(k, k ^ 1) for k in range(8)])  3.2 us
    pallas_call x1, Pallas kernels, per_device(): call(second_factor_kernel, halves, [SMEM] + [VMEM] * 16, [VMEM] * 2, scra...  2.87 us
  transfers between devices with their start and end apart: 29, of which 9 were waited for; matrix products, arithmetic and copies ran while one was open for 0% of the time, Pallas kernels for 13%

profile of v4, /device:TPU:0, one launch (start us, length us, event | category | flops | bytes accessed | tf_op | source)
XLA Modules:
  0.0 63.5 jit_solution(10413247815677953882)
XLA Ops:
  0.1 0.9 %copy-done.1 = f32[256,128]{1,0:T(8,128)S(1)} copy-done((f32[256,128]{1,0:T(8,128)S(1)}, f32[256,128]{1,0:T(8,128)}, u32[]{:S(2)}) %copy-start.1) | copy-done | bytes 131096
  1.7 2.6 %invert.1 = f32[264,128]{1,0:T(8,128)S(1)} custom-call(s32[2]{0:T(128)S(1)} %pad_add_fusion.place_ref, f32[256,128]{1,0:T(8,128)S(1)} %copy-done.1, f32[2,128]{1,0:T(2,128)S(1)} %copy-done.2), custom_call_target="tpu_custom_call" | custom-call | flops 3500000000 | bytes 2097152 | tf_op jit(solution)/shard_map/invert/pallas_call | solution.py:349
  4.2 2.1 %collective-permute-start.1 = (f32[264,128]{1,0:T(8,128)S(1)}, f32[264,128]{1,0:T(8,128)S(1)}, u32[]{:S(2)}, u32[]{:S(2)}) collective-permute-start(f32[264,128]{1,0:T(8,128)S(1)} %invert.1), channel_id=1, source_target_pairs={{0,16},{4,20},{8,24},{12,28},{16,0},{20,4},{24,8},{28,12},{1,17},{... | collective-permute-start | bytes 405512 | tf_op jit(solution)/shard_map/ppermute | solution.py:298
  6.3 6.8 %collective-permute-done.1 = f32[264,128]{1,0:T(8,128)S(1)} collective-permute-done((f32[264,128]{1,0:T(8,128)S(1)}, f32[264,128]{1,0:T(8,128)S(1)}, u32[]{:S(2)}, u32[]{:S(2)}) %collective-permute-start.1) | collective-permute-done | bytes 135200 | tf_op jit(solution)/shard_map/ppermute | solution.py:298
  13.1 2.0 %collective-permute-start.8 = (f32[2,264,128]{2,1,0:T(8,128)S(1)}, f32[2,264,128]{2,1,0:T(8,128)S(1)}, u32[]{:S(2)}, u32[]{:S(2)}) collective-permute-start(f32[2,264,128]{2,1,0:T(8,128)S(1)} %pad_maximum_fusion.refs_0_), channel_id=1, source_target_pairs={{0,4},{4,0},{8,12},{12,8},{16,20},{20,16},{24,28},{28,24},{1,5},{5... | collective-permute-start | bytes 811016 | tf_op jit(solution)/shard_map/ppermute | solution.py:302
  15.2 1.5 %collective-permute-start.9 = (f32[2,264,128]{2,1,0:T(8,128)S(1)}, f32[2,264,128]{2,1,0:T(8,128)S(1)}, u32[]{:S(2)}, u32[]{:S(2)}) collective-permute-start(f32[2,264,128]{2,1,0:T(8,128)S(1)} %pad_maximum_fusion.refs_0_), channel_id=1, source_target_pairs={{0,2},{1,3},{2,0},{3,1},{4,6},{5,7},{6,4},{7,5},{8,10},{9,11},{10,... | collective-permute-start | bytes 811016 | tf_op jit(solution)/shard_map/ppermute | solution.py:306
  16.7 2.7 %collective-permute-start.7 = (f32[256,128]{1,0:T(8,128)S(1)}, f32[256,128]{1,0:T(8,128)S(1)}, u32[]{:S(2)}, u32[]{:S(2)}) collective-permute-start(f32[256,128]{1,0:T(8,128)S(1)} %copy-done.3), channel_id=1, source_target_pairs={{0,16},{4,20},{8,24},{12,28},{16,0},{20,4},{24,8},{28,12},{1,17},{... | collective-permute-start | bytes 393224 | tf_op jit(solution)/shard_map/ppermute | solution.py:298
  20.5 1.2 %collective-permute-start.14 = (f32[2,264,128]{2,1,0:T(8,128)S(1)}, f32[2,264,128]{2,1,0:T(8,128)S(1)}, u32[]{:S(2)}, u32[]{:S(2)}) collective-permute-start(f32[2,264,128]{2,1,0:T(8,128)S(1)} %collective-permute-done.8.refs_1_), channel_id=1, source_target_pairs={{0,2},{1,3},{2,0},{3,1},{4,6},{5,7},{6,4},{7,5},{8,10},{9,11},{10,... | collective-permute-start | bytes 811016 | tf_op jit(solution)/shard_map/ppermute | solution.py:306
  21.7 3.2 %collective-permute-done.7 = f32[256,128]{1,0:T(8,128)S(1)} collective-permute-done((f32[256,128]{1,0:T(8,128)S(1)}, f32[256,128]{1,0:T(8,128)S(1)}, u32[]{:S(2)}, u32[]{:S(2)}) %collective-permute-start.7) | collective-permute-done | bytes 131104 | tf_op jit(solution)/shard_map/ppermute | solution.py:298
  27.2 3.5 %collective-permute-start.3 = (f32[2,32,256]{2,1,0:T(8,128)S(1)}, f32[2,32,256]{2,1,0:T(8,128)S(1)}, u32[]{:S(2)}, u32[]{:S(2)}) collective-permute-start(f32[2,32,256]{2,1,0:T(8,128)S(1)} %get-tuple-element.39), channel_id=1, source_target_pairs={{0,8},{4,12},{8,0},{12,4},{16,24},{20,28},{24,16},{28,20},{1,9},{5... | collective-permute-start | bytes 196616 | tf_op jit(solution)/shard_map/ppermute | solution.py:298
  30.7 1.6 %collective-permute-start.4 = (f32[2,32,256]{2,1,0:T(8,128)S(1)}, f32[2,32,256]{2,1,0:T(8,128)S(1)}, u32[]{:S(2)}, u32[]{:S(2)}) collective-permute-start(f32[2,32,256]{2,1,0:T(8,128)S(1)} %get-tuple-element.41), channel_id=1, source_target_pairs={{0,16},{4,20},{8,24},{12,28},{16,0},{20,4},{24,8},{28,12},{1,17},{... | collective-permute-start | bytes 196616 | tf_op jit(solution)/shard_map/ppermute | solution.py:298
  32.3 1.0 %collective-permute-start.5 = (f32[2,32,256]{2,1,0:T(8,128)S(1)}, f32[2,32,256]{2,1,0:T(8,128)S(1)}, u32[]{:S(2)}, u32[]{:S(2)}) collective-permute-start(f32[2,32,256]{2,1,0:T(8,128)S(1)} %get-tuple-element.43), channel_id=1, source_target_pairs={{0,24},{4,28},{8,16},{12,20},{16,8},{20,12},{24,0},{28,4},{1,25},{... | collective-permute-start | bytes 196616 | tf_op jit(solution)/shard_map/ppermute | solution.py:298
  33.8 1.5 %collective-permute-start.13 = (f32[2,256,128]{2,1,0:T(8,128)S(1)}, f32[2,256,128]{2,1,0:T(8,128)S(1)}, u32[]{:S(2)}, u32[]{:S(2)}) collective-permute-start(f32[2,256,128]{2,1,0:T(8,128)S(1)} %pad_maximum_fusion.2.refs_0_), channel_id=1, source_target_pairs={{0,4},{4,0},{8,12},{12,8},{16,20},{20,16},{24,28},{28,24},{1,5},{5... | collective-permute-start | bytes 786440 | tf_op jit(solution)/shard_map/ppermute | solution.py:302
  35.3 3.0 %collective-permute-start.11 = (f32[2,256,128]{2,1,0:T(8,128)S(1)}, f32[2,256,128]{2,1,0:T(8,128)S(1)}, u32[]{:S(2)}, u32[]{:S(2)}) collective-permute-start(f32[2,256,128]{2,1,0:T(8,128)S(1)} %pad_maximum_fusion.2.refs_0_), channel_id=1, source_target_pairs={{0,8},{4,12},{8,0},{12,4},{16,24},{20,28},{24,16},{28,20},{1,9},{5... | collective-permute-start | bytes 786440 | tf_op jit(solution)/shard_map/ppermute | solution.py:298
  39.3 1.4 %collective-permute-start.6 = (f32[32,1024]{1,0:T(8,128)S(1)}, f32[32,1024]{1,0:T(8,128)S(1)}, u32[]{:S(2)}, u32[]{:S(2)}) collective-permute-start(f32[32,1024]{1,0:T(8,128)S(1)} %get-tuple-element.45), channel_id=1, source_target_pairs={{0,2},{1,3},{2,0},{3,1},{4,6},{5,7},{6,4},{7,5},{8,10},{9,11},{10,... | collective-permute-start | bytes 393224 | tf_op jit(solution)/shard_map/ppermute | solution.py:306
  41.3 3.1 %collective-permute-done.6 = f32[32,1024]{1,0:T(8,128)S(1)} collective-permute-done((f32[32,1024]{1,0:T(8,128)S(1)}, f32[32,1024]{1,0:T(8,128)S(1)}, u32[]{:S(2)}, u32[]{:S(2)}) %collective-permute-start.6) | collective-permute-done | bytes 131104 | tf_op jit(solution)/shard_map/ppermute | solution.py:306
  46.7 1.6 %collective-permute-start.25 = (f32[2,256,128]{2,1,0:T(8,128)S(1)}, f32[2,256,128]{2,1,0:T(8,128)S(1)}, u32[]{:S(2)}, u32[]{:S(2)}) collective-permute-start(f32[2,256,128]{2,1,0:T(8,128)S(1)} %collective-permute-done.11.refs_1_), channel_id=1, source_target_pairs={{0,4},{4,0},{8,12},{12,8},{16,20},{20,16},{24,28},{28,24},{1,5},{5... | collective-permute-start | bytes 786440 | tf_op jit(solution)/shard_map/ppermute | solution.py:302
  48.3 3.6 %first_panel.1.x_ref = f32[128,1024]{1,0:T(8,128)S(1)} custom-call(s32[2]{0:T(128)S(1)} %pad_add_fusion.place_ref, f32[2,32,1024]{2,1,0:T(8,128)S(1)} %pad_maximum_fusion.1.pair, f32[2,32,1024]{2,1,0:T(8,128)S(1)} %collective-permute-done.12.other_pair, f32[2,264,128]{2,1,0:T(8,128)S(1)} %pad_maximum_fusion.refs_0_, ...), custom_call_target="tpu_custom_call" | custom-call | flops 200000000 | bytes 2097152 | tf_op jit(solution)/shard_map/first_panel/pallas_call | solution.py:393
  51.9 3.1 %collective-permute-done.25.refs_3_ = f32[2,256,128]{2,1,0:T(8,128)S(1)} collective-permute-done((f32[2,256,128]{2,1,0:T(8,128)S(1)}, f32[2,256,128]{2,1,0:T(8,128)S(1)}, u32[]{:S(2)}, u32[]{:S(2)}) %collective-permute-start.25) | collective-permute-done | bytes 262176 | tf_op jit(solution)/shard_map/ppermute | solution.py:302
  55.0 1.3 %update.1 = (f32[32,256]{1,0:T(8,128)S(1)}, f32[32,256]{1,0:T(8,128)S(1)}, f32[32,256]{1,0:T(8,128)S(1)}, f32[32,256]{1,0:T(8,128)S(1)}) custom-call(s32[2]{0:T(128)S(1)} %pad_add_fusion.place_ref, f32[128,1024]{1,0:T(8,128)S(1)} %first_panel.1.x_ref, f32[2,256,128]{2,1,0:T(8,128)S(1)} %pad_maximum_fusion.2.refs_0_, ...), custom_call_target="tpu_custom_call" | custom-call | flops 2000000000 | bytes 2097152 | tf_op jit(solution)/shard_map/update/pallas_call | solution.py:404
  56.3 1.4 %collective-permute-start.26 = (f32[32,256]{1,0:T(8,128)S(1)}, f32[32,256]{1,0:T(8,128)S(1)}, u32[]{:S(2)}, u32[]{:S(2)}) collective-permute-start(f32[32,256]{1,0:T(8,128)S(1)} %get-tuple-element.66), channel_id=1, source_target_pairs={{0,2},{1,3},{2,0},{3,1},{4,6},{5,7},{6,4},{7,5},{8,10},{9,11},{10,... | collective-permute-start | bytes 98312 | tf_op jit(solution)/shard_map/ppermute | solution.py:306
  57.7 0.8 %collective-permute-start.28 = (f32[32,256]{1,0:T(8,128)S(1)}, f32[32,256]{1,0:T(8,128)S(1)}, u32[]{:S(2)}, u32[]{:S(2)}) collective-permute-start(f32[32,256]{1,0:T(8,128)S(1)} %get-tuple-element.68), channel_id=1, source_target_pairs={{0,3},{1,2},{2,1},{3,0},{4,7},{5,6},{6,5},{7,4},{8,11},{9,10},{10,... | collective-permute-start | bytes 98312 | tf_op jit(solution)/shard_map/ppermute | solution.py:306
  58.5 2.9 %second_factor.1 = (bf16[1024,1024]{1,0:T(8,128)(2,1)S(1)}, bf16[1024,1024]{1,0:T(8,128)(2,1)S(1)}) custom-call(s32[2]{0:T(128)S(1)} %pad_add_fusion.place_ref, f32[2,264,128]{2,1,0:T(8,128)S(1)} %pad_maximum_fusion.refs_0_, f32[2,264,128]{2,1,0:T(8,128)S(1)} %collective-permute-done.8.refs_1_, f32[2,264,128]{2,1,0:T(8,128)S(1)} %collective-permute-done.9.refs_2_, ...), custom_call_target="tpu_custom_call" | custom-call | flops 3000000000 | bytes 2097152 | tf_op jit(solution)/shard_map/second_factor/pallas_call | solution.py:416
  61.4 2.1 %second_panel.1 = f32[32,2048]{1,0:T(8,128)} custom-call(s32[2]{0:T(128)S(1)} %pad_add_fusion.place_ref, f32[128,1024]{1,0:T(8,128)S(1)} %first_panel.1.x_ref, f32[2,32,1024]{2,1,0:T(8,128)S(1)} %get-tuple-element.61.both_ref, bf16[1024,1024]{1,0:T(8,128)(2,1)S(1)} %get-tuple-element.64.uh_ref, bf16[1024,1024]{1,0:T(8,128)(2,1)S(1)} %get-tuple-element.65.ul_ref, ...), custom_call_target="tpu_custom_call" | custom-call | flops 2500000000 | bytes 2097152 | tf_op jit(solution)/shard_map/second_panel/pallas_call | solution.py:420
  (54 shorter events, 8.6 us)
Async XLA Ops:
  4.2 8.9 %collective-permute-start.1 = (f32[264,128]{1,0:T(8,128)S(1)}, f32[264,128]{1,0:T(8,128)S(1)}, u32[]{:S(2)}, u32[]{:S(2)}) collective-permute-start(f32[264,128]{1,0:T(8,128)S(1)} %invert.1), channel_id=1, source_target_pairs={{0,16},{4,20},{8,24},{12,28},{16,0},{20,4},{24,8},{28,12},{1,17},{... | collective-permute-start | bytes 405512 | tf_op jit(solution)/shard_map/ppermute | solution.py:298
  13.1 7.4 %collective-permute-start.8 = (f32[2,264,128]{2,1,0:T(8,128)S(1)}, f32[2,264,128]{2,1,0:T(8,128)S(1)}, u32[]{:S(2)}, u32[]{:S(2)}) collective-permute-start(f32[2,264,128]{2,1,0:T(8,128)S(1)} %pad_maximum_fusion.refs_0_), channel_id=1, source_target_pairs={{0,4},{4,0},{8,12},{12,8},{16,20},{20,16},{24,28},{28,24},{1,5},{5... | collective-permute-start | bytes 811016 | tf_op jit(solution)/shard_map/ppermute | solution.py:302
  15.2 9.8 %collective-permute-start.9 = (f32[2,264,128]{2,1,0:T(8,128)S(1)}, f32[2,264,128]{2,1,0:T(8,128)S(1)}, u32[]{:S(2)}, u32[]{:S(2)}) collective-permute-start(f32[2,264,128]{2,1,0:T(8,128)S(1)} %pad_maximum_fusion.refs_0_), channel_id=1, source_target_pairs={{0,2},{1,3},{2,0},{3,1},{4,6},{5,7},{6,4},{7,5},{8,10},{9,11},{10,... | collective-permute-start | bytes 811016 | tf_op jit(solution)/shard_map/ppermute | solution.py:306
  16.7 9.0 %collective-permute-start.2 = (f32[2,264,128]{2,1,0:T(8,128)S(1)}, f32[2,264,128]{2,1,0:T(8,128)S(1)}, u32[]{:S(2)}, u32[]{:S(2)}) collective-permute-start(f32[2,264,128]{2,1,0:T(8,128)S(1)} %pad_maximum_fusion.refs_0_), channel_id=1, source_target_pairs={{0,8},{4,12},{8,0},{12,4},{16,24},{20,28},{24,16},{28,20},{1,9},{5... | collective-permute-start | bytes 811016 | tf_op jit(solution)/shard_map/ppermute | solution.py:298
  16.7 8.2 %collective-permute-start.7 = (f32[256,128]{1,0:T(8,128)S(1)}, f32[256,128]{1,0:T(8,128)S(1)}, u32[]{:S(2)}, u32[]{:S(2)}) collective-permute-start(f32[256,128]{1,0:T(8,128)S(1)} %copy-done.3), channel_id=1, source_target_pairs={{0,16},{4,20},{8,24},{12,28},{16,0},{20,4},{24,8},{28,12},{1,17},{... | collective-permute-start | bytes 393224 | tf_op jit(solution)/shard_map/ppermute | solution.py:298
  19.9 5.0 %collective-permute-start = (f32[4,32,256]{2,1,0:T(8,128)S(1)}, f32[4,32,256]{2,1,0:T(8,128)S(1)}, u32[]{:S(2)}, u32[]{:S(2)}) collective-permute-start(f32[4,32,256]{2,1,0:T(8,128)S(1)} %leave.1), channel_id=1, source_target_pairs={{0,4},{4,0},{8,12},{12,8},{16,20},{20,16},{24,28},{28,24},{1,5},{5... | collective-permute-start | bytes 393224 | tf_op jit(solution)/shard_map/ppermute | solution.py:302
  20.5 11.8 %collective-permute-start.14 = (f32[2,264,128]{2,1,0:T(8,128)S(1)}, f32[2,264,128]{2,1,0:T(8,128)S(1)}, u32[]{:S(2)}, u32[]{:S(2)}) collective-permute-start(f32[2,264,128]{2,1,0:T(8,128)S(1)} %collective-permute-done.8.refs_1_), channel_id=1, source_target_pairs={{0,2},{1,3},{2,0},{3,1},{4,6},{5,7},{6,4},{7,5},{8,10},{9,11},{10,... | collective-permute-start | bytes 811016 | tf_op jit(solution)/shard_map/ppermute | solution.py:306
  25.6 8.1 %collective-permute-start.10 = (f32[2,264,128]{2,1,0:T(8,128)S(1)}, f32[2,264,128]{2,1,0:T(8,128)S(1)}, u32[]{:S(2)}, u32[]{:S(2)}) collective-permute-start(f32[2,264,128]{2,1,0:T(8,128)S(1)} %collective-permute-done.2.refs_4_), channel_id=1, source_target_pairs={{0,2},{4,6},{8,10},{12,14},{16,18},{20,22},{24,26},{28,30},{1,5},{... | collective-permute-start | bytes 811016 | tf_op jit(solution)/shard_map/ppermute | solution.py:315
  26.3 9.0 %collective-permute-start.15 = (f32[2,264,128]{2,1,0:T(8,128)S(1)}, f32[2,264,128]{2,1,0:T(8,128)S(1)}, u32[]{:S(2)}, u32[]{:S(2)}) collective-permute-start(f32[2,264,128]{2,1,0:T(8,128)S(1)} %collective-permute-done.2.refs_4_), channel_id=1, source_target_pairs={{0,4},{4,0},{8,12},{12,8},{16,20},{20,16},{24,28},{28,24},{1,3},{5... | collective-permute-start | bytes 811016 | tf_op jit(solution)/shard_map/ppermute | solution.py:315
  27.2 11.0 %collective-permute-start.3 = (f32[2,32,256]{2,1,0:T(8,128)S(1)}, f32[2,32,256]{2,1,0:T(8,128)S(1)}, u32[]{:S(2)}, u32[]{:S(2)}) collective-permute-start(f32[2,32,256]{2,1,0:T(8,128)S(1)} %get-tuple-element.39), channel_id=1, source_target_pairs={{0,8},{4,12},{8,0},{12,4},{16,24},{20,28},{24,16},{28,20},{1,9},{5... | collective-permute-start | bytes 196616 | tf_op jit(solution)/shard_map/ppermute | solution.py:298
  30.7 8.0 %collective-permute-start.4 = (f32[2,32,256]{2,1,0:T(8,128)S(1)}, f32[2,32,256]{2,1,0:T(8,128)S(1)}, u32[]{:S(2)}, u32[]{:S(2)}) collective-permute-start(f32[2,32,256]{2,1,0:T(8,128)S(1)} %get-tuple-element.41), channel_id=1, source_target_pairs={{0,16},{4,20},{8,24},{12,28},{16,0},{20,4},{24,8},{28,12},{1,17},{... | collective-permute-start | bytes 196616 | tf_op jit(solution)/shard_map/ppermute | solution.py:298
  32.3 6.4 %collective-permute-start.5 = (f32[2,32,256]{2,1,0:T(8,128)S(1)}, f32[2,32,256]{2,1,0:T(8,128)S(1)}, u32[]{:S(2)}, u32[]{:S(2)}) collective-permute-start(f32[2,32,256]{2,1,0:T(8,128)S(1)} %get-tuple-element.43), channel_id=1, source_target_pairs={{0,24},{4,28},{8,16},{12,20},{16,8},{20,12},{24,0},{28,4},{1,25},{... | collective-permute-start | bytes 196616 | tf_op jit(solution)/shard_map/ppermute | solution.py:298
  33.8 7.0 %collective-permute-start.13 = (f32[2,256,128]{2,1,0:T(8,128)S(1)}, f32[2,256,128]{2,1,0:T(8,128)S(1)}, u32[]{:S(2)}, u32[]{:S(2)}) collective-permute-start(f32[2,256,128]{2,1,0:T(8,128)S(1)} %pad_maximum_fusion.2.refs_0_), channel_id=1, source_target_pairs={{0,4},{4,0},{8,12},{12,8},{16,20},{20,16},{24,28},{28,24},{1,5},{5... | collective-permute-start | bytes 786440 | tf_op jit(solution)/shard_map/ppermute | solution.py:302
  35.3 9.1 %collective-permute-start.11 = (f32[2,256,128]{2,1,0:T(8,128)S(1)}, f32[2,256,128]{2,1,0:T(8,128)S(1)}, u32[]{:S(2)}, u32[]{:S(2)}) collective-permute-start(f32[2,256,128]{2,1,0:T(8,128)S(1)} %pad_maximum_fusion.2.refs_0_), channel_id=1, source_target_pairs={{0,8},{4,12},{8,0},{12,4},{16,24},{20,28},{24,16},{28,20},{1,9},{5... | collective-permute-start | bytes 786440 | tf_op jit(solution)/shard_map/ppermute | solution.py:298
  38.2 6.7 %collective-permute-start.16 = (f32[2,264,128]{2,1,0:T(8,128)S(1)}, f32[2,264,128]{2,1,0:T(8,128)S(1)}, u32[]{:S(2)}, u32[]{:S(2)}) collective-permute-start(f32[2,264,128]{2,1,0:T(8,128)S(1)} %collective-permute-done.10.refs_5_), channel_id=1, source_target_pairs={{0,4},{4,0},{8,12},{12,8},{16,20},{20,16},{24,28},{28,24},{1,3},{5... | collective-permute-start | bytes 811016 | tf_op jit(solution)/shard_map/ppermute | solution.py:315
  39.3 5.0 %collective-permute-start.6 = (f32[32,1024]{1,0:T(8,128)S(1)}, f32[32,1024]{1,0:T(8,128)S(1)}, u32[]{:S(2)}, u32[]{:S(2)}) collective-permute-start(f32[32,1024]{1,0:T(8,128)S(1)} %get-tuple-element.45), channel_id=1, source_target_pairs={{0,2},{1,3},{2,0},{3,1},{4,6},{5,7},{6,4},{7,5},{8,10},{9,11},{10,... | collective-permute-start | bytes 393224 | tf_op jit(solution)/shard_map/ppermute | solution.py:306
  40.7 4.3 %collective-permute-start.17 = (f32[2,264,128]{2,1,0:T(8,128)S(1)}, f32[2,264,128]{2,1,0:T(8,128)S(1)}, u32[]{:S(2)}, u32[]{:S(2)}) collective-permute-start(f32[2,264,128]{2,1,0:T(8,128)S(1)} %pad_maximum_fusion.refs_0_), channel_id=1, source_target_pairs={{0,1},{1,0},{2,3},{3,2},{4,5},{5,4},{6,7},{7,6},{8,9},{9,8},{10,11... | collective-permute-start | bytes 811016 | tf_op jit(solution)/shard_map/ppermute | solution.py:306
  40.7 4.8 %collective-permute-start.18 = (f32[2,264,128]{2,1,0:T(8,128)S(1)}, f32[2,264,128]{2,1,0:T(8,128)S(1)}, u32[]{:S(2)}, u32[]{:S(2)}) collective-permute-start(f32[2,264,128]{2,1,0:T(8,128)S(1)} %collective-permute-done.8.refs_1_), channel_id=1, source_target_pairs={{0,1},{1,0},{2,3},{3,2},{4,5},{5,4},{6,7},{7,6},{8,9},{9,8},{10,11... | collective-permute-start | bytes 811016 | tf_op jit(solution)/shard_map/ppermute | solution.py:306
  45.0 3.3 %collective-permute-start.21 = (f32[2,264,128]{2,1,0:T(8,128)S(1)}, f32[2,264,128]{2,1,0:T(8,128)S(1)}, u32[]{:S(2)}, u32[]{:S(2)}) collective-permute-start(f32[2,264,128]{2,1,0:T(8,128)S(1)} %collective-permute-done.2.refs_4_), channel_id=1, source_target_pairs={{0,1},{1,0},{2,3},{3,2},{4,5},{5,4},{6,7},{7,6},{8,9},{9,8},{10,11... | collective-permute-start | bytes 811016 | tf_op jit(solution)/shard_map/ppermute | solution.py:306
  45.5 2.8 %collective-permute-start.22 = (f32[2,264,128]{2,1,0:T(8,128)S(1)}, f32[2,264,128]{2,1,0:T(8,128)S(1)}, u32[]{:S(2)}, u32[]{:S(2)}) collective-permute-start(f32[2,264,128]{2,1,0:T(8,128)S(1)} %collective-permute-done.10.refs_5_), channel_id=1, source_target_pairs={{0,1},{1,0},{2,3},{3,2},{4,5},{5,4},{6,7},{7,6},{8,9},{9,8},{10,11... | collective-permute-start | bytes 811016 | tf_op jit(solution)/shard_map/ppermute | solution.py:306
  46.7 8.4 %collective-permute-start.25 = (f32[2,256,128]{2,1,0:T(8,128)S(1)}, f32[2,256,128]{2,1,0:T(8,128)S(1)}, u32[]{:S(2)}, u32[]{:S(2)}) collective-permute-start(f32[2,256,128]{2,1,0:T(8,128)S(1)} %collective-permute-done.11.refs_1_), channel_id=1, source_target_pairs={{0,4},{4,0},{8,12},{12,8},{16,20},{20,16},{24,28},{28,24},{1,5},{5... | collective-permute-start | bytes 786440 | tf_op jit(solution)/shard_map/ppermute | solution.py:302
  56.3 5.1 %collective-permute-start.26 = (f32[32,256]{1,0:T(8,128)S(1)}, f32[32,256]{1,0:T(8,128)S(1)}, u32[]{:S(2)}, u32[]{:S(2)}) collective-permute-start(f32[32,256]{1,0:T(8,128)S(1)} %get-tuple-element.66), channel_id=1, source_target_pairs={{0,2},{1,3},{2,0},{3,1},{4,6},{5,7},{6,4},{7,5},{8,10},{9,11},{10,... | collective-permute-start | bytes 98312 | tf_op jit(solution)/shard_map/ppermute | solution.py:306
  57.7 3.7 %collective-permute-start.27 = (f32[32,256]{1,0:T(8,128)S(1)}, f32[32,256]{1,0:T(8,128)S(1)}, u32[]{:S(2)}, u32[]{:S(2)}) collective-permute-start(f32[32,256]{1,0:T(8,128)S(1)} %get-tuple-element.67), channel_id=1, source_target_pairs={{0,1},{1,0},{2,3},{3,2},{4,5},{5,4},{6,7},{7,6},{8,9},{9,8},{10,11... | collective-permute-start | bytes 98312 | tf_op jit(solution)/shard_map/ppermute | solution.py:306
  57.7 3.7 %collective-permute-start.28 = (f32[32,256]{1,0:T(8,128)S(1)}, f32[32,256]{1,0:T(8,128)S(1)}, u32[]{:S(2)}, u32[]{:S(2)}) collective-permute-start(f32[32,256]{1,0:T(8,128)S(1)} %get-tuple-element.68), channel_id=1, source_target_pairs={{0,3},{1,2},{2,1},{3,0},{4,7},{5,6},{6,5},{7,4},{8,11},{9,10},{10,... | collective-permute-start | bytes 98312 | tf_op jit(solution)/shard_map/ppermute | solution.py:306
  (9 other events, 43.8 us)

commit v5 on v4

--- a/solution.py
+++ b/solution.py
@@ -156,8 +156,11 @@
         for m in range(4):
             for second in range(2):
                 for first in range(2):
-                    buf = bufs[8 * crossed + 4 * (m % 2) + 2 * second + first]
-                    found.append((buf.at[m // 2], (crossed, first, second, m)))
+                    buf = bufs[5 * crossed + 2 * (m % 2) + second]
+                    entry = 2 * first + m // 2
+                    if m % 2 == 1 and first + second == 2:
+                        buf, entry = bufs[5 * crossed + 4], m // 2
+                    found.append((buf.at[entry], (crossed, first, second, m)))
     return found
 
 
@@ -196,7 +199,7 @@
 
 
 def first_kernel(place_ref, pair, other_pair, *refs):
-    bufs, (x_ref, high, low, diag) = refs[:16], refs[16:]
+    bufs, (x_ref, high, low, diag) = refs[:10], refs[10:]
     place_pieces(place_ref, bufs, False, high, low, diag)
     n = 128
     i, j = iotas(n)
@@ -235,7 +238,7 @@
 
 
 def second_factor_kernel(place_ref, *refs):
-    bufs, (high, low, diag) = refs[:16], refs[16:]
+    bufs, (high, low, diag) = refs[:10], refs[10:]
     place_pieces(place_ref, bufs, True, high, low, diag)
     n = 128
     i, j = iotas(n)
@@ -368,7 +371,7 @@
     b_out = call(spread_kernel, [shape(2, 32, 256)] * 3, [SMEM, VMEM, VMEM], [VMEM] * 3, [], SPREAD, 4, "spread")(
         place, blocks, came
     )
-    b_z = [swap_z(after(b, far), m + 1) for m, b in enumerate(b_out)]
+    b_z = [swap_z(after(b, far, *((near01,) if m == 2 else ())), m + 1) for m, b in enumerate(b_out)]
     c_far = swap_z(after(c_near, far0), 1)
     c_far_got = swap_y(c_far)
     far01 = cross(after(far0, far1, near01), 1)
@@ -385,15 +388,16 @@
     )(place, blocks, came, *b_z)
     pair = jnp.stack([left, swap_rep(after(left, came), 2)])
     other_pair = swap_rep(after(pair, c_far), 1)
-    bufs = [near, near0, near1, near01, far, far0, far1, far01]
-    bufs += [swap_rep(after(b, b_z[2], far0), 1) for b in bufs[:7]] + [swap_rep(after(far01, far1), 1)]
+    bufs = [jnp.concatenate([near, near0], axis=0), jnp.concatenate([near1, near01], axis=0)]
+    bufs += [jnp.concatenate([far, far0], axis=0), far1, far01]
+    bufs += [swap_rep(after(b, b_z[2], far0), 1) for b in bufs[:4]] + [swap_rep(after(far01, far1), 1)]
 
     scratch = [pltpu.VMEM((8, 136, 128), F32)]
     halves = [shape(1024, 1024, dtype=BF16)] * 2
     x = call(
         first_kernel,
         shape(128, 1024),
-        [SMEM] + [VMEM] * 18,
+        [SMEM] + [VMEM] * 12,
         VMEM,
         [pltpu.VMEM((1024, 1024), BF16)] * 2 + scratch,
         FIRST,
@@ -414,7 +418,7 @@
     back = [swap_rep(to_x, 2), swap_rep(to_core, 1), swap_rep(to_both, 3)]
 
     uh, ul = call(
-        second_factor_kernel, halves, [SMEM] + [VMEM] * 16, [VMEM] * 2, scratch, SECOND, 24, "second_factor"
+        second_factor_kernel, halves, [SMEM] + [VMEM] * 10, [VMEM] * 2, scratch, SECOND, 24, "second_factor"
     )(after(place, mine), *bufs)
 
     return call(second_kernel, shape(32, 2048), [SMEM] + [VMEM] * 8, VMEM, [], 2_500_000_000, 24, "second_panel")(

time: 63.7 us -> 68.2 us (1.071)
  waiting for transfers between devices: 18.3 us -> 20.8 us
  starting transfers between devices: 29.3 us -> 31.1 us
    ppermute x3, starting transfers between devices: 1.53 us -> 3.68 us  [cross(): return lax.ppermute(x, BOTH, pairs)]
    ppermute x4, waiting for transfers between devices: 3.2 us -> 5.35 us  [swap_y(): return lax.ppermute(x, 'bulk', [(k, k ^ 1) for k in range(8)])]
    ppermute x15 -> x12, waiting for transfers between devices: 3.97 us -> 5.87 us  [swap_rep(): return lax.ppermute(x, 'rep', [(k, k ^ bits) for k in range(4)])]
    ppermute x4, starting transfers between devices: 5.72 us -> 4.25 us  [swap_y(): return lax.ppermute(x, 'bulk', [(k, k ^ 1) for k in range(8)])]
    ppermute x7, waiting for transfers between devices: 10.7 us -> 9.6 us  [swap_z(): return lax.ppermute(x, 'bulk', [(k, k ^ 2 * m) for k in range(8)])]
    ppermute x15 -> x12, starting transfers between devices: 8.21 us -> 9.13 us  [swap_rep(): return lax.ppermute(x, 'rep', [(k, k ^ bits) for k in range(4)])]
    unnamed x8 -> x10, local copies, waits for them, and re-layouts: 1.59 us -> 1.63 us
  transfers between devices with their start and end apart: 29 -> 26, of which waited for: 9 -> 9; matrix products, arithmetic and copies ran while one was open for 0% -> 0% of each run, Pallas kernels for 13% -> 12%
where the time goes in v5:
time: 68.2 us; the launch traced here: 67.9 us
  starting transfers between devices  31.1 us (46%)
  waiting for transfers between devices  20.8 us (30%)
  Pallas kernels  14 us (21%)
  local copies, waits for them, and re-layouts  1.67 us (2%)
    ppermute x7, starting transfers between devices, swap_z(): return lax.ppermute(x, 'bulk', [(k, k ^ 2 * m) for k in range(8)])  14 us
    ppermute x7, waiting for transfers between devices, swap_z(): return lax.ppermute(x, 'bulk', [(k, k ^ 2 * m) for k in range(8)])  9.6 us
    ppermute x12, starting transfers between devices, swap_rep(): return lax.ppermute(x, 'rep', [(k, k ^ bits) for k in range(4)])  9.13 us
    ppermute x12, waiting for transfers between devices, swap_rep(): return lax.ppermute(x, 'rep', [(k, k ^ bits) for k in range(4)])  5.87 us
    ppermute x4, waiting for transfers between devices, swap_y(): return lax.ppermute(x, 'bulk', [(k, k ^ 1) for k in range(8)])  5.35 us
    ppermute x4, starting transfers between devices, swap_y(): return lax.ppermute(x, 'bulk', [(k, k ^ 1) for k in range(8)])  4.25 us
    ppermute x3, starting transfers between devices, cross(): return lax.ppermute(x, BOTH, pairs)  3.68 us
    pallas_call x1, Pallas kernels, per_device(): call(first_kernel, shape(128, 1024), [SMEM] + [VMEM] * 12, VMEM, [pltpu.V...  3.58 us
  transfers between devices with their start and end apart: 26, of which 9 were waited for; matrix products, arithmetic and copies ran while one was open for 0% of the time, Pallas kernels for 12%

profile of v5, /device:TPU:0, one launch (start us, length us, event | category | flops | bytes accessed | tf_op | source)
XLA Modules:
  0.0 67.9 jit_solution(13959102561162543038)
XLA Ops:
  0.1 0.9 %copy-done.1 = f32[256,128]{1,0:T(8,128)S(1)} copy-done((f32[256,128]{1,0:T(8,128)S(1)}, f32[256,128]{1,0:T(8,128)}, u32[]{:S(2)}) %copy-start.1) | copy-done | bytes 131096
  1.7 2.6 %invert.1 = f32[264,128]{1,0:T(8,128)S(1)} custom-call(s32[2]{0:T(128)S(1)} %pad_add_fusion.place_ref, f32[256,128]{1,0:T(8,128)S(1)} %copy-done.1, f32[2,128]{1,0:T(2,128)S(1)} %copy-done.2), custom_call_target="tpu_custom_call" | custom-call | flops 3500000000 | bytes 2097152 | tf_op jit(solution)/shard_map/invert/pallas_call | solution.py:352
  4.2 2.1 %collective-permute-start.1 = (f32[264,128]{1,0:T(8,128)S(1)}, f32[264,128]{1,0:T(8,128)S(1)}, u32[]{:S(2)}, u32[]{:S(2)}) collective-permute-start(f32[264,128]{1,0:T(8,128)S(1)} %invert.1), channel_id=1, source_target_pairs={{0,16},{4,20},{8,24},{12,28},{16,0},{20,4},{24,8},{28,12},{1,17},{... | collective-permute-start | bytes 405512 | tf_op jit(solution)/shard_map/ppermute | solution.py:301
  6.3 6.8 %collective-permute-done.1 = f32[264,128]{1,0:T(8,128)S(1)} collective-permute-done((f32[264,128]{1,0:T(8,128)S(1)}, f32[264,128]{1,0:T(8,128)S(1)}, u32[]{:S(2)}, u32[]{:S(2)}) %collective-permute-start.1) | collective-permute-done | bytes 135200 | tf_op jit(solution)/shard_map/ppermute | solution.py:301
  13.1 2.0 %collective-permute-start.5 = (f32[2,264,128]{2,1,0:T(8,128)S(1)}, f32[2,264,128]{2,1,0:T(8,128)S(1)}, u32[]{:S(2)}, u32[]{:S(2)}) collective-permute-start(f32[2,264,128]{2,1,0:T(8,128)S(1)} %pad_maximum_fusion.1), channel_id=1, source_target_pairs={{0,4},{4,0},{8,12},{12,8},{16,20},{20,16},{24,28},{28,24},{1,5},{5... | collective-permute-start | bytes 811016 | tf_op jit(solution)/shard_map/ppermute | solution.py:305
  15.9 2.0 %collective-permute-start.10 = (f32[2,264,128]{2,1,0:T(8,128)S(1)}, f32[2,264,128]{2,1,0:T(8,128)S(1)}, u32[]{:S(2)}, u32[]{:S(2)}) collective-permute-start(f32[2,264,128]{2,1,0:T(8,128)S(1)} %pad_maximum_fusion.1), channel_id=1, source_target_pairs={{0,2},{1,3},{2,0},{3,1},{4,6},{5,7},{6,4},{7,5},{8,10},{9,11},{10,... | collective-permute-start | bytes 811016 | tf_op jit(solution)/shard_map/ppermute | solution.py:309
  17.8 2.7 %collective-permute-start.9 = (f32[256,128]{1,0:T(8,128)S(1)}, f32[256,128]{1,0:T(8,128)S(1)}, u32[]{:S(2)}, u32[]{:S(2)}) collective-permute-start(f32[256,128]{1,0:T(8,128)S(1)} %copy-done.3), channel_id=1, source_target_pairs={{0,16},{4,20},{8,24},{12,28},{16,0},{20,4},{24,8},{28,12},{1,17},{... | collective-permute-start | bytes 393224 | tf_op jit(solution)/shard_map/ppermute | solution.py:301
  21.6 2.0 %collective-permute-start.6 = (f32[2,264,128]{2,1,0:T(8,128)S(1)}, f32[2,264,128]{2,1,0:T(8,128)S(1)}, u32[]{:S(2)}, u32[]{:S(2)}) collective-permute-start(f32[2,264,128]{2,1,0:T(8,128)S(1)} %collective-permute-done.5), channel_id=1, source_target_pairs={{0,2},{1,3},{2,0},{3,1},{4,6},{5,7},{6,4},{7,5},{8,10},{9,11},{10,... | collective-permute-start | bytes 811016 | tf_op jit(solution)/shard_map/ppermute | solution.py:309
  23.7 2.1 %collective-permute-done.9 = f32[256,128]{1,0:T(8,128)S(1)} collective-permute-done((f32[256,128]{1,0:T(8,128)S(1)}, f32[256,128]{1,0:T(8,128)S(1)}, u32[]{:S(2)}, u32[]{:S(2)}) %collective-permute-start.9) | collective-permute-done | bytes 131104 | tf_op jit(solution)/shard_map/ppermute | solution.py:301
  26.5 1.5 %collective-permute-start.15 = (f32[2,264,128]{2,1,0:T(8,128)S(1)}, f32[2,264,128]{2,1,0:T(8,128)S(1)}, u32[]{:S(2)}, u32[]{:S(2)}) collective-permute-start(f32[2,264,128]{2,1,0:T(8,128)S(1)} %collective-permute-done.2), channel_id=1, source_target_pairs={{0,4},{4,0},{8,12},{12,8},{16,20},{20,16},{24,28},{28,24},{1,3},{5... | collective-permute-start | bytes 811016 | tf_op jit(solution)/shard_map/ppermute | solution.py:318
  28.7 3.3 %collective-permute-start.3 = (f32[2,32,256]{2,1,0:T(8,128)S(1)}, f32[2,32,256]{2,1,0:T(8,128)S(1)}, u32[]{:S(2)}, u32[]{:S(2)}) collective-permute-start(f32[2,32,256]{2,1,0:T(8,128)S(1)} %get-tuple-element.36), channel_id=1, source_target_pairs={{0,8},{4,12},{8,0},{12,4},{16,24},{20,28},{24,16},{28,20},{1,9},{5... | collective-permute-start | bytes 196616 | tf_op jit(solution)/shard_map/ppermute | solution.py:301
  31.9 1.6 %collective-permute-start.4 = (f32[2,32,256]{2,1,0:T(8,128)S(1)}, f32[2,32,256]{2,1,0:T(8,128)S(1)}, u32[]{:S(2)}, u32[]{:S(2)}) collective-permute-start(f32[2,32,256]{2,1,0:T(8,128)S(1)} %get-tuple-element.38), channel_id=1, source_target_pairs={{0,16},{4,20},{8,24},{12,28},{16,0},{20,4},{24,8},{28,12},{1,17},{... | collective-permute-start | bytes 196616 | tf_op jit(solution)/shard_map/ppermute | solution.py:301
  33.7 4.1 %collective-permute-start.7 = (f32[2,32,256]{2,1,0:T(8,128)S(1)}, f32[2,32,256]{2,1,0:T(8,128)S(1)}, u32[]{:S(2)}, u32[]{:S(2)}) collective-permute-start(f32[2,32,256]{2,1,0:T(8,128)S(1)} %get-tuple-element.40), channel_id=1, source_target_pairs={{0,24},{4,28},{8,16},{12,20},{16,8},{20,12},{24,0},{28,4},{1,25},{... | collective-permute-start | bytes 196616 | tf_op jit(solution)/shard_map/ppermute | solution.py:301
  37.8 1.6 %collective-permute-start.14 = (f32[2,256,128]{2,1,0:T(8,128)S(1)}, f32[2,256,128]{2,1,0:T(8,128)S(1)}, u32[]{:S(2)}, u32[]{:S(2)}) collective-permute-start(f32[2,256,128]{2,1,0:T(8,128)S(1)} %pad_maximum_fusion.3.refs_0_), channel_id=1, source_target_pairs={{0,4},{4,0},{8,12},{12,8},{16,20},{20,16},{24,28},{28,24},{1,5},{5... | collective-permute-start | bytes 786440 | tf_op jit(solution)/shard_map/ppermute | solution.py:305
  39.6 1.5 %collective-permute-start.16 = (f32[2,264,128]{2,1,0:T(8,128)S(1)}, f32[2,264,128]{2,1,0:T(8,128)S(1)}, u32[]{:S(2)}, u32[]{:S(2)}) collective-permute-start(f32[2,264,128]{2,1,0:T(8,128)S(1)} %collective-permute-done.11), channel_id=1, source_target_pairs={{0,4},{4,0},{8,12},{12,8},{16,20},{20,16},{24,28},{28,24},{1,3},{5... | collective-permute-start | bytes 811016 | tf_op jit(solution)/shard_map/ppermute | solution.py:318
  41.7 1.8 %collective-permute-start.8 = (f32[32,1024]{1,0:T(8,128)S(1)}, f32[32,1024]{1,0:T(8,128)S(1)}, u32[]{:S(2)}, u32[]{:S(2)}) collective-permute-start(f32[32,1024]{1,0:T(8,128)S(1)} %get-tuple-element.42), channel_id=1, source_target_pairs={{0,2},{1,3},{2,0},{3,1},{4,6},{5,7},{6,4},{7,5},{8,10},{9,11},{10,... | collective-permute-start | bytes 393224 | tf_op jit(solution)/shard_map/ppermute | solution.py:309
  44.2 3.8 %collective-permute-done.8 = f32[32,1024]{1,0:T(8,128)S(1)} collective-permute-done((f32[32,1024]{1,0:T(8,128)S(1)}, f32[32,1024]{1,0:T(8,128)S(1)}, u32[]{:S(2)}, u32[]{:S(2)}) %collective-permute-start.8) | collective-permute-done | bytes 131104 | tf_op jit(solution)/shard_map/ppermute | solution.py:309
  49.1 2.0 %collective-permute-done.13.other_pair = f32[2,32,1024]{2,1,0:T(8,128)S(1)} collective-permute-done((f32[2,32,1024]{2,1,0:T(8,128)S(1)}, f32[2,32,1024]{2,1,0:T(8,128)S(1)}, u32[]{:S(2)}, u32[]{:S(2)}) %collective-permute-start.13) | collective-permute-done | bytes 262176 | tf_op jit(solution)/shard_map/ppermute | solution.py:309
  51.6 3.6 %first_panel.1.x_ref = f32[128,1024]{1,0:T(8,128)S(1)} custom-call(s32[2]{0:T(128)S(1)} %pad_add_fusion.place_ref, f32[2,32,1024]{2,1,0:T(8,128)S(1)} %pad_maximum_fusion.2.pair, f32[2,32,1024]{2,1,0:T(8,128)S(1)} %collective-permute-done.13.other_pair, f32[4,264,128]{2,1,0:T(8,128)S(1)} %pad_maximum_fusion.refs_0_, ...), custom_call_target="tpu_custom_call" | custom-call | flops 200000000 | bytes 2097152 | tf_op jit(solution)/shard_map/first_panel/pallas_call | solution.py:397
  55.2 4.2 %collective-permute-done.22.refs_3_ = f32[2,256,128]{2,1,0:T(8,128)S(1)} collective-permute-done((f32[2,256,128]{2,1,0:T(8,128)S(1)}, f32[2,256,128]{2,1,0:T(8,128)S(1)}, u32[]{:S(2)}, u32[]{:S(2)}) %collective-permute-start.22) | collective-permute-done | bytes 262176 | tf_op jit(solution)/shard_map/ppermute | solution.py:305
  59.5 1.3 %update.1 = (f32[32,256]{1,0:T(8,128)S(1)}, f32[32,256]{1,0:T(8,128)S(1)}, f32[32,256]{1,0:T(8,128)S(1)}, f32[32,256]{1,0:T(8,128)S(1)}) custom-call(s32[2]{0:T(128)S(1)} %pad_add_fusion.place_ref, f32[128,1024]{1,0:T(8,128)S(1)} %first_panel.1.x_ref, f32[2,256,128]{2,1,0:T(8,128)S(1)} %pad_maximum_fusion.3.refs_0_, ...), custom_call_target="tpu_custom_call" | custom-call | flops 2000000000 | bytes 2097152 | tf_op jit(solution)/shard_map/update/pallas_call | solution.py:408
  60.7 1.8 %collective-permute-start.23 = (f32[32,256]{1,0:T(8,128)S(1)}, f32[32,256]{1,0:T(8,128)S(1)}, u32[]{:S(2)}, u32[]{:S(2)}) collective-permute-start(f32[32,256]{1,0:T(8,128)S(1)} %get-tuple-element.60), channel_id=1, source_target_pairs={{0,2},{1,3},{2,0},{3,1},{4,6},{5,7},{6,4},{7,5},{8,10},{9,11},{10,... | collective-permute-start | bytes 98312 | tf_op jit(solution)/shard_map/ppermute | solution.py:309
  62.9 2.9 %second_factor.1 = (bf16[1024,1024]{1,0:T(8,128)(2,1)S(1)}, bf16[1024,1024]{1,0:T(8,128)(2,1)S(1)}) custom-call(s32[2]{0:T(128)S(1)} %pad_add_fusion.place_ref, f32[4,264,128]{2,1,0:T(8,128)S(1)} %pad_maximum_fusion.refs_0_, f32[4,264,128]{2,1,0:T(8,128)S(1)} %constant_dynamic-update-slice_fusion.refs_1_, ...), custom_call_target="tpu_custom_call" | custom-call | flops 3000000000 | bytes 2097152 | tf_op jit(solution)/shard_map/second_factor/pallas_call | solution.py:420
  65.9 2.1 %second_panel.1 = f32[32,2048]{1,0:T(8,128)} custom-call(s32[2]{0:T(128)S(1)} %pad_add_fusion.place_ref, f32[128,1024]{1,0:T(8,128)S(1)} %first_panel.1.x_ref, f32[2,32,1024]{2,1,0:T(8,128)S(1)} %get-tuple-element.55.both_ref, bf16[1024,1024]{1,0:T(8,128)(2,1)S(1)} %get-tuple-element.58.uh_ref, bf16[1024,1024]{1,0:T(8,128)(2,1)S(1)} %get-tuple-element.59.ul_ref, ...), custom_call_target="tpu_custom_call" | custom-call | flops 2500000000 | bytes 2097152 | tf_op jit(solution)/shard_map/second_panel/pallas_call | solution.py:424
  (53 shorter events, 7.6 us)
Async XLA Ops:
  4.2 8.9 %collective-permute-start.1 = (f32[264,128]{1,0:T(8,128)S(1)}, f32[264,128]{1,0:T(8,128)S(1)}, u32[]{:S(2)}, u32[]{:S(2)}) collective-permute-start(f32[264,128]{1,0:T(8,128)S(1)} %invert.1), channel_id=1, source_target_pairs={{0,16},{4,20},{8,24},{12,28},{16,0},{20,4},{24,8},{28,12},{1,17},{... | collective-permute-start | bytes 405512 | tf_op jit(solution)/shard_map/ppermute | solution.py:301
  13.1 8.5 %collective-permute-start.5 = (f32[2,264,128]{2,1,0:T(8,128)S(1)}, f32[2,264,128]{2,1,0:T(8,128)S(1)}, u32[]{:S(2)}, u32[]{:S(2)}) collective-permute-start(f32[2,264,128]{2,1,0:T(8,128)S(1)} %pad_maximum_fusion.1), channel_id=1, source_target_pairs={{0,4},{4,0},{8,12},{12,8},{16,20},{20,16},{24,28},{28,24},{1,5},{5... | collective-permute-start | bytes 811016 | tf_op jit(solution)/shard_map/ppermute | solution.py:305
  15.7 5.3 %collective-permute-start = (f32[4,32,256]{2,1,0:T(8,128)S(1)}, f32[4,32,256]{2,1,0:T(8,128)S(1)}, u32[]{:S(2)}, u32[]{:S(2)}) collective-permute-start(f32[4,32,256]{2,1,0:T(8,128)S(1)} %leave.1), channel_id=1, source_target_pairs={{0,4},{4,0},{8,12},{12,8},{16,20},{20,16},{24,28},{28,24},{1,5},{5... | collective-permute-start | bytes 393224 | tf_op jit(solution)/shard_map/ppermute | solution.py:305
  15.9 9.9 %collective-permute-start.10 = (f32[2,264,128]{2,1,0:T(8,128)S(1)}, f32[2,264,128]{2,1,0:T(8,128)S(1)}, u32[]{:S(2)}, u32[]{:S(2)}) collective-permute-start(f32[2,264,128]{2,1,0:T(8,128)S(1)} %pad_maximum_fusion.1), channel_id=1, source_target_pairs={{0,2},{1,3},{2,0},{3,1},{4,6},{5,7},{6,4},{7,5},{8,10},{9,11},{10,... | collective-permute-start | bytes 811016 | tf_op jit(solution)/shard_map/ppermute | solution.py:309
  17.8 8.7 %collective-permute-start.2 = (f32[2,264,128]{2,1,0:T(8,128)S(1)}, f32[2,264,128]{2,1,0:T(8,128)S(1)}, u32[]{:S(2)}, u32[]{:S(2)}) collective-permute-start(f32[2,264,128]{2,1,0:T(8,128)S(1)} %pad_maximum_fusion.1), channel_id=1, source_target_pairs={{0,8},{4,12},{8,0},{12,4},{16,24},{20,28},{24,16},{28,20},{1,9},{5... | collective-permute-start | bytes 811016 | tf_op jit(solution)/shard_map/ppermute | solution.py:301
  17.8 8.0 %collective-permute-start.9 = (f32[256,128]{1,0:T(8,128)S(1)}, f32[256,128]{1,0:T(8,128)S(1)}, u32[]{:S(2)}, u32[]{:S(2)}) collective-permute-start(f32[256,128]{1,0:T(8,128)S(1)} %copy-done.3), channel_id=1, source_target_pairs={{0,16},{4,20},{8,24},{12,28},{16,0},{20,4},{24,8},{28,12},{1,17},{... | collective-permute-start | bytes 393224 | tf_op jit(solution)/shard_map/ppermute | solution.py:301
  21.6 12.0 %collective-permute-start.6 = (f32[2,264,128]{2,1,0:T(8,128)S(1)}, f32[2,264,128]{2,1,0:T(8,128)S(1)}, u32[]{:S(2)}, u32[]{:S(2)}) collective-permute-start(f32[2,264,128]{2,1,0:T(8,128)S(1)} %collective-permute-done.5), channel_id=1, source_target_pairs={{0,2},{1,3},{2,0},{3,1},{4,6},{5,7},{6,4},{7,5},{8,10},{9,11},{10,... | collective-permute-start | bytes 811016 | tf_op jit(solution)/shard_map/ppermute | solution.py:309
  26.5 11.2 %collective-permute-start.15 = (f32[2,264,128]{2,1,0:T(8,128)S(1)}, f32[2,264,128]{2,1,0:T(8,128)S(1)}, u32[]{:S(2)}, u32[]{:S(2)}) collective-permute-start(f32[2,264,128]{2,1,0:T(8,128)S(1)} %collective-permute-done.2), channel_id=1, source_target_pairs={{0,4},{4,0},{8,12},{12,8},{16,20},{20,16},{24,28},{28,24},{1,3},{5... | collective-permute-start | bytes 811016 | tf_op jit(solution)/shard_map/ppermute | solution.py:318
  28.0 11.3 %collective-permute-start.11 = (f32[2,264,128]{2,1,0:T(8,128)S(1)}, f32[2,264,128]{2,1,0:T(8,128)S(1)}, u32[]{:S(2)}, u32[]{:S(2)}) collective-permute-start(f32[2,264,128]{2,1,0:T(8,128)S(1)} %collective-permute-done.2), channel_id=1, source_target_pairs={{0,2},{4,6},{8,10},{12,14},{16,18},{20,22},{24,26},{28,30},{1,5},{... | collective-permute-start | bytes 811016 | tf_op jit(solution)/shard_map/ppermute | solution.py:318
  28.7 10.9 %collective-permute-start.3 = (f32[2,32,256]{2,1,0:T(8,128)S(1)}, f32[2,32,256]{2,1,0:T(8,128)S(1)}, u32[]{:S(2)}, u32[]{:S(2)}) collective-permute-start(f32[2,32,256]{2,1,0:T(8,128)S(1)} %get-tuple-element.36), channel_id=1, source_target_pairs={{0,8},{4,12},{8,0},{12,4},{16,24},{20,28},{24,16},{28,20},{1,9},{5... | collective-permute-start | bytes 196616 | tf_op jit(solution)/shard_map/ppermute | solution.py:301
  31.9 9.1 %collective-permute-start.4 = (f32[2,32,256]{2,1,0:T(8,128)S(1)}, f32[2,32,256]{2,1,0:T(8,128)S(1)}, u32[]{:S(2)}, u32[]{:S(2)}) collective-permute-start(f32[2,32,256]{2,1,0:T(8,128)S(1)} %get-tuple-element.38), channel_id=1, source_target_pairs={{0,16},{4,20},{8,24},{12,28},{16,0},{20,4},{24,8},{28,12},{1,17},{... | collective-permute-start | bytes 196616 | tf_op jit(solution)/shard_map/ppermute | solution.py:301
  33.7 7.4 %collective-permute-start.7 = (f32[2,32,256]{2,1,0:T(8,128)S(1)}, f32[2,32,256]{2,1,0:T(8,128)S(1)}, u32[]{:S(2)}, u32[]{:S(2)}) collective-permute-start(f32[2,32,256]{2,1,0:T(8,128)S(1)} %get-tuple-element.40), channel_id=1, source_target_pairs={{0,24},{4,28},{8,16},{12,20},{16,8},{20,12},{24,0},{28,4},{1,25},{... | collective-permute-start | bytes 196616 | tf_op jit(solution)/shard_map/ppermute | solution.py:301
  37.8 6.4 %collective-permute-start.14 = (f32[2,256,128]{2,1,0:T(8,128)S(1)}, f32[2,256,128]{2,1,0:T(8,128)S(1)}, u32[]{:S(2)}, u32[]{:S(2)}) collective-permute-start(f32[2,256,128]{2,1,0:T(8,128)S(1)} %pad_maximum_fusion.3.refs_0_), channel_id=1, source_target_pairs={{0,4},{4,0},{8,12},{12,8},{16,20},{20,16},{24,28},{28,24},{1,5},{5... | collective-permute-start | bytes 786440 | tf_op jit(solution)/shard_map/ppermute | solution.py:305
  39.3 8.7 %collective-permute-start.12 = (f32[2,256,128]{2,1,0:T(8,128)S(1)}, f32[2,256,128]{2,1,0:T(8,128)S(1)}, u32[]{:S(2)}, u32[]{:S(2)}) collective-permute-start(f32[2,256,128]{2,1,0:T(8,128)S(1)} %pad_maximum_fusion.3.refs_0_), channel_id=1, source_target_pairs={{0,8},{4,12},{8,0},{12,4},{16,24},{20,28},{24,16},{28,20},{1,9},{5... | collective-permute-start | bytes 786440 | tf_op jit(solution)/shard_map/ppermute | solution.py:301
  39.6 9.0 %collective-permute-start.16 = (f32[2,264,128]{2,1,0:T(8,128)S(1)}, f32[2,264,128]{2,1,0:T(8,128)S(1)}, u32[]{:S(2)}, u32[]{:S(2)}) collective-permute-start(f32[2,264,128]{2,1,0:T(8,128)S(1)} %collective-permute-done.11), channel_id=1, source_target_pairs={{0,4},{4,0},{8,12},{12,8},{16,20},{20,16},{24,28},{28,24},{1,3},{5... | collective-permute-start | bytes 811016 | tf_op jit(solution)/shard_map/ppermute | solution.py:318
  41.7 6.3 %collective-permute-start.8 = (f32[32,1024]{1,0:T(8,128)S(1)}, f32[32,1024]{1,0:T(8,128)S(1)}, u32[]{:S(2)}, u32[]{:S(2)}) collective-permute-start(f32[32,1024]{1,0:T(8,128)S(1)} %get-tuple-element.42), channel_id=1, source_target_pairs={{0,2},{1,3},{2,0},{3,1},{4,6},{5,7},{6,4},{7,5},{8,10},{9,11},{10,... | collective-permute-start | bytes 393224 | tf_op jit(solution)/shard_map/ppermute | solution.py:309
  43.5 5.1 %collective-permute-start.20 = (f32[2,264,128]{2,1,0:T(8,128)S(1)}, f32[2,264,128]{2,1,0:T(8,128)S(1)}, u32[]{:S(2)}, u32[]{:S(2)}) collective-permute-start(f32[2,264,128]{2,1,0:T(8,128)S(1)} %collective-permute-done.15.refs_3_), channel_id=1, source_target_pairs={{0,1},{1,0},{2,3},{3,2},{4,5},{5,4},{6,7},{7,6},{8,9},{9,8},{10,11... | collective-permute-start | bytes 811016 | tf_op jit(solution)/shard_map/ppermute | solution.py:309
  44.2 7.4 %collective-permute-start.18 = (f32[4,264,128]{2,1,0:T(8,128)S(1)}, f32[4,264,128]{2,1,0:T(8,128)S(1)}, u32[]{:S(2)}, u32[]{:S(2)}) collective-permute-start(f32[4,264,128]{2,1,0:T(8,128)S(1)} %constant_dynamic-update-slice_fusion.refs_1_), channel_id=1, source_target_pairs={{0,1},{1,0},{2,3},{3,2},{4,5},{5,4},{6,7},{7,6},{8,9},{9,8},{10,11... | collective-permute-start | bytes 1622024 | tf_op jit(solution)/shard_map/ppermute | solution.py:309
  48.0 3.6 %collective-permute-start.19 = (f32[4,264,128]{2,1,0:T(8,128)S(1)}, f32[4,264,128]{2,1,0:T(8,128)S(1)}, u32[]{:S(2)}, u32[]{:S(2)}) collective-permute-start(f32[4,264,128]{2,1,0:T(8,128)S(1)} %constant_dynamic-update-slice_fusion.2.refs_2_), channel_id=1, source_target_pairs={{0,1},{1,0},{2,3},{3,2},{4,5},{5,4},{6,7},{7,6},{8,9},{9,8},{10,11... | collective-permute-start | bytes 1622024 | tf_op jit(solution)/shard_map/ppermute | solution.py:309
  48.0 3.6 %collective-permute-start.17 = (f32[4,264,128]{2,1,0:T(8,128)S(1)}, f32[4,264,128]{2,1,0:T(8,128)S(1)}, u32[]{:S(2)}, u32[]{:S(2)}) collective-permute-start(f32[4,264,128]{2,1,0:T(8,128)S(1)} %pad_maximum_fusion.refs_0_), channel_id=1, source_target_pairs={{0,1},{1,0},{2,3},{3,2},{4,5},{5,4},{6,7},{7,6},{8,9},{9,8},{10,11... | collective-permute-start | bytes 1622024 | tf_op jit(solution)/shard_map/ppermute | solution.py:309
  51.1 8.3 %collective-permute-start.22 = (f32[2,256,128]{2,1,0:T(8,128)S(1)}, f32[2,256,128]{2,1,0:T(8,128)S(1)}, u32[]{:S(2)}, u32[]{:S(2)}) collective-permute-start(f32[2,256,128]{2,1,0:T(8,128)S(1)} %collective-permute-done.12.refs_1_), channel_id=1, source_target_pairs={{0,4},{4,0},{8,12},{12,8},{16,20},{20,16},{24,28},{28,24},{1,5},{5... | collective-permute-start | bytes 786440 | tf_op jit(solution)/shard_map/ppermute | solution.py:305
  60.7 5.1 %collective-permute-start.23 = (f32[32,256]{1,0:T(8,128)S(1)}, f32[32,256]{1,0:T(8,128)S(1)}, u32[]{:S(2)}, u32[]{:S(2)}) collective-permute-start(f32[32,256]{1,0:T(8,128)S(1)} %get-tuple-element.60), channel_id=1, source_target_pairs={{0,2},{1,3},{2,0},{3,1},{4,6},{5,7},{6,4},{7,5},{8,10},{9,11},{10,... | collective-permute-start | bytes 98312 | tf_op jit(solution)/shard_map/ppermute | solution.py:309
  62.5 3.3 %collective-permute-start.24 = (f32[32,256]{1,0:T(8,128)S(1)}, f32[32,256]{1,0:T(8,128)S(1)}, u32[]{:S(2)}, u32[]{:S(2)}) collective-permute-start(f32[32,256]{1,0:T(8,128)S(1)} %get-tuple-element.61), channel_id=1, source_target_pairs={{0,1},{1,0},{2,3},{3,2},{4,5},{5,4},{6,7},{7,6},{8,9},{9,8},{10,11... | collective-permute-start | bytes 98312 | tf_op jit(solution)/shard_map/ppermute | solution.py:309
  62.5 3.3 %collective-permute-start.25 = (f32[32,256]{1,0:T(8,128)S(1)}, f32[32,256]{1,0:T(8,128)S(1)}, u32[]{:S(2)}, u32[]{:S(2)}) collective-permute-start(f32[32,256]{1,0:T(8,128)S(1)} %get-tuple-element.62), channel_id=1, source_target_pairs={{0,3},{1,2},{2,1},{3,0},{4,7},{5,6},{6,5},{7,4},{8,11},{9,10},{10,... | collective-permute-start | bytes 98312 | tf_op jit(solution)/shard_map/ppermute | solution.py:309
  (6 other events, 34.2 us)

commit v6 on v4

--- a/solution.py
+++ b/solution.py
@@ -401,6 +401,10 @@
         "first_panel",
     )(place, pair, after(other_pair, c_near_got), *bufs)
 
+    uh, ul = call(
+        second_factor_kernel, halves, [SMEM] + [VMEM] * 16, [VMEM] * 2, scratch, SECOND, 24, "second_factor"
+    )(after(place, x), *bufs)
+
     mine, to_x, to_core, to_both = call(
         update_kernel,
         [shape(32, 256)] * 4,
@@ -410,12 +414,8 @@
         2_000_000_000,
         24,
         "update",
-    )(place, x, c_near, c_far, c_near_got, c_far_got)
+    )(place, after(x, uh), c_near, c_far, c_near_got, c_far_got)
     back = [swap_rep(to_x, 2), swap_rep(to_core, 1), swap_rep(to_both, 3)]
-
-    uh, ul = call(
-        second_factor_kernel, halves, [SMEM] + [VMEM] * 16, [VMEM] * 2, scratch, SECOND, 24, "second_factor"
-    )(after(place, mine), *bufs)
 
     return call(second_kernel, shape(32, 2048), [SMEM] + [VMEM] * 8, VMEM, [], 2_500_000_000, 24, "second_panel")(
         place, x, both, uh, ul, mine, *back

time: 63.7 us -> 70.3 us (1.10)
  waiting for transfers between devices: 18.3 us -> 24.9 us
    ppermute x15, waiting for transfers between devices: 3.97 us -> 7.96 us  [swap_rep(): return lax.ppermute(x, 'rep', [(k, k ^ bits) for k in range(4)])]
    ppermute x3, waiting for transfers between devices: 0.41 us -> 2.59 us  [cross(): return lax.ppermute(x, BOTH, pairs)]
    ppermute x4, waiting for transfers between devices: 3.2 us -> 5.17 us  [swap_y(): return lax.ppermute(x, 'bulk', [(k, k ^ 1) for k in range(8)])]
    ppermute x4, starting transfers between devices: 5.72 us -> 3.89 us  [swap_y(): return lax.ppermute(x, 'bulk', [(k, k ^ 1) for k in range(8)])]
    ppermute x7, waiting for transfers between devices: 10.7 us -> 9.19 us  [swap_z(): return lax.ppermute(x, 'bulk', [(k, k ^ 2 * m) for k in range(8)])]
    ppermute x3, starting transfers between devices: 1.53 us -> 2.85 us  [cross(): return lax.ppermute(x, BOTH, pairs)]
  transfers between devices with their start and end apart: 29 -> 29, of which waited for: 9 -> 16; matrix products, arithmetic and copies ran while one was open for 0% -> 0% of each run, Pallas kernels for 13% -> 12%
where the time goes in v6:
time: 70.3 us; the launch traced here: 69.6 us
  starting transfers between devices  28.8 us (41%)
  waiting for transfers between devices  24.9 us (35%)
  Pallas kernels  14 us (20%)
  local copies, waits for them, and re-layouts  1.59 us (2%)
    ppermute x7, starting transfers between devices, swap_z(): return lax.ppermute(x, 'bulk', [(k, k ^ 2 * m) for k in range(8)])  14.3 us
    ppermute x7, waiting for transfers between devices, swap_z(): return lax.ppermute(x, 'bulk', [(k, k ^ 2 * m) for k in range(8)])  9.19 us
    ppermute x15, waiting for transfers between devices, swap_rep(): return lax.ppermute(x, 'rep', [(k, k ^ bits) for k in range(4)])  7.96 us
    ppermute x15, starting transfers between devices, swap_rep(): return lax.ppermute(x, 'rep', [(k, k ^ bits) for k in range(4)])  7.82 us
    ppermute x4, waiting for transfers between devices, swap_y(): return lax.ppermute(x, 'bulk', [(k, k ^ 1) for k in range(8)])  5.17 us
    ppermute x4, starting transfers between devices, swap_y(): return lax.ppermute(x, 'bulk', [(k, k ^ 1) for k in range(8)])  3.89 us
    pallas_call x1, Pallas kernels, per_device(): call(first_kernel, shape(128, 1024), [SMEM] + [VMEM] * 18, VMEM, [pltpu.V...  3.58 us
    pallas_call x1, Pallas kernels, per_device(): call(second_factor_kernel, halves, [SMEM] + [VMEM] * 16, [VMEM] * 2, scra...  2.88 us
  transfers between devices with their start and end apart: 29, of which 16 were waited for; matrix products, arithmetic and copies ran while one was open for 0% of the time, Pallas kernels for 12%

profile of v6, /device:TPU:0, one launch (start us, length us, event | category | flops | bytes accessed | tf_op | source)
XLA Modules:
  0.0 69.6 jit_solution(4379512493675445749)
XLA Ops:
  1.7 2.6 %invert.1 = f32[264,128]{1,0:T(8,128)S(1)} custom-call(s32[2]{0:T(128)S(1)} %pad_add_fusion.place_ref, f32[256,128]{1,0:T(8,128)S(1)} %copy-done.1, f32[2,128]{1,0:T(2,128)S(1)} %copy-done.2), custom_call_target="tpu_custom_call" | custom-call | flops 3500000000 | bytes 2097152 | tf_op jit(solution)/shard_map/invert/pallas_call | solution.py:349
  4.2 2.1 %collective-permute-start.1 = (f32[264,128]{1,0:T(8,128)S(1)}, f32[264,128]{1,0:T(8,128)S(1)}, u32[]{:S(2)}, u32[]{:S(2)}) collective-permute-start(f32[264,128]{1,0:T(8,128)S(1)} %invert.1), channel_id=1, source_target_pairs={{0,16},{4,20},{8,24},{12,28},{16,0},{20,4},{24,8},{28,12},{1,17},{... | collective-permute-start | bytes 405512 | tf_op jit(solution)/shard_map/ppermute | solution.py:298
  6.3 6.8 %collective-permute-done.1 = f32[264,128]{1,0:T(8,128)S(1)} collective-permute-done((f32[264,128]{1,0:T(8,128)S(1)}, f32[264,128]{1,0:T(8,128)S(1)}, u32[]{:S(2)}, u32[]{:S(2)}) %collective-permute-start.1) | collective-permute-done | bytes 135200 | tf_op jit(solution)/shard_map/ppermute | solution.py:298
  13.6 1.6 %collective-permute-start.8 = (f32[2,264,128]{2,1,0:T(8,128)S(1)}, f32[2,264,128]{2,1,0:T(8,128)S(1)}, u32[]{:S(2)}, u32[]{:S(2)}) collective-permute-start(f32[2,264,128]{2,1,0:T(8,128)S(1)} %pad_maximum_fusion.refs_0_), channel_id=1, source_target_pairs={{0,4},{4,0},{8,12},{12,8},{16,20},{20,16},{24,28},{28,24},{1,5},{5... | collective-permute-start | bytes 811016 | tf_op jit(solution)/shard_map/ppermute | solution.py:302
  15.2 1.5 %collective-permute-start.9 = (f32[2,264,128]{2,1,0:T(8,128)S(1)}, f32[2,264,128]{2,1,0:T(8,128)S(1)}, u32[]{:S(2)}, u32[]{:S(2)}) collective-permute-start(f32[2,264,128]{2,1,0:T(8,128)S(1)} %pad_maximum_fusion.refs_0_), channel_id=1, source_target_pairs={{0,2},{1,3},{2,0},{3,1},{4,6},{5,7},{6,4},{7,5},{8,10},{9,11},{10,... | collective-permute-start | bytes 811016 | tf_op jit(solution)/shard_map/ppermute | solution.py:306
  16.7 2.6 %collective-permute-start.7 = (f32[256,128]{1,0:T(8,128)S(1)}, f32[256,128]{1,0:T(8,128)S(1)}, u32[]{:S(2)}, u32[]{:S(2)}) collective-permute-start(f32[256,128]{1,0:T(8,128)S(1)} %copy-done.3), channel_id=1, source_target_pairs={{0,16},{4,20},{8,24},{12,28},{16,0},{20,4},{24,8},{28,12},{1,17},{... | collective-permute-start | bytes 393224 | tf_op jit(solution)/shard_map/ppermute | solution.py:298
  20.5 2.4 %collective-permute-done.7 = f32[256,128]{1,0:T(8,128)S(1)} collective-permute-done((f32[256,128]{1,0:T(8,128)S(1)}, f32[256,128]{1,0:T(8,128)S(1)}, u32[]{:S(2)}, u32[]{:S(2)}) %collective-permute-start.7) | collective-permute-done | bytes 131104 | tf_op jit(solution)/shard_map/ppermute | solution.py:298
  22.9 2.0 %collective-permute-done.came = f32[4,32,256]{2,1,0:T(8,128)S(1)} collective-permute-done((f32[4,32,256]{2,1,0:T(8,128)S(1)}, f32[4,32,256]{2,1,0:T(8,128)S(1)}, u32[]{:S(2)}, u32[]{:S(2)}) %collective-permute-start) | collective-permute-done | bytes 131104 | tf_op jit(solution)/shard_map/ppermute | solution.py:302
  28.7 2.0 %collective-permute-start.3 = (f32[2,32,256]{2,1,0:T(8,128)S(1)}, f32[2,32,256]{2,1,0:T(8,128)S(1)}, u32[]{:S(2)}, u32[]{:S(2)}) collective-permute-start(f32[2,32,256]{2,1,0:T(8,128)S(1)} %get-tuple-element.40), channel_id=1, source_target_pairs={{0,8},{4,12},{8,0},{12,4},{16,24},{20,28},{24,16},{28,20},{1,9},{5... | collective-permute-start | bytes 196616 | tf_op jit(solution)/shard_map/ppermute | solution.py:298
  30.8 1.8 %collective-permute-start.4 = (f32[2,32,256]{2,1,0:T(8,128)S(1)}, f32[2,32,256]{2,1,0:T(8,128)S(1)}, u32[]{:S(2)}, u32[]{:S(2)}) collective-permute-start(f32[2,32,256]{2,1,0:T(8,128)S(1)} %get-tuple-element.42), channel_id=1, source_target_pairs={{0,16},{4,20},{8,24},{12,28},{16,0},{20,4},{24,8},{28,12},{1,17},{... | collective-permute-start | bytes 196616 | tf_op jit(solution)/shard_map/ppermute | solution.py:298
  32.5 1.8 %collective-permute-done.10.refs_5_ = f32[2,264,128]{2,1,0:T(8,128)S(1)} collective-permute-done((f32[2,264,128]{2,1,0:T(8,128)S(1)}, f32[2,264,128]{2,1,0:T(8,128)S(1)}, u32[]{:S(2)}, u32[]{:S(2)}) %collective-permute-start.10) | collective-permute-done | bytes 270368 | tf_op jit(solution)/shard_map/ppermute | solution.py:315
  34.4 3.0 %collective-permute-start.5 = (f32[2,32,256]{2,1,0:T(8,128)S(1)}, f32[2,32,256]{2,1,0:T(8,128)S(1)}, u32[]{:S(2)}, u32[]{:S(2)}) collective-permute-start(f32[2,32,256]{2,1,0:T(8,128)S(1)} %get-tuple-element.44), channel_id=1, source_target_pairs={{0,24},{4,28},{8,16},{12,20},{16,8},{20,12},{24,0},{28,4},{1,25},{... | collective-permute-start | bytes 196616 | tf_op jit(solution)/shard_map/ppermute | solution.py:298
  37.4 1.9 %collective-permute-done.14.refs_3_ = f32[2,264,128]{2,1,0:T(8,128)S(1)} collective-permute-done((f32[2,264,128]{2,1,0:T(8,128)S(1)}, f32[2,264,128]{2,1,0:T(8,128)S(1)}, u32[]{:S(2)}, u32[]{:S(2)}) %collective-permute-start.14) | collective-permute-done | bytes 270368 | tf_op jit(solution)/shard_map/ppermute | solution.py:306
  39.3 2.2 %collective-permute-start.11 = (f32[2,256,128]{2,1,0:T(8,128)S(1)}, f32[2,256,128]{2,1,0:T(8,128)S(1)}, u32[]{:S(2)}, u32[]{:S(2)}) collective-permute-start(f32[2,256,128]{2,1,0:T(8,128)S(1)} %pad_maximum_fusion.2.refs_0_), channel_id=1, source_target_pairs={{0,8},{4,12},{8,0},{12,4},{16,24},{20,28},{24,16},{28,20},{1,9},{5... | collective-permute-start | bytes 786440 | tf_op jit(solution)/shard_map/ppermute | solution.py:298
  42.6 1.7 %collective-permute-start.6 = (f32[32,1024]{1,0:T(8,128)S(1)}, f32[32,1024]{1,0:T(8,128)S(1)}, u32[]{:S(2)}, u32[]{:S(2)}) collective-permute-start(f32[32,1024]{1,0:T(8,128)S(1)} %get-tuple-element.46), channel_id=1, source_target_pairs={{0,2},{1,3},{2,0},{3,1},{4,6},{5,7},{6,4},{7,5},{8,10},{9,11},{10,... | collective-permute-start | bytes 393224 | tf_op jit(solution)/shard_map/ppermute | solution.py:306
  44.3 1.4 %collective-permute-start.13 = (f32[2,256,128]{2,1,0:T(8,128)S(1)}, f32[2,256,128]{2,1,0:T(8,128)S(1)}, u32[]{:S(2)}, u32[]{:S(2)}) collective-permute-start(f32[2,256,128]{2,1,0:T(8,128)S(1)} %pad_maximum_fusion.2.refs_0_), channel_id=1, source_target_pairs={{0,4},{4,0},{8,12},{12,8},{16,20},{20,16},{24,28},{28,24},{1,5},{5... | collective-permute-start | bytes 786440 | tf_op jit(solution)/shard_map/ppermute | solution.py:302
  45.7 2.0 %collective-permute-done.6 = f32[32,1024]{1,0:T(8,128)S(1)} collective-permute-done((f32[32,1024]{1,0:T(8,128)S(1)}, f32[32,1024]{1,0:T(8,128)S(1)}, u32[]{:S(2)}, u32[]{:S(2)}) %collective-permute-start.6) | collective-permute-done | bytes 131104 | tf_op jit(solution)/shard_map/ppermute | solution.py:306
  48.9 2.8 %collective-permute-done.13.refs_2_ = f32[2,256,128]{2,1,0:T(8,128)S(1)} collective-permute-done((f32[2,256,128]{2,1,0:T(8,128)S(1)}, f32[2,256,128]{2,1,0:T(8,128)S(1)}, u32[]{:S(2)}, u32[]{:S(2)}) %collective-permute-start.13) | collective-permute-done | bytes 262176 | tf_op jit(solution)/shard_map/ppermute | solution.py:302
  54.8 3.6 %first_panel.1.x_ref = f32[128,1024]{1,0:T(8,128)S(1)} custom-call(s32[2]{0:T(128)S(1)} %pad_add_fusion.place_ref, f32[2,32,1024]{2,1,0:T(8,128)S(1)} %pad_maximum_fusion.1.pair, f32[2,32,1024]{2,1,0:T(8,128)S(1)} %collective-permute-done.12.other_pair, f32[2,264,128]{2,1,0:T(8,128)S(1)} %pad_maximum_fusion.refs_0_, ...), custom_call_target="tpu_custom_call" | custom-call | flops 200000000 | bytes 2097152 | tf_op jit(solution)/shard_map/first_panel/pallas_call | solution.py:393
  58.4 2.9 %second_factor.1 = (bf16[1024,1024]{1,0:T(8,128)(2,1)S(1)}, bf16[1024,1024]{1,0:T(8,128)(2,1)S(1)}) custom-call(s32[2]{0:T(128)S(1)} %pad_add_fusion.place_ref, f32[2,264,128]{2,1,0:T(8,128)S(1)} %pad_maximum_fusion.refs_0_, f32[2,264,128]{2,1,0:T(8,128)S(1)} %collective-permute-done.8.refs_1_, f32[2,264,128]{2,1,0:T(8,128)S(1)} %collective-permute-done.9.refs_2_, ...), custom_call_target="tpu_custom_call" | custom-call | flops 3000000000 | bytes 2097152 | tf_op jit(solution)/shard_map/second_factor/pallas_call | solution.py:404
  61.6 1.3 %update.1 = (f32[32,256]{1,0:T(8,128)S(1)}, f32[32,256]{1,0:T(8,128)S(1)}, f32[32,256]{1,0:T(8,128)S(1)}, f32[32,256]{1,0:T(8,128)S(1)}) custom-call(s32[2]{0:T(128)S(1)} %pad_add_fusion.place_ref, f32[128,1024]{1,0:T(8,128)S(1)} %first_panel.1.x_ref, f32[2,256,128]{2,1,0:T(8,128)S(1)} %pad_maximum_fusion.2.refs_0_, ...), custom_call_target="tpu_custom_call" | custom-call | flops 2000000000 | bytes 2097152 | tf_op jit(solution)/shard_map/update/pallas_call | solution.py:408
  62.9 1.3 %collective-permute-start.26 = (f32[32,256]{1,0:T(8,128)S(1)}, f32[32,256]{1,0:T(8,128)S(1)}, u32[]{:S(2)}, u32[]{:S(2)}) collective-permute-start(f32[32,256]{1,0:T(8,128)S(1)} %get-tuple-element.68), channel_id=1, source_target_pairs={{0,2},{1,3},{2,0},{3,1},{4,6},{5,7},{6,4},{7,5},{8,10},{9,11},{10,... | collective-permute-start | bytes 98312 | tf_op jit(solution)/shard_map/ppermute | solution.py:306
  65.1 1.8 %collective-permute-done.26.from_x = f32[32,256]{1,0:T(8,128)S(1)} collective-permute-done((f32[32,256]{1,0:T(8,128)S(1)}, f32[32,256]{1,0:T(8,128)S(1)}, u32[]{:S(2)}, u32[]{:S(2)}) %collective-permute-start.26) | collective-permute-done | bytes 32800 | tf_op jit(solution)/shard_map/ppermute | solution.py:306
  67.5 2.1 %second_panel.1 = f32[32,2048]{1,0:T(8,128)} custom-call(s32[2]{0:T(128)S(1)} %pad_add_fusion.place_ref, f32[128,1024]{1,0:T(8,128)S(1)} %first_panel.1.x_ref, f32[2,32,1024]{2,1,0:T(8,128)S(1)} %get-tuple-element.62.both_ref, bf16[1024,1024]{1,0:T(8,128)(2,1)S(1)} %get-tuple-element.64.uh_ref, bf16[1024,1024]{1,0:T(8,128)(2,1)S(1)} %get-tuple-element.65.ul_ref, ...), custom_call_target="tpu_custom_call" | custom-call | flops 2500000000 | bytes 2097152 | tf_op jit(solution)/shard_map/second_panel/pallas_call | solution.py:420
  (54 shorter events, 14.5 us)
Async XLA Ops:
  4.2 8.9 %collective-permute-start.1 = (f32[264,128]{1,0:T(8,128)S(1)}, f32[264,128]{1,0:T(8,128)S(1)}, u32[]{:S(2)}, u32[]{:S(2)}) collective-permute-start(f32[264,128]{1,0:T(8,128)S(1)} %invert.1), channel_id=1, source_target_pairs={{0,16},{4,20},{8,24},{12,28},{16,0},{20,4},{24,8},{28,12},{1,17},{... | collective-permute-start | bytes 405512 | tf_op jit(solution)/shard_map/ppermute | solution.py:298
  13.1 11.9 %collective-permute-start.2 = (f32[2,264,128]{2,1,0:T(8,128)S(1)}, f32[2,264,128]{2,1,0:T(8,128)S(1)}, u32[]{:S(2)}, u32[]{:S(2)}) collective-permute-start(f32[2,264,128]{2,1,0:T(8,128)S(1)} %pad_maximum_fusion.refs_0_), channel_id=1, source_target_pairs={{0,8},{4,12},{8,0},{12,4},{16,24},{20,28},{24,16},{28,20},{1,9},{5... | collective-permute-start | bytes 811016 | tf_op jit(solution)/shard_map/ppermute | solution.py:298
  13.6 11.4 %collective-permute-start.8 = (f32[2,264,128]{2,1,0:T(8,128)S(1)}, f32[2,264,128]{2,1,0:T(8,128)S(1)}, u32[]{:S(2)}, u32[]{:S(2)}) collective-permute-start(f32[2,264,128]{2,1,0:T(8,128)S(1)} %pad_maximum_fusion.refs_0_), channel_id=1, source_target_pairs={{0,4},{4,0},{8,12},{12,8},{16,20},{20,16},{24,28},{28,24},{1,5},{5... | collective-permute-start | bytes 811016 | tf_op jit(solution)/shard_map/ppermute | solution.py:302
  15.2 9.7 %collective-permute-start.9 = (f32[2,264,128]{2,1,0:T(8,128)S(1)}, f32[2,264,128]{2,1,0:T(8,128)S(1)}, u32[]{:S(2)}, u32[]{:S(2)}) collective-permute-start(f32[2,264,128]{2,1,0:T(8,128)S(1)} %pad_maximum_fusion.refs_0_), channel_id=1, source_target_pairs={{0,2},{1,3},{2,0},{3,1},{4,6},{5,7},{6,4},{7,5},{8,10},{9,11},{10,... | collective-permute-start | bytes 811016 | tf_op jit(solution)/shard_map/ppermute | solution.py:306
  16.7 6.2 %collective-permute-start.7 = (f32[256,128]{1,0:T(8,128)S(1)}, f32[256,128]{1,0:T(8,128)S(1)}, u32[]{:S(2)}, u32[]{:S(2)}) collective-permute-start(f32[256,128]{1,0:T(8,128)S(1)} %copy-done.3), channel_id=1, source_target_pairs={{0,16},{4,20},{8,24},{12,28},{16,0},{20,4},{24,8},{28,12},{1,17},{... | collective-permute-start | bytes 393224 | tf_op jit(solution)/shard_map/ppermute | solution.py:298
  19.9 5.0 %collective-permute-start = (f32[4,32,256]{2,1,0:T(8,128)S(1)}, f32[4,32,256]{2,1,0:T(8,128)S(1)}, u32[]{:S(2)}, u32[]{:S(2)}) collective-permute-start(f32[4,32,256]{2,1,0:T(8,128)S(1)} %leave.1), channel_id=1, source_target_pairs={{0,4},{4,0},{8,12},{12,8},{16,20},{20,16},{24,28},{28,24},{1,5},{5... | collective-permute-start | bytes 393224 | tf_op jit(solution)/shard_map/ppermute | solution.py:302
  25.0 9.4 %collective-permute-start.10 = (f32[2,264,128]{2,1,0:T(8,128)S(1)}, f32[2,264,128]{2,1,0:T(8,128)S(1)}, u32[]{:S(2)}, u32[]{:S(2)}) collective-permute-start(f32[2,264,128]{2,1,0:T(8,128)S(1)} %collective-permute-done.2.refs_4_), channel_id=1, source_target_pairs={{0,2},{4,6},{8,10},{12,14},{16,18},{20,22},{24,26},{28,30},{1,5},{... | collective-permute-start | bytes 811016 | tf_op jit(solution)/shard_map/ppermute | solution.py:315
  26.2 13.1 %collective-permute-start.14 = (f32[2,264,128]{2,1,0:T(8,128)S(1)}, f32[2,264,128]{2,1,0:T(8,128)S(1)}, u32[]{:S(2)}, u32[]{:S(2)}) collective-permute-start(f32[2,264,128]{2,1,0:T(8,128)S(1)} %collective-permute-done.8.refs_1_), channel_id=1, source_target_pairs={{0,2},{1,3},{2,0},{3,1},{4,6},{5,7},{6,4},{7,5},{8,10},{9,11},{10,... | collective-permute-start | bytes 811016 | tf_op jit(solution)/shard_map/ppermute | solution.py:306
  27.1 14.4 %collective-permute-start.15 = (f32[2,264,128]{2,1,0:T(8,128)S(1)}, f32[2,264,128]{2,1,0:T(8,128)S(1)}, u32[]{:S(2)}, u32[]{:S(2)}) collective-permute-start(f32[2,264,128]{2,1,0:T(8,128)S(1)} %collective-permute-done.2.refs_4_), channel_id=1, source_target_pairs={{0,4},{4,0},{8,12},{12,8},{16,20},{20,16},{24,28},{28,24},{1,3},{5... | collective-permute-start | bytes 811016 | tf_op jit(solution)/shard_map/ppermute | solution.py:315
  28.7 13.3 %collective-permute-start.3 = (f32[2,32,256]{2,1,0:T(8,128)S(1)}, f32[2,32,256]{2,1,0:T(8,128)S(1)}, u32[]{:S(2)}, u32[]{:S(2)}) collective-permute-start(f32[2,32,256]{2,1,0:T(8,128)S(1)} %get-tuple-element.40), channel_id=1, source_target_pairs={{0,8},{4,12},{8,0},{12,4},{16,24},{20,28},{24,16},{28,20},{1,9},{5... | collective-permute-start | bytes 196616 | tf_op jit(solution)/shard_map/ppermute | solution.py:298
  30.8 11.2 %collective-permute-start.4 = (f32[2,32,256]{2,1,0:T(8,128)S(1)}, f32[2,32,256]{2,1,0:T(8,128)S(1)}, u32[]{:S(2)}, u32[]{:S(2)}) collective-permute-start(f32[2,32,256]{2,1,0:T(8,128)S(1)} %get-tuple-element.42), channel_id=1, source_target_pairs={{0,16},{4,20},{8,24},{12,28},{16,0},{20,4},{24,8},{28,12},{1,17},{... | collective-permute-start | bytes 196616 | tf_op jit(solution)/shard_map/ppermute | solution.py:298
  34.4 7.6 %collective-permute-start.5 = (f32[2,32,256]{2,1,0:T(8,128)S(1)}, f32[2,32,256]{2,1,0:T(8,128)S(1)}, u32[]{:S(2)}, u32[]{:S(2)}) collective-permute-start(f32[2,32,256]{2,1,0:T(8,128)S(1)} %get-tuple-element.44), channel_id=1, source_target_pairs={{0,24},{4,28},{8,16},{12,20},{16,8},{20,12},{24,0},{28,4},{1,25},{... | collective-permute-start | bytes 196616 | tf_op jit(solution)/shard_map/ppermute | solution.py:298
  39.3 8.4 %collective-permute-start.11 = (f32[2,256,128]{2,1,0:T(8,128)S(1)}, f32[2,256,128]{2,1,0:T(8,128)S(1)}, u32[]{:S(2)}, u32[]{:S(2)}) collective-permute-start(f32[2,256,128]{2,1,0:T(8,128)S(1)} %pad_maximum_fusion.2.refs_0_), channel_id=1, source_target_pairs={{0,8},{4,12},{8,0},{12,4},{16,24},{20,28},{24,16},{28,20},{1,9},{5... | collective-permute-start | bytes 786440 | tf_op jit(solution)/shard_map/ppermute | solution.py:298
  41.5 7.4 %collective-permute-start.16 = (f32[2,264,128]{2,1,0:T(8,128)S(1)}, f32[2,264,128]{2,1,0:T(8,128)S(1)}, u32[]{:S(2)}, u32[]{:S(2)}) collective-permute-start(f32[2,264,128]{2,1,0:T(8,128)S(1)} %collective-permute-done.10.refs_5_), channel_id=1, source_target_pairs={{0,4},{4,0},{8,12},{12,8},{16,20},{20,16},{24,28},{28,24},{1,3},{5... | collective-permute-start | bytes 811016 | tf_op jit(solution)/shard_map/ppermute | solution.py:315
  42.6 5.0 %collective-permute-start.6 = (f32[32,1024]{1,0:T(8,128)S(1)}, f32[32,1024]{1,0:T(8,128)S(1)}, u32[]{:S(2)}, u32[]{:S(2)}) collective-permute-start(f32[32,1024]{1,0:T(8,128)S(1)} %get-tuple-element.46), channel_id=1, source_target_pairs={{0,2},{1,3},{2,0},{3,1},{4,6},{5,7},{6,4},{7,5},{8,10},{9,11},{10,... | collective-permute-start | bytes 393224 | tf_op jit(solution)/shard_map/ppermute | solution.py:306
  44.3 7.5 %collective-permute-start.13 = (f32[2,256,128]{2,1,0:T(8,128)S(1)}, f32[2,256,128]{2,1,0:T(8,128)S(1)}, u32[]{:S(2)}, u32[]{:S(2)}) collective-permute-start(f32[2,256,128]{2,1,0:T(8,128)S(1)} %pad_maximum_fusion.2.refs_0_), channel_id=1, source_target_pairs={{0,4},{4,0},{8,12},{12,8},{16,20},{20,16},{24,28},{28,24},{1,5},{5... | collective-permute-start | bytes 786440 | tf_op jit(solution)/shard_map/ppermute | solution.py:302
  45.7 6.1 %collective-permute-start.17 = (f32[2,264,128]{2,1,0:T(8,128)S(1)}, f32[2,264,128]{2,1,0:T(8,128)S(1)}, u32[]{:S(2)}, u32[]{:S(2)}) collective-permute-start(f32[2,264,128]{2,1,0:T(8,128)S(1)} %pad_maximum_fusion.refs_0_), channel_id=1, source_target_pairs={{0,1},{1,0},{2,3},{3,2},{4,5},{5,4},{6,7},{7,6},{8,9},{9,8},{10,11... | collective-permute-start | bytes 811016 | tf_op jit(solution)/shard_map/ppermute | solution.py:306
  47.7 4.6 %collective-permute-start.18 = (f32[2,264,128]{2,1,0:T(8,128)S(1)}, f32[2,264,128]{2,1,0:T(8,128)S(1)}, u32[]{:S(2)}, u32[]{:S(2)}) collective-permute-start(f32[2,264,128]{2,1,0:T(8,128)S(1)} %collective-permute-done.8.refs_1_), channel_id=1, source_target_pairs={{0,1},{1,0},{2,3},{3,2},{4,5},{5,4},{6,7},{7,6},{8,9},{9,8},{10,11... | collective-permute-start | bytes 811016 | tf_op jit(solution)/shard_map/ppermute | solution.py:306
  47.7 4.7 %collective-permute-start.19 = (f32[2,264,128]{2,1,0:T(8,128)S(1)}, f32[2,264,128]{2,1,0:T(8,128)S(1)}, u32[]{:S(2)}, u32[]{:S(2)}) collective-permute-start(f32[2,264,128]{2,1,0:T(8,128)S(1)} %collective-permute-done.9.refs_2_), channel_id=1, source_target_pairs={{0,1},{1,0},{2,3},{3,2},{4,5},{5,4},{6,7},{7,6},{8,9},{9,8},{10,11... | collective-permute-start | bytes 811016 | tf_op jit(solution)/shard_map/ppermute | solution.py:306
  48.9 3.8 %collective-permute-start.12 = (f32[2,32,1024]{2,1,0:T(8,128)S(1)}, f32[2,32,1024]{2,1,0:T(8,128)S(1)}, u32[]{:S(2)}, u32[]{:S(2)}) collective-permute-start(f32[2,32,1024]{2,1,0:T(8,128)S(1)} %pad_maximum_fusion.1.pair), channel_id=1, source_target_pairs={{0,1},{1,0},{2,3},{3,2},{4,5},{5,4},{6,7},{7,6},{8,9},{9,8},{10,11... | collective-permute-start | bytes 786440 | tf_op jit(solution)/shard_map/ppermute | solution.py:306
  53.3 8.3 %collective-permute-start.25 = (f32[2,256,128]{2,1,0:T(8,128)S(1)}, f32[2,256,128]{2,1,0:T(8,128)S(1)}, u32[]{:S(2)}, u32[]{:S(2)}) collective-permute-start(f32[2,256,128]{2,1,0:T(8,128)S(1)} %collective-permute-done.11.refs_1_), channel_id=1, source_target_pairs={{0,4},{4,0},{8,12},{12,8},{16,20},{20,16},{24,28},{28,24},{1,5},{5... | collective-permute-start | bytes 786440 | tf_op jit(solution)/shard_map/ppermute | solution.py:302
  62.9 4.0 %collective-permute-start.26 = (f32[32,256]{1,0:T(8,128)S(1)}, f32[32,256]{1,0:T(8,128)S(1)}, u32[]{:S(2)}, u32[]{:S(2)}) collective-permute-start(f32[32,256]{1,0:T(8,128)S(1)} %get-tuple-element.68), channel_id=1, source_target_pairs={{0,2},{1,3},{2,0},{3,1},{4,6},{5,7},{6,4},{7,5},{8,10},{9,11},{10,... | collective-permute-start | bytes 98312 | tf_op jit(solution)/shard_map/ppermute | solution.py:306
  64.2 2.7 %collective-permute-start.27 = (f32[32,256]{1,0:T(8,128)S(1)}, f32[32,256]{1,0:T(8,128)S(1)}, u32[]{:S(2)}, u32[]{:S(2)}) collective-permute-start(f32[32,256]{1,0:T(8,128)S(1)} %get-tuple-element.69), channel_id=1, source_target_pairs={{0,1},{1,0},{2,3},{3,2},{4,5},{5,4},{6,7},{7,6},{8,9},{9,8},{10,11... | collective-permute-start | bytes 98312 | tf_op jit(solution)/shard_map/ppermute | solution.py:306
  64.2 3.3 %collective-permute-start.28 = (f32[32,256]{1,0:T(8,128)S(1)}, f32[32,256]{1,0:T(8,128)S(1)}, u32[]{:S(2)}, u32[]{:S(2)}) collective-permute-start(f32[32,256]{1,0:T(8,128)S(1)} %get-tuple-element.70), channel_id=1, source_target_pairs={{0,3},{1,2},{2,1},{3,0},{4,7},{5,6},{6,5},{7,4},{8,11},{9,10},{10,... | collective-permute-start | bytes 98312 | tf_op jit(solution)/shard_map/ppermute | solution.py:306
  (9 other events, 43.8 us)

commit v7 on v4

--- a/solution.py
+++ b/solution.py
@@ -362,13 +362,13 @@
     c_near = jnp.stack([coupling, swap_z(after(coup, near), 2)])
     c_near_got = swap_y(c_near)
 
-    far_now = after(far, near0, near1, came, c_near)
+    far_now = after(far, near0, near1, came)
     far0 = cross(far_now, 0)
     far1 = cross(far_now, 1)
     b_out = call(spread_kernel, [shape(2, 32, 256)] * 3, [SMEM, VMEM, VMEM], [VMEM] * 3, [], SPREAD, 4, "spread")(
         place, blocks, came
     )
-    b_z = [swap_z(after(b, far), m + 1) for m, b in enumerate(b_out)]
+    b_z = [swap_z(after(b, far, *((near01, c_near) if m == 2 else ())), m + 1) for m, b in enumerate(b_out)]
     c_far = swap_z(after(c_near, far0), 1)
     c_far_got = swap_y(c_far)
     far01 = cross(after(far0, far1, near01), 1)

time: 63.7 us -> 64.9 us (1.019)
  waiting for transfers between devices: 18.3 us -> 24.7 us
  starting transfers between devices: 29.3 us -> 24.2 us
    ppermute x7, starting transfers between devices: 13.9 us -> 7.45 us  [swap_z(): return lax.ppermute(x, 'bulk', [(k, k ^ 2 * m) for k in range(8)])]
    ppermute x4, waiting for transfers between devices: 3.2 us -> 5.97 us  [swap_y(): return lax.ppermute(x, 'bulk', [(k, k ^ 1) for k in range(8)])]
    ppermute x7, waiting for transfers between devices: 10.7 us -> 13.4 us  [swap_z(): return lax.ppermute(x, 'bulk', [(k, k ^ 2 * m) for k in range(8)])]
    ppermute x15, waiting for transfers between devices: 3.97 us -> 5.34 us  [swap_rep(): return lax.ppermute(x, 'rep', [(k, k ^ bits) for k in range(4)])]
    ppermute x15, starting transfers between devices: 8.21 us -> 9.15 us  [swap_rep(): return lax.ppermute(x, 'rep', [(k, k ^ bits) for k in range(4)])]
  transfers between devices with their start and end apart: 29 -> 29, of which waited for: 9 -> 12; matrix products, arithmetic and copies ran while one was open for 0% -> 0% of each run, Pallas kernels for 13% -> 13%
where the time goes in v7:
time: 64.9 us; the launch traced here: 64.8 us
  waiting for transfers between devices  24.7 us (38%)
  starting transfers between devices  24.2 us (37%)
  Pallas kernels  14 us (22%)
  local copies, waits for them, and re-layouts  1.59 us (2%)
    ppermute x7, waiting for transfers between devices, swap_z(): return lax.ppermute(x, 'bulk', [(k, k ^ 2 * m) for k in range(8)])  13.4 us
    ppermute x15, starting transfers between devices, swap_rep(): return lax.ppermute(x, 'rep', [(k, k ^ bits) for k in range(4)])  9.15 us
    ppermute x7, starting transfers between devices, swap_z(): return lax.ppermute(x, 'bulk', [(k, k ^ 2 * m) for k in range(8)])  7.45 us
    ppermute x4, waiting for transfers between devices, swap_y(): return lax.ppermute(x, 'bulk', [(k, k ^ 1) for k in range(8)])  5.97 us
    ppermute x4, starting transfers between devices, swap_y(): return lax.ppermute(x, 'bulk', [(k, k ^ 1) for k in range(8)])  5.58 us
    ppermute x15, waiting for transfers between devices, swap_rep(): return lax.ppermute(x, 'rep', [(k, k ^ bits) for k in range(4)])  5.34 us
    pallas_call x1, Pallas kernels, per_device(): call(first_kernel, shape(128, 1024), [SMEM] + [VMEM] * 18, VMEM, [pltpu.V...  3.58 us
    pallas_call x1, Pallas kernels, per_device(): call(second_factor_kernel, halves, [SMEM] + [VMEM] * 16, [VMEM] * 2, scra...  2.87 us
  transfers between devices with their start and end apart: 29, of which 12 were waited for; matrix products, arithmetic and copies ran while one was open for 0% of the time, Pallas kernels for 13%

profile of v7, /device:TPU:0, one launch (start us, length us, event | category | flops | bytes accessed | tf_op | source)
XLA Modules:
  0.0 64.8 jit_solution(17620636126632400219)
XLA Ops:
  1.7 2.6 %invert.1 = f32[264,128]{1,0:T(8,128)S(1)} custom-call(s32[2]{0:T(128)S(1)} %pad_add_fusion.place_ref, f32[256,128]{1,0:T(8,128)S(1)} %copy-done.1, f32[2,128]{1,0:T(2,128)S(1)} %copy-done.2), custom_call_target="tpu_custom_call" | custom-call | flops 3500000000 | bytes 2097152 | tf_op jit(solution)/shard_map/invert/pallas_call | solution.py:349
  4.2 2.1 %collective-permute-start.1 = (f32[264,128]{1,0:T(8,128)S(1)}, f32[264,128]{1,0:T(8,128)S(1)}, u32[]{:S(2)}, u32[]{:S(2)}) collective-permute-start(f32[264,128]{1,0:T(8,128)S(1)} %invert.1), channel_id=1, source_target_pairs={{0,16},{4,20},{8,24},{12,28},{16,0},{20,4},{24,8},{28,12},{1,17},{... | collective-permute-start | bytes 405512 | tf_op jit(solution)/shard_map/ppermute | solution.py:298
  6.3 6.8 %collective-permute-done.1 = f32[264,128]{1,0:T(8,128)S(1)} collective-permute-done((f32[264,128]{1,0:T(8,128)S(1)}, f32[264,128]{1,0:T(8,128)S(1)}, u32[]{:S(2)}, u32[]{:S(2)}) %collective-permute-start.1) | collective-permute-done | bytes 135200 | tf_op jit(solution)/shard_map/ppermute | solution.py:298
  13.1 2.0 %collective-permute-start.5 = (f32[2,264,128]{2,1,0:T(8,128)S(1)}, f32[2,264,128]{2,1,0:T(8,128)S(1)}, u32[]{:S(2)}, u32[]{:S(2)}) collective-permute-start(f32[2,264,128]{2,1,0:T(8,128)S(1)} %pad_maximum_fusion.refs_0_), channel_id=1, source_target_pairs={{0,4},{4,0},{8,12},{12,8},{16,20},{20,16},{24,28},{28,24},{1,5},{5... | collective-permute-start | bytes 811016 | tf_op jit(solution)/shard_map/ppermute | solution.py:302
  15.2 1.5 %collective-permute-start.10 = (f32[2,264,128]{2,1,0:T(8,128)S(1)}, f32[2,264,128]{2,1,0:T(8,128)S(1)}, u32[]{:S(2)}, u32[]{:S(2)}) collective-permute-start(f32[2,264,128]{2,1,0:T(8,128)S(1)} %pad_maximum_fusion.refs_0_), channel_id=1, source_target_pairs={{0,2},{1,3},{2,0},{3,1},{4,6},{5,7},{6,4},{7,5},{8,10},{9,11},{10,... | collective-permute-start | bytes 811016 | tf_op jit(solution)/shard_map/ppermute | solution.py:306
  17.8 2.8 %collective-permute-done.5.refs_1_ = f32[2,264,128]{2,1,0:T(8,128)S(1)} collective-permute-done((f32[2,264,128]{2,1,0:T(8,128)S(1)}, f32[2,264,128]{2,1,0:T(8,128)S(1)}, u32[]{:S(2)}, u32[]{:S(2)}) %collective-permute-start.5) | collective-permute-done | bytes 270368 | tf_op jit(solution)/shard_map/ppermute | solution.py:302
  20.6 2.5 %collective-permute-start.6 = (f32[2,264,128]{2,1,0:T(8,128)S(1)}, f32[2,264,128]{2,1,0:T(8,128)S(1)}, u32[]{:S(2)}, u32[]{:S(2)}) collective-permute-start(f32[2,264,128]{2,1,0:T(8,128)S(1)} %collective-permute-done.5.refs_1_), channel_id=1, source_target_pairs={{0,2},{1,3},{2,0},{3,1},{4,6},{5,7},{6,4},{7,5},{8,10},{9,11},{10,... | collective-permute-start | bytes 811016 | tf_op jit(solution)/shard_map/ppermute | solution.py:306
  23.0 0.9 %collective-permute-done.10.refs_2_ = f32[2,264,128]{2,1,0:T(8,128)S(1)} collective-permute-done((f32[2,264,128]{2,1,0:T(8,128)S(1)}, f32[2,264,128]{2,1,0:T(8,128)S(1)}, u32[]{:S(2)}, u32[]{:S(2)}) %collective-permute-start.10) | collective-permute-done | bytes 270368 | tf_op jit(solution)/shard_map/ppermute | solution.py:306
  24.5 1.4 %collective-permute-start.11 = (f32[2,264,128]{2,1,0:T(8,128)S(1)}, f32[2,264,128]{2,1,0:T(8,128)S(1)}, u32[]{:S(2)}, u32[]{:S(2)}) collective-permute-start(f32[2,264,128]{2,1,0:T(8,128)S(1)} %collective-permute-done.2.refs_4_), channel_id=1, source_target_pairs={{0,2},{4,6},{8,10},{12,14},{16,18},{20,22},{24,26},{28,30},{1,5},{... | collective-permute-start | bytes 811016 | tf_op jit(solution)/shard_map/ppermute | solution.py:315
  26.6 4.1 %collective-permute-done.7 = f32[256,128]{1,0:T(8,128)S(1)} collective-permute-done((f32[256,128]{1,0:T(8,128)S(1)}, f32[256,128]{1,0:T(8,128)S(1)}, u32[]{:S(2)}, u32[]{:S(2)}) %collective-permute-start.7) | collective-permute-done | bytes 131104 | tf_op jit(solution)/shard_map/ppermute | solution.py:298
  30.8 2.4 %collective-permute-start.4 = (f32[2,32,256]{2,1,0:T(8,128)S(1)}, f32[2,32,256]{2,1,0:T(8,128)S(1)}, u32[]{:S(2)}, u32[]{:S(2)}) collective-permute-start(f32[2,32,256]{2,1,0:T(8,128)S(1)} %get-tuple-element.41), channel_id=1, source_target_pairs={{0,16},{4,20},{8,24},{12,28},{16,0},{20,4},{24,8},{28,12},{1,17},{... | collective-permute-start | bytes 196616 | tf_op jit(solution)/shard_map/ppermute | solution.py:298
  33.2 1.9 %collective-permute-start.8 = (f32[2,32,256]{2,1,0:T(8,128)S(1)}, f32[2,32,256]{2,1,0:T(8,128)S(1)}, u32[]{:S(2)}, u32[]{:S(2)}) collective-permute-start(f32[2,32,256]{2,1,0:T(8,128)S(1)} %get-tuple-element.45), channel_id=1, source_target_pairs={{0,24},{4,28},{8,16},{12,20},{16,8},{20,12},{24,0},{28,4},{1,25},{... | collective-permute-start | bytes 196616 | tf_op jit(solution)/shard_map/ppermute | solution.py:298
  35.2 1.5 %collective-permute-start.14 = (f32[2,256,128]{2,1,0:T(8,128)S(1)}, f32[2,256,128]{2,1,0:T(8,128)S(1)}, u32[]{:S(2)}, u32[]{:S(2)}) collective-permute-start(f32[2,256,128]{2,1,0:T(8,128)S(1)} %pad_maximum_fusion.1.refs_0_), channel_id=1, source_target_pairs={{0,4},{4,0},{8,12},{12,8},{16,20},{20,16},{24,28},{28,24},{1,5},{5... | collective-permute-start | bytes 786440 | tf_op jit(solution)/shard_map/ppermute | solution.py:302
  38.1 1.9 %collective-permute-done.8.b3 = f32[2,32,256]{2,1,0:T(8,128)S(1)} collective-permute-done((f32[2,32,256]{2,1,0:T(8,128)S(1)}, f32[2,32,256]{2,1,0:T(8,128)S(1)}, u32[]{:S(2)}, u32[]{:S(2)}) %collective-permute-start.8) | collective-permute-done | bytes 65568 | tf_op jit(solution)/shard_map/ppermute | solution.py:298
  40.6 1.1 %collective-permute-start.9 = (f32[32,1024]{1,0:T(8,128)S(1)}, f32[32,1024]{1,0:T(8,128)S(1)}, u32[]{:S(2)}, u32[]{:S(2)}) collective-permute-start(f32[32,1024]{1,0:T(8,128)S(1)} %get-tuple-element.47), channel_id=1, source_target_pairs={{0,2},{1,3},{2,0},{3,1},{4,6},{5,7},{6,4},{7,5},{8,10},{9,11},{10,... | collective-permute-start | bytes 393224 | tf_op jit(solution)/shard_map/ppermute | solution.py:306
  42.2 3.5 %collective-permute-done.9 = f32[32,1024]{1,0:T(8,128)S(1)} collective-permute-done((f32[32,1024]{1,0:T(8,128)S(1)}, f32[32,1024]{1,0:T(8,128)S(1)}, u32[]{:S(2)}, u32[]{:S(2)}) %collective-permute-start.9) | collective-permute-done | bytes 131104 | tf_op jit(solution)/shard_map/ppermute | solution.py:306
  48.0 1.4 %collective-permute-start.25 = (f32[2,256,128]{2,1,0:T(8,128)S(1)}, f32[2,256,128]{2,1,0:T(8,128)S(1)}, u32[]{:S(2)}, u32[]{:S(2)}) collective-permute-start(f32[2,256,128]{2,1,0:T(8,128)S(1)} %collective-permute-done.12.refs_1_), channel_id=1, source_target_pairs={{0,4},{4,0},{8,12},{12,8},{16,20},{20,16},{24,28},{28,24},{1,5},{5... | collective-permute-start | bytes 786440 | tf_op jit(solution)/shard_map/ppermute | solution.py:302
  49.5 3.6 %first_panel.1.x_ref = f32[128,1024]{1,0:T(8,128)S(1)} custom-call(s32[2]{0:T(128)S(1)} %pad_add_fusion.place_ref, f32[2,32,1024]{2,1,0:T(8,128)S(1)} %pad_maximum_fusion.2.pair, f32[2,32,1024]{2,1,0:T(8,128)S(1)} %collective-permute-done.13.other_pair, f32[2,264,128]{2,1,0:T(8,128)S(1)} %pad_maximum_fusion.refs_0_, ...), custom_call_target="tpu_custom_call" | custom-call | flops 200000000 | bytes 2097152 | tf_op jit(solution)/shard_map/first_panel/pallas_call | solution.py:393
  53.1 3.2 %collective-permute-done.25.refs_3_ = f32[2,256,128]{2,1,0:T(8,128)S(1)} collective-permute-done((f32[2,256,128]{2,1,0:T(8,128)S(1)}, f32[2,256,128]{2,1,0:T(8,128)S(1)}, u32[]{:S(2)}, u32[]{:S(2)}) %collective-permute-start.25) | collective-permute-done | bytes 262176 | tf_op jit(solution)/shard_map/ppermute | solution.py:302
  56.3 1.3 %update.1 = (f32[32,256]{1,0:T(8,128)S(1)}, f32[32,256]{1,0:T(8,128)S(1)}, f32[32,256]{1,0:T(8,128)S(1)}, f32[32,256]{1,0:T(8,128)S(1)}) custom-call(s32[2]{0:T(128)S(1)} %pad_add_fusion.place_ref, f32[128,1024]{1,0:T(8,128)S(1)} %first_panel.1.x_ref, f32[2,256,128]{2,1,0:T(8,128)S(1)} %pad_maximum_fusion.1.refs_0_, ...), custom_call_target="tpu_custom_call" | custom-call | flops 2000000000 | bytes 2097152 | tf_op jit(solution)/shard_map/update/pallas_call | solution.py:404
  57.6 1.1 %collective-permute-start.26 = (f32[32,256]{1,0:T(8,128)S(1)}, f32[32,256]{1,0:T(8,128)S(1)}, u32[]{:S(2)}, u32[]{:S(2)}) collective-permute-start(f32[32,256]{1,0:T(8,128)S(1)} %get-tuple-element.66), channel_id=1, source_target_pairs={{0,2},{1,3},{2,0},{3,1},{4,6},{5,7},{6,4},{7,5},{8,10},{9,11},{10,... | collective-permute-start | bytes 98312 | tf_op jit(solution)/shard_map/ppermute | solution.py:306
  58.7 1.1 %collective-permute-start.28 = (f32[32,256]{1,0:T(8,128)S(1)}, f32[32,256]{1,0:T(8,128)S(1)}, u32[]{:S(2)}, u32[]{:S(2)}) collective-permute-start(f32[32,256]{1,0:T(8,128)S(1)} %get-tuple-element.68), channel_id=1, source_target_pairs={{0,3},{1,2},{2,1},{3,0},{4,7},{5,6},{6,5},{7,4},{8,11},{9,10},{10,... | collective-permute-start | bytes 98312 | tf_op jit(solution)/shard_map/ppermute | solution.py:306
  59.8 2.9 %second_factor.1 = (bf16[1024,1024]{1,0:T(8,128)(2,1)S(1)}, bf16[1024,1024]{1,0:T(8,128)(2,1)S(1)}) custom-call(s32[2]{0:T(128)S(1)} %pad_add_fusion.place_ref, f32[2,264,128]{2,1,0:T(8,128)S(1)} %pad_maximum_fusion.refs_0_, f32[2,264,128]{2,1,0:T(8,128)S(1)} %collective-permute-done.5.refs_1_, f32[2,264,128]{2,1,0:T(8,128)S(1)} %collective-permute-done.10.refs_2_, ...), custom_call_target="tpu_custom_call" | custom-call | flops 3000000000 | bytes 2097152 | tf_op jit(solution)/shard_map/second_factor/pallas_call | solution.py:416
  62.7 2.1 %second_panel.1 = f32[32,2048]{1,0:T(8,128)} custom-call(s32[2]{0:T(128)S(1)} %pad_add_fusion.place_ref, f32[128,1024]{1,0:T(8,128)S(1)} %first_panel.1.x_ref, f32[2,32,1024]{2,1,0:T(8,128)S(1)} %get-tuple-element.61.both_ref, bf16[1024,1024]{1,0:T(8,128)(2,1)S(1)} %get-tuple-element.64.uh_ref, bf16[1024,1024]{1,0:T(8,128)(2,1)S(1)} %get-tuple-element.65.ul_ref, ...), custom_call_target="tpu_custom_call" | custom-call | flops 2500000000 | bytes 2097152 | tf_op jit(solution)/shard_map/second_panel/pallas_call | solution.py:420
  (54 shorter events, 9.0 us)
Async XLA Ops:
  4.2 8.9 %collective-permute-start.1 = (f32[264,128]{1,0:T(8,128)S(1)}, f32[264,128]{1,0:T(8,128)S(1)}, u32[]{:S(2)}, u32[]{:S(2)}) collective-permute-start(f32[264,128]{1,0:T(8,128)S(1)} %invert.1), channel_id=1, source_target_pairs={{0,16},{4,20},{8,24},{12,28},{16,0},{20,4},{24,8},{28,12},{1,17},{... | collective-permute-start | bytes 405512 | tf_op jit(solution)/shard_map/ppermute | solution.py:298
  13.1 7.4 %collective-permute-start.5 = (f32[2,264,128]{2,1,0:T(8,128)S(1)}, f32[2,264,128]{2,1,0:T(8,128)S(1)}, u32[]{:S(2)}, u32[]{:S(2)}) collective-permute-start(f32[2,264,128]{2,1,0:T(8,128)S(1)} %pad_maximum_fusion.refs_0_), channel_id=1, source_target_pairs={{0,4},{4,0},{8,12},{12,8},{16,20},{20,16},{24,28},{28,24},{1,5},{5... | collective-permute-start | bytes 811016 | tf_op jit(solution)/shard_map/ppermute | solution.py:302
  15.2 8.8 %collective-permute-start.10 = (f32[2,264,128]{2,1,0:T(8,128)S(1)}, f32[2,264,128]{2,1,0:T(8,128)S(1)}, u32[]{:S(2)}, u32[]{:S(2)}) collective-permute-start(f32[2,264,128]{2,1,0:T(8,128)S(1)} %pad_maximum_fusion.refs_0_), channel_id=1, source_target_pairs={{0,2},{1,3},{2,0},{3,1},{4,6},{5,7},{6,4},{7,5},{8,10},{9,11},{10,... | collective-permute-start | bytes 811016 | tf_op jit(solution)/shard_map/ppermute | solution.py:306
  16.7 7.9 %collective-permute-start.2 = (f32[2,264,128]{2,1,0:T(8,128)S(1)}, f32[2,264,128]{2,1,0:T(8,128)S(1)}, u32[]{:S(2)}, u32[]{:S(2)}) collective-permute-start(f32[2,264,128]{2,1,0:T(8,128)S(1)} %pad_maximum_fusion.refs_0_), channel_id=1, source_target_pairs={{0,8},{4,12},{8,0},{12,4},{16,24},{20,28},{24,16},{28,20},{1,9},{5... | collective-permute-start | bytes 811016 | tf_op jit(solution)/shard_map/ppermute | solution.py:298
  17.2 5.8 %collective-permute-start = (f32[4,32,256]{2,1,0:T(8,128)S(1)}, f32[4,32,256]{2,1,0:T(8,128)S(1)}, u32[]{:S(2)}, u32[]{:S(2)}) collective-permute-start(f32[4,32,256]{2,1,0:T(8,128)S(1)} %leave.1), channel_id=1, source_target_pairs={{0,4},{4,0},{8,12},{12,8},{16,20},{20,16},{24,28},{28,24},{1,5},{5... | collective-permute-start | bytes 393224 | tf_op jit(solution)/shard_map/ppermute | solution.py:302
  20.6 12.7 %collective-permute-start.6 = (f32[2,264,128]{2,1,0:T(8,128)S(1)}, f32[2,264,128]{2,1,0:T(8,128)S(1)}, u32[]{:S(2)}, u32[]{:S(2)}) collective-permute-start(f32[2,264,128]{2,1,0:T(8,128)S(1)} %collective-permute-done.5.refs_1_), channel_id=1, source_target_pairs={{0,2},{1,3},{2,0},{3,1},{4,6},{5,7},{6,4},{7,5},{8,10},{9,11},{10,... | collective-permute-start | bytes 811016 | tf_op jit(solution)/shard_map/ppermute | solution.py:306
  23.0 7.7 %collective-permute-start.7 = (f32[256,128]{1,0:T(8,128)S(1)}, f32[256,128]{1,0:T(8,128)S(1)}, u32[]{:S(2)}, u32[]{:S(2)}) collective-permute-start(f32[256,128]{1,0:T(8,128)S(1)} %copy-done.3), channel_id=1, source_target_pairs={{0,16},{4,20},{8,24},{12,28},{16,0},{20,4},{24,8},{28,12},{1,17},{... | collective-permute-start | bytes 393224 | tf_op jit(solution)/shard_map/ppermute | solution.py:298
  24.5 10.7 %collective-permute-start.11 = (f32[2,264,128]{2,1,0:T(8,128)S(1)}, f32[2,264,128]{2,1,0:T(8,128)S(1)}, u32[]{:S(2)}, u32[]{:S(2)}) collective-permute-start(f32[2,264,128]{2,1,0:T(8,128)S(1)} %collective-permute-done.2.refs_4_), channel_id=1, source_target_pairs={{0,2},{4,6},{8,10},{12,14},{16,18},{20,22},{24,26},{28,30},{1,5},{... | collective-permute-start | bytes 811016 | tf_op jit(solution)/shard_map/ppermute | solution.py:315
  25.9 10.8 %collective-permute-start.15 = (f32[2,264,128]{2,1,0:T(8,128)S(1)}, f32[2,264,128]{2,1,0:T(8,128)S(1)}, u32[]{:S(2)}, u32[]{:S(2)}) collective-permute-start(f32[2,264,128]{2,1,0:T(8,128)S(1)} %collective-permute-done.2.refs_4_), channel_id=1, source_target_pairs={{0,4},{4,0},{8,12},{12,8},{16,20},{20,16},{24,28},{28,24},{1,3},{5... | collective-permute-start | bytes 811016 | tf_op jit(solution)/shard_map/ppermute | solution.py:315
  30.7 6.9 %collective-permute-start.3 = (f32[2,32,256]{2,1,0:T(8,128)S(1)}, f32[2,32,256]{2,1,0:T(8,128)S(1)}, u32[]{:S(2)}, u32[]{:S(2)}) collective-permute-start(f32[2,32,256]{2,1,0:T(8,128)S(1)} %get-tuple-element.39), channel_id=1, source_target_pairs={{0,8},{4,12},{8,0},{12,4},{16,24},{20,28},{24,16},{28,20},{1,9},{5... | collective-permute-start | bytes 196616 | tf_op jit(solution)/shard_map/ppermute | solution.py:298
  30.8 7.3 %collective-permute-start.4 = (f32[2,32,256]{2,1,0:T(8,128)S(1)}, f32[2,32,256]{2,1,0:T(8,128)S(1)}, u32[]{:S(2)}, u32[]{:S(2)}) collective-permute-start(f32[2,32,256]{2,1,0:T(8,128)S(1)} %get-tuple-element.41), channel_id=1, source_target_pairs={{0,16},{4,20},{8,24},{12,28},{16,0},{20,4},{24,8},{28,12},{1,17},{... | collective-permute-start | bytes 196616 | tf_op jit(solution)/shard_map/ppermute | solution.py:298
  33.2 6.8 %collective-permute-start.8 = (f32[2,32,256]{2,1,0:T(8,128)S(1)}, f32[2,32,256]{2,1,0:T(8,128)S(1)}, u32[]{:S(2)}, u32[]{:S(2)}) collective-permute-start(f32[2,32,256]{2,1,0:T(8,128)S(1)} %get-tuple-element.45), channel_id=1, source_target_pairs={{0,24},{4,28},{8,16},{12,20},{16,8},{20,12},{24,0},{28,4},{1,25},{... | collective-permute-start | bytes 196616 | tf_op jit(solution)/shard_map/ppermute | solution.py:298
  35.2 6.5 %collective-permute-start.14 = (f32[2,256,128]{2,1,0:T(8,128)S(1)}, f32[2,256,128]{2,1,0:T(8,128)S(1)}, u32[]{:S(2)}, u32[]{:S(2)}) collective-permute-start(f32[2,256,128]{2,1,0:T(8,128)S(1)} %pad_maximum_fusion.1.refs_0_), channel_id=1, source_target_pairs={{0,4},{4,0},{8,12},{12,8},{16,20},{20,16},{24,28},{28,24},{1,5},{5... | collective-permute-start | bytes 786440 | tf_op jit(solution)/shard_map/ppermute | solution.py:302
  36.7 8.9 %collective-permute-start.12 = (f32[2,256,128]{2,1,0:T(8,128)S(1)}, f32[2,256,128]{2,1,0:T(8,128)S(1)}, u32[]{:S(2)}, u32[]{:S(2)}) collective-permute-start(f32[2,256,128]{2,1,0:T(8,128)S(1)} %pad_maximum_fusion.1.refs_0_), channel_id=1, source_target_pairs={{0,8},{4,12},{8,0},{12,4},{16,24},{20,28},{24,16},{28,20},{1,9},{5... | collective-permute-start | bytes 786440 | tf_op jit(solution)/shard_map/ppermute | solution.py:298
  37.6 8.6 %collective-permute-start.16 = (f32[2,264,128]{2,1,0:T(8,128)S(1)}, f32[2,264,128]{2,1,0:T(8,128)S(1)}, u32[]{:S(2)}, u32[]{:S(2)}) collective-permute-start(f32[2,264,128]{2,1,0:T(8,128)S(1)} %collective-permute-done.11.refs_5_), channel_id=1, source_target_pairs={{0,4},{4,0},{8,12},{12,8},{16,20},{20,16},{24,28},{28,24},{1,3},{5... | collective-permute-start | bytes 811016 | tf_op jit(solution)/shard_map/ppermute | solution.py:315
  40.6 5.0 %collective-permute-start.9 = (f32[32,1024]{1,0:T(8,128)S(1)}, f32[32,1024]{1,0:T(8,128)S(1)}, u32[]{:S(2)}, u32[]{:S(2)}) collective-permute-start(f32[32,1024]{1,0:T(8,128)S(1)} %get-tuple-element.47), channel_id=1, source_target_pairs={{0,2},{1,3},{2,0},{3,1},{4,6},{5,7},{6,4},{7,5},{8,10},{9,11},{10,... | collective-permute-start | bytes 393224 | tf_op jit(solution)/shard_map/ppermute | solution.py:306
  41.7 4.6 %collective-permute-start.17 = (f32[2,264,128]{2,1,0:T(8,128)S(1)}, f32[2,264,128]{2,1,0:T(8,128)S(1)}, u32[]{:S(2)}, u32[]{:S(2)}) collective-permute-start(f32[2,264,128]{2,1,0:T(8,128)S(1)} %pad_maximum_fusion.refs_0_), channel_id=1, source_target_pairs={{0,1},{1,0},{2,3},{3,2},{4,5},{5,4},{6,7},{7,6},{8,9},{9,8},{10,11... | collective-permute-start | bytes 811016 | tf_op jit(solution)/shard_map/ppermute | solution.py:306
  41.7 5.1 %collective-permute-start.18 = (f32[2,264,128]{2,1,0:T(8,128)S(1)}, f32[2,264,128]{2,1,0:T(8,128)S(1)}, u32[]{:S(2)}, u32[]{:S(2)}) collective-permute-start(f32[2,264,128]{2,1,0:T(8,128)S(1)} %collective-permute-done.5.refs_1_), channel_id=1, source_target_pairs={{0,1},{1,0},{2,3},{3,2},{4,5},{5,4},{6,7},{7,6},{8,9},{9,8},{10,11... | collective-permute-start | bytes 811016 | tf_op jit(solution)/shard_map/ppermute | solution.py:306
  46.3 3.1 %collective-permute-start.21 = (f32[2,264,128]{2,1,0:T(8,128)S(1)}, f32[2,264,128]{2,1,0:T(8,128)S(1)}, u32[]{:S(2)}, u32[]{:S(2)}) collective-permute-start(f32[2,264,128]{2,1,0:T(8,128)S(1)} %collective-permute-done.2.refs_4_), channel_id=1, source_target_pairs={{0,1},{1,0},{2,3},{3,2},{4,5},{5,4},{6,7},{7,6},{8,9},{9,8},{10,11... | collective-permute-start | bytes 811016 | tf_op jit(solution)/shard_map/ppermute | solution.py:306
  46.8 2.6 %collective-permute-start.22 = (f32[2,264,128]{2,1,0:T(8,128)S(1)}, f32[2,264,128]{2,1,0:T(8,128)S(1)}, u32[]{:S(2)}, u32[]{:S(2)}) collective-permute-start(f32[2,264,128]{2,1,0:T(8,128)S(1)} %collective-permute-done.11.refs_5_), channel_id=1, source_target_pairs={{0,1},{1,0},{2,3},{3,2},{4,5},{5,4},{6,7},{7,6},{8,9},{9,8},{10,11... | collective-permute-start | bytes 811016 | tf_op jit(solution)/shard_map/ppermute | solution.py:306
  48.0 8.4 %collective-permute-start.25 = (f32[2,256,128]{2,1,0:T(8,128)S(1)}, f32[2,256,128]{2,1,0:T(8,128)S(1)}, u32[]{:S(2)}, u32[]{:S(2)}) collective-permute-start(f32[2,256,128]{2,1,0:T(8,128)S(1)} %collective-permute-done.12.refs_1_), channel_id=1, source_target_pairs={{0,4},{4,0},{8,12},{12,8},{16,20},{20,16},{24,28},{28,24},{1,5},{5... | collective-permute-start | bytes 786440 | tf_op jit(solution)/shard_map/ppermute | solution.py:302
  57.6 5.1 %collective-permute-start.26 = (f32[32,256]{1,0:T(8,128)S(1)}, f32[32,256]{1,0:T(8,128)S(1)}, u32[]{:S(2)}, u32[]{:S(2)}) collective-permute-start(f32[32,256]{1,0:T(8,128)S(1)} %get-tuple-element.66), channel_id=1, source_target_pairs={{0,2},{1,3},{2,0},{3,1},{4,6},{5,7},{6,4},{7,5},{8,10},{9,11},{10,... | collective-permute-start | bytes 98312 | tf_op jit(solution)/shard_map/ppermute | solution.py:306
  58.6 4.0 %collective-permute-start.27 = (f32[32,256]{1,0:T(8,128)S(1)}, f32[32,256]{1,0:T(8,128)S(1)}, u32[]{:S(2)}, u32[]{:S(2)}) collective-permute-start(f32[32,256]{1,0:T(8,128)S(1)} %get-tuple-element.67), channel_id=1, source_target_pairs={{0,1},{1,0},{2,3},{3,2},{4,5},{5,4},{6,7},{7,6},{8,9},{9,8},{10,11... | collective-permute-start | bytes 98312 | tf_op jit(solution)/shard_map/ppermute | solution.py:306
  58.7 4.0 %collective-permute-start.28 = (f32[32,256]{1,0:T(8,128)S(1)}, f32[32,256]{1,0:T(8,128)S(1)}, u32[]{:S(2)}, u32[]{:S(2)}) collective-permute-start(f32[32,256]{1,0:T(8,128)S(1)} %get-tuple-element.68), channel_id=1, source_target_pairs={{0,3},{1,2},{2,1},{3,0},{4,7},{5,6},{6,5},{7,4},{8,11},{9,10},{10,... | collective-permute-start | bytes 98312 | tf_op jit(solution)/shard_map/ppermute | solution.py:306
  (9 other events, 44.7 us)

commit v8 on v4

--- a/solution.py
+++ b/solution.py
@@ -141,13 +141,7 @@
 
 def origin(place_ref, crossed, first, second, m):
     rep, bulk = place_ref[0], place_ref[1]
-    if m % 2 == 0:
-        dx, dy = second, first
-    else:
-        core = (rep & 1) ^ crossed
-        dx = jnp.where(core == 0, first, second)
-        dy = jnp.where(core == 0, second, first)
-    return rep ^ (2 * dx + crossed), bulk ^ (2 * m + dy)
+    return rep ^ (2 * second + crossed), bulk ^ (2 * m + first)
 
 
 def pieces(bufs):
@@ -289,8 +283,6 @@
     out_ref[:, 1536:2048] = xb
 
 
-BOTH = ("bulk", "rep")
-
 SPREAD, INVERT, LEAVE, ROWS, FIRST, SECOND = 1_000_000_000, 3_500_000_000, 500_000_000, 1_000_000_000, 200_000_000, 3_000_000_000
 
 
@@ -304,15 +296,6 @@
 
 def swap_rep(x, bits):
     return lax.ppermute(x, "rep", [(k, k ^ bits) for k in range(4)])
-
-
-def cross(x, stage):
-    pairs = []
-    for rep in range(4):
-        for bulk in range(8):
-            to = (rep ^ 2, bulk) if (rep & 1) == stage else (rep, bulk ^ 1)
-            pairs.append((bulk * 4 + rep, to[1] * 4 + to[0]))
-    return lax.ppermute(x, BOTH, pairs)
 
 
 def after(x, *deps):
@@ -363,15 +346,15 @@
     c_near_got = swap_y(c_near)
 
     far_now = after(far, near0, near1, came, c_near)
-    far0 = cross(far_now, 0)
-    far1 = cross(far_now, 1)
+    far0 = swap_y(far_now)
+    far1 = swap_rep(far_now, 2)
     b_out = call(spread_kernel, [shape(2, 32, 256)] * 3, [SMEM, VMEM, VMEM], [VMEM] * 3, [], SPREAD, 4, "spread")(
         place, blocks, came
     )
     b_z = [swap_z(after(b, far), m + 1) for m, b in enumerate(b_out)]
     c_far = swap_z(after(c_near, far0), 1)
     c_far_got = swap_y(c_far)
-    far01 = cross(after(far0, far1, near01), 1)
+    far01 = swap_rep(after(far0, far1, near01), 2)
 
     left, both = call(
         rows_kernel,

time: 63.7 us -> 65.2 us (1.024)
  waiting for transfers between devices: 18.3 us -> 20.8 us
  starting transfers between devices: 29.3 us -> 28.4 us
    ppermute x15 -> x17, waiting for transfers between devices: 3.97 us -> 5.57 us  [swap_rep(): return lax.ppermute(x, 'rep', [(k, k ^ bits) for k in range(4)])]
    ppermute x3 -> x0, starting transfers between devices: 1.53 us -> none  [cross(): return lax.ppermute(x, BOTH, pairs)]
    ppermute x7, waiting for transfers between devices: 10.7 us -> 11.9 us  [swap_z(): return lax.ppermute(x, 'bulk', [(k, k ^ 2 * m) for k in range(8)])]
    ppermute x15 -> x17, starting transfers between devices: 8.21 us -> 9.22 us  [swap_rep(): return lax.ppermute(x, 'rep', [(k, k ^ bits) for k in range(4)])]
    ppermute x7, starting transfers between devices: 13.9 us -> 13 us  [swap_z(): return lax.ppermute(x, 'bulk', [(k, k ^ 2 * m) for k in range(8)])]
    ppermute x4 -> x5, starting transfers between devices: 5.72 us -> 6.18 us  [swap_y(): return lax.ppermute(x, 'bulk', [(k, k ^ 1) for k in range(8)])]
    ppermute x4 -> x5, waiting for transfers between devices: 3.2 us -> 3.29 us  [swap_y(): return lax.ppermute(x, 'bulk', [(k, k ^ 1) for k in range(8)])]
  transfers between devices with their start and end apart: 29 -> 29, of which waited for: 9 -> 9; matrix products, arithmetic and copies ran while one was open for 0% -> 0% of each run, Pallas kernels for 13% -> 12%
where the time goes in v8:
time: 65.2 us; the launch traced here: 65 us
  starting transfers between devices  28.4 us (44%)
  waiting for transfers between devices  20.8 us (32%)
  Pallas kernels  14 us (21%)
  local copies, waits for them, and re-layouts  1.59 us (2%)
    ppermute x7, starting transfers between devices, swap_z(): return lax.ppermute(x, 'bulk', [(k, k ^ 2 * m) for k in range(8)])  13 us
    ppermute x7, waiting for transfers between devices, swap_z(): return lax.ppermute(x, 'bulk', [(k, k ^ 2 * m) for k in range(8)])  11.9 us
    ppermute x17, starting transfers between devices, swap_rep(): return lax.ppermute(x, 'rep', [(k, k ^ bits) for k in range(4)])  9.22 us
    ppermute x5, starting transfers between devices, swap_y(): return lax.ppermute(x, 'bulk', [(k, k ^ 1) for k in range(8)])  6.18 us
    ppermute x17, waiting for transfers between devices, swap_rep(): return lax.ppermute(x, 'rep', [(k, k ^ bits) for k in range(4)])  5.57 us
    pallas_call x1, Pallas kernels, per_device(): call(first_kernel, shape(128, 1024), [SMEM] + [VMEM] * 18, VMEM, [pltpu.V...  3.56 us
    ppermute x5, waiting for transfers between devices, swap_y(): return lax.ppermute(x, 'bulk', [(k, k ^ 1) for k in range(8)])  3.29 us
    pallas_call x1, Pallas kernels, per_device(): call(second_factor_kernel, halves, [SMEM] + [VMEM] * 16, [VMEM] * 2, scra...  2.84 us
  transfers between devices with their start and end apart: 29, of which 9 were waited for; matrix products, arithmetic and copies ran while one was open for 0% of the time, Pallas kernels for 12%

profile of v8, /device:TPU:0, one launch (start us, length us, event | category | flops | bytes accessed | tf_op | source)
XLA Modules:
  0.0 65.0 jit_solution(10882250750280428867)
XLA Ops:
  0.1 0.9 %copy-done.1 = f32[256,128]{1,0:T(8,128)S(1)} copy-done((f32[256,128]{1,0:T(8,128)S(1)}, f32[256,128]{1,0:T(8,128)}, u32[]{:S(2)}) %copy-start.1) | copy-done | bytes 131096
  1.7 2.6 %invert.1 = f32[264,128]{1,0:T(8,128)S(1)} custom-call(s32[2]{0:T(128)S(1)} %pad_add_fusion.place_ref, f32[256,128]{1,0:T(8,128)S(1)} %copy-done.1, f32[2,128]{1,0:T(2,128)S(1)} %copy-done.2), custom_call_target="tpu_custom_call" | custom-call | flops 3500000000 | bytes 2097152 | tf_op jit(solution)/shard_map/invert/pallas_call | solution.py:332
  4.2 2.1 %collective-permute-start.1 = (f32[264,128]{1,0:T(8,128)S(1)}, f32[264,128]{1,0:T(8,128)S(1)}, u32[]{:S(2)}, u32[]{:S(2)}) collective-permute-start(f32[264,128]{1,0:T(8,128)S(1)} %invert.1), channel_id=1, source_target_pairs={{0,16},{4,20},{8,24},{12,28},{16,0},{20,4},{24,8},{28,12},{1,17},{... | collective-permute-start | bytes 405512 | tf_op jit(solution)/shard_map/ppermute | solution.py:290
  6.3 6.8 %collective-permute-done.1 = f32[264,128]{1,0:T(8,128)S(1)} collective-permute-done((f32[264,128]{1,0:T(8,128)S(1)}, f32[264,128]{1,0:T(8,128)S(1)}, u32[]{:S(2)}, u32[]{:S(2)}) %collective-permute-start.1) | collective-permute-done | bytes 135200 | tf_op jit(solution)/shard_map/ppermute | solution.py:290
  13.1 2.0 %collective-permute-start.8 = (f32[2,264,128]{2,1,0:T(8,128)S(1)}, f32[2,264,128]{2,1,0:T(8,128)S(1)}, u32[]{:S(2)}, u32[]{:S(2)}) collective-permute-start(f32[2,264,128]{2,1,0:T(8,128)S(1)} %pad_maximum_fusion.refs_0_), channel_id=1, source_target_pairs={{0,4},{4,0},{8,12},{12,8},{16,20},{20,16},{24,28},{28,24},{1,5},{5... | collective-permute-start | bytes 811016 | tf_op jit(solution)/shard_map/ppermute | solution.py:294
  15.2 1.5 %collective-permute-start.9 = (f32[2,264,128]{2,1,0:T(8,128)S(1)}, f32[2,264,128]{2,1,0:T(8,128)S(1)}, u32[]{:S(2)}, u32[]{:S(2)}) collective-permute-start(f32[2,264,128]{2,1,0:T(8,128)S(1)} %pad_maximum_fusion.refs_0_), channel_id=1, source_target_pairs={{0,2},{1,3},{2,0},{3,1},{4,6},{5,7},{6,4},{7,5},{8,10},{9,11},{10,... | collective-permute-start | bytes 811016 | tf_op jit(solution)/shard_map/ppermute | solution.py:298
  16.7 2.7 %collective-permute-start.7 = (f32[256,128]{1,0:T(8,128)S(1)}, f32[256,128]{1,0:T(8,128)S(1)}, u32[]{:S(2)}, u32[]{:S(2)}) collective-permute-start(f32[256,128]{1,0:T(8,128)S(1)} %copy-done.3), channel_id=1, source_target_pairs={{0,16},{4,20},{8,24},{12,28},{16,0},{20,4},{24,8},{28,12},{1,17},{... | collective-permute-start | bytes 393224 | tf_op jit(solution)/shard_map/ppermute | solution.py:290
  20.5 1.2 %collective-permute-start.14 = (f32[2,264,128]{2,1,0:T(8,128)S(1)}, f32[2,264,128]{2,1,0:T(8,128)S(1)}, u32[]{:S(2)}, u32[]{:S(2)}) collective-permute-start(f32[2,264,128]{2,1,0:T(8,128)S(1)} %collective-permute-done.8.refs_1_), channel_id=1, source_target_pairs={{0,2},{1,3},{2,0},{3,1},{4,6},{5,7},{6,4},{7,5},{8,10},{9,11},{10,... | collective-permute-start | bytes 811016 | tf_op jit(solution)/shard_map/ppermute | solution.py:298
  21.7 3.2 %collective-permute-done.7 = f32[256,128]{1,0:T(8,128)S(1)} collective-permute-done((f32[256,128]{1,0:T(8,128)S(1)}, f32[256,128]{1,0:T(8,128)S(1)}, u32[]{:S(2)}, u32[]{:S(2)}) %collective-permute-start.7) | collective-permute-done | bytes 131104 | tf_op jit(solution)/shard_map/ppermute | solution.py:290
  27.2 3.5 %collective-permute-start.3 = (f32[2,32,256]{2,1,0:T(8,128)S(1)}, f32[2,32,256]{2,1,0:T(8,128)S(1)}, u32[]{:S(2)}, u32[]{:S(2)}) collective-permute-start(f32[2,32,256]{2,1,0:T(8,128)S(1)} %get-tuple-element.39), channel_id=1, source_target_pairs={{0,8},{4,12},{8,0},{12,4},{16,24},{20,28},{24,16},{28,20},{1,9},{5... | collective-permute-start | bytes 196616 | tf_op jit(solution)/shard_map/ppermute | solution.py:290
  30.7 1.6 %collective-permute-start.4 = (f32[2,32,256]{2,1,0:T(8,128)S(1)}, f32[2,32,256]{2,1,0:T(8,128)S(1)}, u32[]{:S(2)}, u32[]{:S(2)}) collective-permute-start(f32[2,32,256]{2,1,0:T(8,128)S(1)} %get-tuple-element.41), channel_id=1, source_target_pairs={{0,16},{4,20},{8,24},{12,28},{16,0},{20,4},{24,8},{28,12},{1,17},{... | collective-permute-start | bytes 196616 | tf_op jit(solution)/shard_map/ppermute | solution.py:290
  32.3 1.0 %collective-permute-start.5 = (f32[2,32,256]{2,1,0:T(8,128)S(1)}, f32[2,32,256]{2,1,0:T(8,128)S(1)}, u32[]{:S(2)}, u32[]{:S(2)}) collective-permute-start(f32[2,32,256]{2,1,0:T(8,128)S(1)} %get-tuple-element.43), channel_id=1, source_target_pairs={{0,24},{4,28},{8,16},{12,20},{16,8},{20,12},{24,0},{28,4},{1,25},{... | collective-permute-start | bytes 196616 | tf_op jit(solution)/shard_map/ppermute | solution.py:290
  33.4 1.5 %collective-permute-start.13 = (f32[2,256,128]{2,1,0:T(8,128)S(1)}, f32[2,256,128]{2,1,0:T(8,128)S(1)}, u32[]{:S(2)}, u32[]{:S(2)}) collective-permute-start(f32[2,256,128]{2,1,0:T(8,128)S(1)} %pad_maximum_fusion.2.refs_0_), channel_id=1, source_target_pairs={{0,4},{4,0},{8,12},{12,8},{16,20},{20,16},{24,28},{28,24},{1,5},{5... | collective-permute-start | bytes 786440 | tf_op jit(solution)/shard_map/ppermute | solution.py:294
  34.9 2.1 %collective-permute-start.11 = (f32[2,256,128]{2,1,0:T(8,128)S(1)}, f32[2,256,128]{2,1,0:T(8,128)S(1)}, u32[]{:S(2)}, u32[]{:S(2)}) collective-permute-start(f32[2,256,128]{2,1,0:T(8,128)S(1)} %pad_maximum_fusion.2.refs_0_), channel_id=1, source_target_pairs={{0,8},{4,12},{8,0},{12,4},{16,24},{20,28},{24,16},{28,20},{1,9},{5... | collective-permute-start | bytes 786440 | tf_op jit(solution)/shard_map/ppermute | solution.py:290
  37.8 1.3 %collective-permute-done.5.b3 = f32[2,32,256]{2,1,0:T(8,128)S(1)} collective-permute-done((f32[2,32,256]{2,1,0:T(8,128)S(1)}, f32[2,32,256]{2,1,0:T(8,128)S(1)}, u32[]{:S(2)}, u32[]{:S(2)}) %collective-permute-start.5) | collective-permute-done | bytes 65568 | tf_op jit(solution)/shard_map/ppermute | solution.py:290
  39.7 1.0 %collective-permute-start.6 = (f32[32,1024]{1,0:T(8,128)S(1)}, f32[32,1024]{1,0:T(8,128)S(1)}, u32[]{:S(2)}, u32[]{:S(2)}) collective-permute-start(f32[32,1024]{1,0:T(8,128)S(1)} %get-tuple-element.45), channel_id=1, source_target_pairs={{0,2},{1,3},{2,0},{3,1},{4,6},{5,7},{6,4},{7,5},{8,10},{9,11},{10,... | collective-permute-start | bytes 393224 | tf_op jit(solution)/shard_map/ppermute | solution.py:298
  41.3 4.7 %collective-permute-done.6 = f32[32,1024]{1,0:T(8,128)S(1)} collective-permute-done((f32[32,1024]{1,0:T(8,128)S(1)}, f32[32,1024]{1,0:T(8,128)S(1)}, u32[]{:S(2)}, u32[]{:S(2)}) %collective-permute-start.6) | collective-permute-done | bytes 131104 | tf_op jit(solution)/shard_map/ppermute | solution.py:298
  48.3 1.5 %collective-permute-start.25 = (f32[2,256,128]{2,1,0:T(8,128)S(1)}, f32[2,256,128]{2,1,0:T(8,128)S(1)}, u32[]{:S(2)}, u32[]{:S(2)}) collective-permute-start(f32[2,256,128]{2,1,0:T(8,128)S(1)} %collective-permute-done.11.refs_1_), channel_id=1, source_target_pairs={{0,4},{4,0},{8,12},{12,8},{16,20},{20,16},{24,28},{28,24},{1,5},{5... | collective-permute-start | bytes 786440 | tf_op jit(solution)/shard_map/ppermute | solution.py:294
  49.8 3.6 %first_panel.1.x_ref = f32[128,1024]{1,0:T(8,128)S(1)} custom-call(s32[2]{0:T(128)S(1)} %pad_add_fusion.place_ref, f32[2,32,1024]{2,1,0:T(8,128)S(1)} %pad_maximum_fusion.1.pair, f32[2,32,1024]{2,1,0:T(8,128)S(1)} %collective-permute-done.12.other_pair, f32[2,264,128]{2,1,0:T(8,128)S(1)} %pad_maximum_fusion.refs_0_, ...), custom_call_target="tpu_custom_call" | custom-call | flops 200000000 | bytes 2097152 | tf_op jit(solution)/shard_map/first_panel/pallas_call | solution.py:376
  53.4 3.2 %collective-permute-done.25.refs_3_ = f32[2,256,128]{2,1,0:T(8,128)S(1)} collective-permute-done((f32[2,256,128]{2,1,0:T(8,128)S(1)}, f32[2,256,128]{2,1,0:T(8,128)S(1)}, u32[]{:S(2)}, u32[]{:S(2)}) %collective-permute-start.25) | collective-permute-done | bytes 262176 | tf_op jit(solution)/shard_map/ppermute | solution.py:294
  56.6 1.3 %update.1 = (f32[32,256]{1,0:T(8,128)S(1)}, f32[32,256]{1,0:T(8,128)S(1)}, f32[32,256]{1,0:T(8,128)S(1)}, f32[32,256]{1,0:T(8,128)S(1)}) custom-call(s32[2]{0:T(128)S(1)} %pad_add_fusion.place_ref, f32[128,1024]{1,0:T(8,128)S(1)} %first_panel.1.x_ref, f32[2,256,128]{2,1,0:T(8,128)S(1)} %pad_maximum_fusion.2.refs_0_, ...), custom_call_target="tpu_custom_call" | custom-call | flops 2000000000 | bytes 2097152 | tf_op jit(solution)/shard_map/update/pallas_call | solution.py:387
  57.9 1.3 %collective-permute-start.26 = (f32[32,256]{1,0:T(8,128)S(1)}, f32[32,256]{1,0:T(8,128)S(1)}, u32[]{:S(2)}, u32[]{:S(2)}) collective-permute-start(f32[32,256]{1,0:T(8,128)S(1)} %get-tuple-element.66), channel_id=1, source_target_pairs={{0,2},{1,3},{2,0},{3,1},{4,6},{5,7},{6,4},{7,5},{8,10},{9,11},{10,... | collective-permute-start | bytes 98312 | tf_op jit(solution)/shard_map/ppermute | solution.py:298
  60.1 2.8 %second_factor.1 = (bf16[1024,1024]{1,0:T(8,128)(2,1)S(1)}, bf16[1024,1024]{1,0:T(8,128)(2,1)S(1)}) custom-call(s32[2]{0:T(128)S(1)} %pad_add_fusion.place_ref, f32[2,264,128]{2,1,0:T(8,128)S(1)} %pad_maximum_fusion.refs_0_, f32[2,264,128]{2,1,0:T(8,128)S(1)} %collective-permute-done.8.refs_1_, f32[2,264,128]{2,1,0:T(8,128)S(1)} %collective-permute-done.9.refs_2_, ...), custom_call_target="tpu_custom_call" | custom-call | flops 3000000000 | bytes 2097152 | tf_op jit(solution)/shard_map/second_factor/pallas_call | solution.py:399
  63.0 2.1 %second_panel.1 = f32[32,2048]{1,0:T(8,128)} custom-call(s32[2]{0:T(128)S(1)} %pad_add_fusion.place_ref, f32[128,1024]{1,0:T(8,128)S(1)} %first_panel.1.x_ref, f32[2,32,1024]{2,1,0:T(8,128)S(1)} %get-tuple-element.61.both_ref, bf16[1024,1024]{1,0:T(8,128)(2,1)S(1)} %get-tuple-element.64.uh_ref, bf16[1024,1024]{1,0:T(8,128)(2,1)S(1)} %get-tuple-element.65.ul_ref, ...), custom_call_target="tpu_custom_call" | custom-call | flops 2500000000 | bytes 2097152 | tf_op jit(solution)/shard_map/second_panel/pallas_call | solution.py:403
  (54 shorter events, 9.4 us)
Async XLA Ops:
  4.2 8.9 %collective-permute-start.1 = (f32[264,128]{1,0:T(8,128)S(1)}, f32[264,128]{1,0:T(8,128)S(1)}, u32[]{:S(2)}, u32[]{:S(2)}) collective-permute-start(f32[264,128]{1,0:T(8,128)S(1)} %invert.1), channel_id=1, source_target_pairs={{0,16},{4,20},{8,24},{12,28},{16,0},{20,4},{24,8},{28,12},{1,17},{... | collective-permute-start | bytes 405512 | tf_op jit(solution)/shard_map/ppermute | solution.py:290
  13.1 7.4 %collective-permute-start.8 = (f32[2,264,128]{2,1,0:T(8,128)S(1)}, f32[2,264,128]{2,1,0:T(8,128)S(1)}, u32[]{:S(2)}, u32[]{:S(2)}) collective-permute-start(f32[2,264,128]{2,1,0:T(8,128)S(1)} %pad_maximum_fusion.refs_0_), channel_id=1, source_target_pairs={{0,4},{4,0},{8,12},{12,8},{16,20},{20,16},{24,28},{28,24},{1,5},{5... | collective-permute-start | bytes 811016 | tf_op jit(solution)/shard_map/ppermute | solution.py:294
  15.2 9.8 %collective-permute-start.9 = (f32[2,264,128]{2,1,0:T(8,128)S(1)}, f32[2,264,128]{2,1,0:T(8,128)S(1)}, u32[]{:S(2)}, u32[]{:S(2)}) collective-permute-start(f32[2,264,128]{2,1,0:T(8,128)S(1)} %pad_maximum_fusion.refs_0_), channel_id=1, source_target_pairs={{0,2},{1,3},{2,0},{3,1},{4,6},{5,7},{6,4},{7,5},{8,10},{9,11},{10,... | collective-permute-start | bytes 811016 | tf_op jit(solution)/shard_map/ppermute | solution.py:298
  16.7 9.0 %collective-permute-start.2 = (f32[2,264,128]{2,1,0:T(8,128)S(1)}, f32[2,264,128]{2,1,0:T(8,128)S(1)}, u32[]{:S(2)}, u32[]{:S(2)}) collective-permute-start(f32[2,264,128]{2,1,0:T(8,128)S(1)} %pad_maximum_fusion.refs_0_), channel_id=1, source_target_pairs={{0,8},{4,12},{8,0},{12,4},{16,24},{20,28},{24,16},{28,20},{1,9},{5... | collective-permute-start | bytes 811016 | tf_op jit(solution)/shard_map/ppermute | solution.py:290
  16.7 8.2 %collective-permute-start.7 = (f32[256,128]{1,0:T(8,128)S(1)}, f32[256,128]{1,0:T(8,128)S(1)}, u32[]{:S(2)}, u32[]{:S(2)}) collective-permute-start(f32[256,128]{1,0:T(8,128)S(1)} %copy-done.3), channel_id=1, source_target_pairs={{0,16},{4,20},{8,24},{12,28},{16,0},{20,4},{24,8},{28,12},{1,17},{... | collective-permute-start | bytes 393224 | tf_op jit(solution)/shard_map/ppermute | solution.py:290
  19.9 5.0 %collective-permute-start = (f32[4,32,256]{2,1,0:T(8,128)S(1)}, f32[4,32,256]{2,1,0:T(8,128)S(1)}, u32[]{:S(2)}, u32[]{:S(2)}) collective-permute-start(f32[4,32,256]{2,1,0:T(8,128)S(1)} %leave.1), channel_id=1, source_target_pairs={{0,4},{4,0},{8,12},{12,8},{16,20},{20,16},{24,28},{28,24},{1,5},{5... | collective-permute-start | bytes 393224 | tf_op jit(solution)/shard_map/ppermute | solution.py:294
  20.5 11.8 %collective-permute-start.14 = (f32[2,264,128]{2,1,0:T(8,128)S(1)}, f32[2,264,128]{2,1,0:T(8,128)S(1)}, u32[]{:S(2)}, u32[]{:S(2)}) collective-permute-start(f32[2,264,128]{2,1,0:T(8,128)S(1)} %collective-permute-done.8.refs_1_), channel_id=1, source_target_pairs={{0,2},{1,3},{2,0},{3,1},{4,6},{5,7},{6,4},{7,5},{8,10},{9,11},{10,... | collective-permute-start | bytes 811016 | tf_op jit(solution)/shard_map/ppermute | solution.py:298
  25.6 7.7 %collective-permute-start.10 = (f32[2,264,128]{2,1,0:T(8,128)S(1)}, f32[2,264,128]{2,1,0:T(8,128)S(1)}, u32[]{:S(2)}, u32[]{:S(2)}) collective-permute-start(f32[2,264,128]{2,1,0:T(8,128)S(1)} %collective-permute-done.2.refs_4_), channel_id=1, source_target_pairs={{0,4},{4,0},{8,12},{12,8},{16,20},{20,16},{24,28},{28,24},{1,5},{5... | collective-permute-start | bytes 811016 | tf_op jit(solution)/shard_map/ppermute | solution.py:294
  26.1 8.7 %collective-permute-start.15 = (f32[2,264,128]{2,1,0:T(8,128)S(1)}, f32[2,264,128]{2,1,0:T(8,128)S(1)}, u32[]{:S(2)}, u32[]{:S(2)}) collective-permute-start(f32[2,264,128]{2,1,0:T(8,128)S(1)} %collective-permute-done.2.refs_4_), channel_id=1, source_target_pairs={{0,2},{1,3},{2,0},{3,1},{4,6},{5,7},{6,4},{7,5},{8,10},{9,11},{10,... | collective-permute-start | bytes 811016 | tf_op jit(solution)/shard_map/ppermute | solution.py:298
  27.2 9.8 %collective-permute-start.3 = (f32[2,32,256]{2,1,0:T(8,128)S(1)}, f32[2,32,256]{2,1,0:T(8,128)S(1)}, u32[]{:S(2)}, u32[]{:S(2)}) collective-permute-start(f32[2,32,256]{2,1,0:T(8,128)S(1)} %get-tuple-element.39), channel_id=1, source_target_pairs={{0,8},{4,12},{8,0},{12,4},{16,24},{20,28},{24,16},{28,20},{1,9},{5... | collective-permute-start | bytes 196616 | tf_op jit(solution)/shard_map/ppermute | solution.py:290
  30.7 7.1 %collective-permute-start.4 = (f32[2,32,256]{2,1,0:T(8,128)S(1)}, f32[2,32,256]{2,1,0:T(8,128)S(1)}, u32[]{:S(2)}, u32[]{:S(2)}) collective-permute-start(f32[2,32,256]{2,1,0:T(8,128)S(1)} %get-tuple-element.41), channel_id=1, source_target_pairs={{0,16},{4,20},{8,24},{12,28},{16,0},{20,4},{24,8},{28,12},{1,17},{... | collective-permute-start | bytes 196616 | tf_op jit(solution)/shard_map/ppermute | solution.py:290
  32.3 6.8 %collective-permute-start.5 = (f32[2,32,256]{2,1,0:T(8,128)S(1)}, f32[2,32,256]{2,1,0:T(8,128)S(1)}, u32[]{:S(2)}, u32[]{:S(2)}) collective-permute-start(f32[2,32,256]{2,1,0:T(8,128)S(1)} %get-tuple-element.43), channel_id=1, source_target_pairs={{0,24},{4,28},{8,16},{12,20},{16,8},{20,12},{24,0},{28,4},{1,25},{... | collective-permute-start | bytes 196616 | tf_op jit(solution)/shard_map/ppermute | solution.py:290
  33.4 7.4 %collective-permute-start.13 = (f32[2,256,128]{2,1,0:T(8,128)S(1)}, f32[2,256,128]{2,1,0:T(8,128)S(1)}, u32[]{:S(2)}, u32[]{:S(2)}) collective-permute-start(f32[2,256,128]{2,1,0:T(8,128)S(1)} %pad_maximum_fusion.2.refs_0_), channel_id=1, source_target_pairs={{0,4},{4,0},{8,12},{12,8},{16,20},{20,16},{24,28},{28,24},{1,5},{5... | collective-permute-start | bytes 786440 | tf_op jit(solution)/shard_map/ppermute | solution.py:294
  34.9 11.1 %collective-permute-start.11 = (f32[2,256,128]{2,1,0:T(8,128)S(1)}, f32[2,256,128]{2,1,0:T(8,128)S(1)}, u32[]{:S(2)}, u32[]{:S(2)}) collective-permute-start(f32[2,256,128]{2,1,0:T(8,128)S(1)} %pad_maximum_fusion.2.refs_0_), channel_id=1, source_target_pairs={{0,8},{4,12},{8,0},{12,4},{16,24},{20,28},{24,16},{28,20},{1,9},{5... | collective-permute-start | bytes 786440 | tf_op jit(solution)/shard_map/ppermute | solution.py:290
  37.0 9.5 %collective-permute-start.16 = (f32[2,264,128]{2,1,0:T(8,128)S(1)}, f32[2,264,128]{2,1,0:T(8,128)S(1)}, u32[]{:S(2)}, u32[]{:S(2)}) collective-permute-start(f32[2,264,128]{2,1,0:T(8,128)S(1)} %collective-permute-done.10.refs_5_), channel_id=1, source_target_pairs={{0,2},{1,3},{2,0},{3,1},{4,6},{5,7},{6,4},{7,5},{8,10},{9,11},{10,... | collective-permute-start | bytes 811016 | tf_op jit(solution)/shard_map/ppermute | solution.py:298
  39.7 6.3 %collective-permute-start.6 = (f32[32,1024]{1,0:T(8,128)S(1)}, f32[32,1024]{1,0:T(8,128)S(1)}, u32[]{:S(2)}, u32[]{:S(2)}) collective-permute-start(f32[32,1024]{1,0:T(8,128)S(1)} %get-tuple-element.45), channel_id=1, source_target_pairs={{0,2},{1,3},{2,0},{3,1},{4,6},{5,7},{6,4},{7,5},{8,10},{9,11},{10,... | collective-permute-start | bytes 393224 | tf_op jit(solution)/shard_map/ppermute | solution.py:298
  40.7 5.8 %collective-permute-start.17 = (f32[2,264,128]{2,1,0:T(8,128)S(1)}, f32[2,264,128]{2,1,0:T(8,128)S(1)}, u32[]{:S(2)}, u32[]{:S(2)}) collective-permute-start(f32[2,264,128]{2,1,0:T(8,128)S(1)} %pad_maximum_fusion.refs_0_), channel_id=1, source_target_pairs={{0,1},{1,0},{2,3},{3,2},{4,5},{5,4},{6,7},{7,6},{8,9},{9,8},{10,11... | collective-permute-start | bytes 811016 | tf_op jit(solution)/shard_map/ppermute | solution.py:298
  40.7 6.3 %collective-permute-start.18 = (f32[2,264,128]{2,1,0:T(8,128)S(1)}, f32[2,264,128]{2,1,0:T(8,128)S(1)}, u32[]{:S(2)}, u32[]{:S(2)}) collective-permute-start(f32[2,264,128]{2,1,0:T(8,128)S(1)} %collective-permute-done.8.refs_1_), channel_id=1, source_target_pairs={{0,1},{1,0},{2,3},{3,2},{4,5},{5,4},{6,7},{7,6},{8,9},{9,8},{10,11... | collective-permute-start | bytes 811016 | tf_op jit(solution)/shard_map/ppermute | solution.py:298
  46.6 3.2 %collective-permute-start.21 = (f32[2,264,128]{2,1,0:T(8,128)S(1)}, f32[2,264,128]{2,1,0:T(8,128)S(1)}, u32[]{:S(2)}, u32[]{:S(2)}) collective-permute-start(f32[2,264,128]{2,1,0:T(8,128)S(1)} %collective-permute-done.2.refs_4_), channel_id=1, source_target_pairs={{0,1},{1,0},{2,3},{3,2},{4,5},{5,4},{6,7},{7,6},{8,9},{9,8},{10,11... | collective-permute-start | bytes 811016 | tf_op jit(solution)/shard_map/ppermute | solution.py:298
  47.1 2.7 %collective-permute-start.22 = (f32[2,264,128]{2,1,0:T(8,128)S(1)}, f32[2,264,128]{2,1,0:T(8,128)S(1)}, u32[]{:S(2)}, u32[]{:S(2)}) collective-permute-start(f32[2,264,128]{2,1,0:T(8,128)S(1)} %collective-permute-done.10.refs_5_), channel_id=1, source_target_pairs={{0,1},{1,0},{2,3},{3,2},{4,5},{5,4},{6,7},{7,6},{8,9},{9,8},{10,11... | collective-permute-start | bytes 811016 | tf_op jit(solution)/shard_map/ppermute | solution.py:298
  48.3 8.4 %collective-permute-start.25 = (f32[2,256,128]{2,1,0:T(8,128)S(1)}, f32[2,256,128]{2,1,0:T(8,128)S(1)}, u32[]{:S(2)}, u32[]{:S(2)}) collective-permute-start(f32[2,256,128]{2,1,0:T(8,128)S(1)} %collective-permute-done.11.refs_1_), channel_id=1, source_target_pairs={{0,4},{4,0},{8,12},{12,8},{16,20},{20,16},{24,28},{28,24},{1,5},{5... | collective-permute-start | bytes 786440 | tf_op jit(solution)/shard_map/ppermute | solution.py:294
  57.9 5.1 %collective-permute-start.26 = (f32[32,256]{1,0:T(8,128)S(1)}, f32[32,256]{1,0:T(8,128)S(1)}, u32[]{:S(2)}, u32[]{:S(2)}) collective-permute-start(f32[32,256]{1,0:T(8,128)S(1)} %get-tuple-element.66), channel_id=1, source_target_pairs={{0,2},{1,3},{2,0},{3,1},{4,6},{5,7},{6,4},{7,5},{8,10},{9,11},{10,... | collective-permute-start | bytes 98312 | tf_op jit(solution)/shard_map/ppermute | solution.py:298
  59.2 3.8 %collective-permute-start.27 = (f32[32,256]{1,0:T(8,128)S(1)}, f32[32,256]{1,0:T(8,128)S(1)}, u32[]{:S(2)}, u32[]{:S(2)}) collective-permute-start(f32[32,256]{1,0:T(8,128)S(1)} %get-tuple-element.67), channel_id=1, source_target_pairs={{0,1},{1,0},{2,3},{3,2},{4,5},{5,4},{6,7},{7,6},{8,9},{9,8},{10,11... | collective-permute-start | bytes 98312 | tf_op jit(solution)/shard_map/ppermute | solution.py:298
  59.2 3.8 %collective-permute-start.28 = (f32[32,256]{1,0:T(8,128)S(1)}, f32[32,256]{1,0:T(8,128)S(1)}, u32[]{:S(2)}, u32[]{:S(2)}) collective-permute-start(f32[32,256]{1,0:T(8,128)S(1)} %get-tuple-element.68), channel_id=1, source_target_pairs={{0,3},{1,2},{2,1},{3,0},{4,7},{5,6},{6,5},{7,4},{8,11},{9,10},{10,... | collective-permute-start | bytes 98312 | tf_op jit(solution)/shard_map/ppermute | solution.py:298
  (9 other events, 43.7 us)

commit v9 on v4

--- a/solution.py
+++ b/solution.py
@@ -221,15 +221,24 @@
             rest = rest[:, 256:] - mul(x, (high[rows, cols], low[rows, cols]), NT)
 
 
-def update_kernel(place_ref, x_ref, *refs):
-    held, outs, (high, low) = refs[:4], refs[4:8], refs[8:]
+def half_update(x, held, got):
+    pairs = [split(piece) for piece in (held[0], held[1], got[0], got[1])]
+    high = jnp.concatenate([p[0] for p in pairs], axis=1)
+    low = jnp.concatenate([p[1] for p in pairs], axis=1)
+    return mul(jnp.concatenate(x, axis=1), (high, low), NT)
+
+
+def columns(place_ref, x_ref, far):
     bulk = place_ref[1]
-    for dy in range(2):
-        for m in range(4):
-            h, l = split(held[2 * dy + m % 2][m // 2])
-            high[:, offset(bulk ^ (2 * m + dy), 128)] = h
-            low[:, offset(bulk ^ (2 * m + dy), 128)] = l
-    upd = mul(x_ref[...], (high[...], low[...]), NT)
+    return [x_ref[:, offset(bulk ^ (2 * m + dy), 128)] for dy in range(2) for m in (far, 2 + far)]
+
+
+def near_kernel(place_ref, x_ref, held, got, out):
+    out[...] = half_update(columns(place_ref, x_ref, 0), held, got)
+
+
+def update_kernel(place_ref, x_ref, near, held, got, *outs):
+    upd = near[...] + half_update(columns(place_ref, x_ref, 1), held, got)
     for k, out in enumerate(outs):
         out[...] = upd[32 * k : 32 * (k + 1)]
 
@@ -401,16 +410,19 @@
         "first_panel",
     )(place, pair, after(other_pair, c_near_got), *bufs)
 
+    near_upd = call(near_kernel, shape(128, 256), [SMEM] + [VMEM] * 3, VMEM, [], 10_000_000, 24, "near_update")(
+        place, x, c_near, c_near_got
+    )
     mine, to_x, to_core, to_both = call(
         update_kernel,
         [shape(32, 256)] * 4,
-        [SMEM] + [VMEM] * 5,
+        [SMEM] + [VMEM] * 4,
         [VMEM] * 4,
-        [pltpu.VMEM((256, 1024), BF16)] * 2,
+        [],
         2_000_000_000,
         24,
         "update",
-    )(place, x, c_near, c_far, c_near_got, c_far_got)
+    )(place, x, near_upd, c_far, c_far_got)
     back = [swap_rep(to_x, 2), swap_rep(to_core, 1), swap_rep(to_both, 3)]
 
     uh, ul = call(

time: 63.7 us -> 63.2 us (level)
  waiting for transfers between devices: 18.3 us -> 17.4 us
    ppermute x4, waiting for transfers between devices: 3.2 us -> 2.34 us  [swap_y(): return lax.ppermute(x, 'bulk', [(k, k ^ 1) for k in range(8)])]
    pallas_call x1 -> x2, Pallas kernels: 1.28 us -> 1.71 us  [the longest x1 0.85 us: per_device(): call(near_kernel, shape(128, 256), [SMEM] + [VMEM] * 3, VMEM, [], 1000000...]
  transfers between devices with their start and end apart: 29 -> 29, of which waited for: 9 -> 9; matrix products, arithmetic and copies ran while one was open for 0% -> 0% of each run, Pallas kernels for 13% -> 14%
where the time goes in v9:
time: 63.2 us; the launch traced here: 63.1 us
  starting transfers between devices  29.3 us (46%)
  waiting for transfers between devices  17.4 us (28%)
  Pallas kernels  14.5 us (23%)
  local copies, waits for them, and re-layouts  1.59 us (3%)
    ppermute x7, starting transfers between devices, swap_z(): return lax.ppermute(x, 'bulk', [(k, k ^ 2 * m) for k in range(8)])  13.9 us
    ppermute x7, waiting for transfers between devices, swap_z(): return lax.ppermute(x, 'bulk', [(k, k ^ 2 * m) for k in range(8)])  10.7 us
    ppermute x15, starting transfers between devices, swap_rep(): return lax.ppermute(x, 'rep', [(k, k ^ bits) for k in range(4)])  8.21 us
    ppermute x4, starting transfers between devices, swap_y(): return lax.ppermute(x, 'bulk', [(k, k ^ 1) for k in range(8)])  5.72 us
    ppermute x15, waiting for transfers between devices, swap_rep(): return lax.ppermute(x, 'rep', [(k, k ^ bits) for k in range(4)])  3.97 us
    pallas_call x1, Pallas kernels, per_device(): call(first_kernel, shape(128, 1024), [SMEM] + [VMEM] * 18, VMEM, [pltpu.V...  3.59 us
    pallas_call x1, Pallas kernels, per_device(): call(second_factor_kernel, halves, [SMEM] + [VMEM] * 16, [VMEM] * 2, scra...  2.87 us
    pallas_call x1, Pallas kernels, per_device(): call(invert_kernel, shape(264, 128), [SMEM, VMEM, VMEM], VMEM, [], INVERT...  2.55 us
  transfers between devices with their start and end apart: 29, of which 9 were waited for; matrix products, arithmetic and copies ran while one was open for 0% of the time, Pallas kernels for 14%

profile of v9, /device:TPU:0, one launch (start us, length us, event | category | flops | bytes accessed | tf_op | source)
XLA Modules:
  0.0 63.1 jit_solution(14614438162562649590)
XLA Ops:
  0.1 0.9 %copy-done.1 = f32[256,128]{1,0:T(8,128)S(1)} copy-done((f32[256,128]{1,0:T(8,128)S(1)}, f32[256,128]{1,0:T(8,128)}, u32[]{:S(2)}) %copy-start.1) | copy-done | bytes 131096
  1.7 2.6 %invert.1 = f32[264,128]{1,0:T(8,128)S(1)} custom-call(s32[2]{0:T(128)S(1)} %pad_add_fusion.place_ref, f32[256,128]{1,0:T(8,128)S(1)} %copy-done.1, f32[2,128]{1,0:T(2,128)S(1)} %copy-done.2), custom_call_target="tpu_custom_call" | custom-call | flops 3500000000 | bytes 2097152 | tf_op jit(solution)/shard_map/invert/pallas_call | solution.py:358
  4.2 2.1 %collective-permute-start.1 = (f32[264,128]{1,0:T(8,128)S(1)}, f32[264,128]{1,0:T(8,128)S(1)}, u32[]{:S(2)}, u32[]{:S(2)}) collective-permute-start(f32[264,128]{1,0:T(8,128)S(1)} %invert.1), channel_id=1, source_target_pairs={{0,16},{4,20},{8,24},{12,28},{16,0},{20,4},{24,8},{28,12},{1,17},{... | collective-permute-start | bytes 405512 | tf_op jit(solution)/shard_map/ppermute | solution.py:307
  6.3 6.8 %collective-permute-done.1 = f32[264,128]{1,0:T(8,128)S(1)} collective-permute-done((f32[264,128]{1,0:T(8,128)S(1)}, f32[264,128]{1,0:T(8,128)S(1)}, u32[]{:S(2)}, u32[]{:S(2)}) %collective-permute-start.1) | collective-permute-done | bytes 135200 | tf_op jit(solution)/shard_map/ppermute | solution.py:307
  13.1 2.0 %collective-permute-start.8 = (f32[2,264,128]{2,1,0:T(8,128)S(1)}, f32[2,264,128]{2,1,0:T(8,128)S(1)}, u32[]{:S(2)}, u32[]{:S(2)}) collective-permute-start(f32[2,264,128]{2,1,0:T(8,128)S(1)} %pad_maximum_fusion.refs_0_), channel_id=1, source_target_pairs={{0,4},{4,0},{8,12},{12,8},{16,20},{20,16},{24,28},{28,24},{1,5},{5... | collective-permute-start | bytes 811016 | tf_op jit(solution)/shard_map/ppermute | solution.py:311
  15.2 1.5 %collective-permute-start.9 = (f32[2,264,128]{2,1,0:T(8,128)S(1)}, f32[2,264,128]{2,1,0:T(8,128)S(1)}, u32[]{:S(2)}, u32[]{:S(2)}) collective-permute-start(f32[2,264,128]{2,1,0:T(8,128)S(1)} %pad_maximum_fusion.refs_0_), channel_id=1, source_target_pairs={{0,2},{1,3},{2,0},{3,1},{4,6},{5,7},{6,4},{7,5},{8,10},{9,11},{10,... | collective-permute-start | bytes 811016 | tf_op jit(solution)/shard_map/ppermute | solution.py:315
  16.7 2.7 %collective-permute-start.7 = (f32[256,128]{1,0:T(8,128)S(1)}, f32[256,128]{1,0:T(8,128)S(1)}, u32[]{:S(2)}, u32[]{:S(2)}) collective-permute-start(f32[256,128]{1,0:T(8,128)S(1)} %copy-done.3), channel_id=1, source_target_pairs={{0,16},{4,20},{8,24},{12,28},{16,0},{20,4},{24,8},{28,12},{1,17},{... | collective-permute-start | bytes 393224 | tf_op jit(solution)/shard_map/ppermute | solution.py:307
  20.5 1.2 %collective-permute-start.14 = (f32[2,264,128]{2,1,0:T(8,128)S(1)}, f32[2,264,128]{2,1,0:T(8,128)S(1)}, u32[]{:S(2)}, u32[]{:S(2)}) collective-permute-start(f32[2,264,128]{2,1,0:T(8,128)S(1)} %collective-permute-done.8.refs_1_), channel_id=1, source_target_pairs={{0,2},{1,3},{2,0},{3,1},{4,6},{5,7},{6,4},{7,5},{8,10},{9,11},{10,... | collective-permute-start | bytes 811016 | tf_op jit(solution)/shard_map/ppermute | solution.py:315
  21.7 3.2 %collective-permute-done.7 = f32[256,128]{1,0:T(8,128)S(1)} collective-permute-done((f32[256,128]{1,0:T(8,128)S(1)}, f32[256,128]{1,0:T(8,128)S(1)}, u32[]{:S(2)}, u32[]{:S(2)}) %collective-permute-start.7) | collective-permute-done | bytes 131104 | tf_op jit(solution)/shard_map/ppermute | solution.py:307
  27.2 3.5 %collective-permute-start.3 = (f32[2,32,256]{2,1,0:T(8,128)S(1)}, f32[2,32,256]{2,1,0:T(8,128)S(1)}, u32[]{:S(2)}, u32[]{:S(2)}) collective-permute-start(f32[2,32,256]{2,1,0:T(8,128)S(1)} %get-tuple-element.39), channel_id=1, source_target_pairs={{0,8},{4,12},{8,0},{12,4},{16,24},{20,28},{24,16},{28,20},{1,9},{5... | collective-permute-start | bytes 196616 | tf_op jit(solution)/shard_map/ppermute | solution.py:307
  30.7 1.6 %collective-permute-start.4 = (f32[2,32,256]{2,1,0:T(8,128)S(1)}, f32[2,32,256]{2,1,0:T(8,128)S(1)}, u32[]{:S(2)}, u32[]{:S(2)}) collective-permute-start(f32[2,32,256]{2,1,0:T(8,128)S(1)} %get-tuple-element.41), channel_id=1, source_target_pairs={{0,16},{4,20},{8,24},{12,28},{16,0},{20,4},{24,8},{28,12},{1,17},{... | collective-permute-start | bytes 196616 | tf_op jit(solution)/shard_map/ppermute | solution.py:307
  32.3 1.0 %collective-permute-start.5 = (f32[2,32,256]{2,1,0:T(8,128)S(1)}, f32[2,32,256]{2,1,0:T(8,128)S(1)}, u32[]{:S(2)}, u32[]{:S(2)}) collective-permute-start(f32[2,32,256]{2,1,0:T(8,128)S(1)} %get-tuple-element.43), channel_id=1, source_target_pairs={{0,24},{4,28},{8,16},{12,20},{16,8},{20,12},{24,0},{28,4},{1,25},{... | collective-permute-start | bytes 196616 | tf_op jit(solution)/shard_map/ppermute | solution.py:307
  33.8 1.5 %collective-permute-start.13 = (f32[2,256,128]{2,1,0:T(8,128)S(1)}, f32[2,256,128]{2,1,0:T(8,128)S(1)}, u32[]{:S(2)}, u32[]{:S(2)}) collective-permute-start(f32[2,256,128]{2,1,0:T(8,128)S(1)} %pad_maximum_fusion.2.held), channel_id=1, source_target_pairs={{0,4},{4,0},{8,12},{12,8},{16,20},{20,16},{24,28},{28,24},{1,5},{5... | collective-permute-start | bytes 786440 | tf_op jit(solution)/shard_map/ppermute | solution.py:311
  35.3 3.0 %collective-permute-start.11 = (f32[2,256,128]{2,1,0:T(8,128)S(1)}, f32[2,256,128]{2,1,0:T(8,128)S(1)}, u32[]{:S(2)}, u32[]{:S(2)}) collective-permute-start(f32[2,256,128]{2,1,0:T(8,128)S(1)} %pad_maximum_fusion.2.held), channel_id=1, source_target_pairs={{0,8},{4,12},{8,0},{12,4},{16,24},{20,28},{24,16},{28,20},{1,9},{5... | collective-permute-start | bytes 786440 | tf_op jit(solution)/shard_map/ppermute | solution.py:307
  39.3 1.4 %collective-permute-start.6 = (f32[32,1024]{1,0:T(8,128)S(1)}, f32[32,1024]{1,0:T(8,128)S(1)}, u32[]{:S(2)}, u32[]{:S(2)}) collective-permute-start(f32[32,1024]{1,0:T(8,128)S(1)} %get-tuple-element.45), channel_id=1, source_target_pairs={{0,2},{1,3},{2,0},{3,1},{4,6},{5,7},{6,4},{7,5},{8,10},{9,11},{10,... | collective-permute-start | bytes 393224 | tf_op jit(solution)/shard_map/ppermute | solution.py:315
  41.3 3.1 %collective-permute-done.6 = f32[32,1024]{1,0:T(8,128)S(1)} collective-permute-done((f32[32,1024]{1,0:T(8,128)S(1)}, f32[32,1024]{1,0:T(8,128)S(1)}, u32[]{:S(2)}, u32[]{:S(2)}) %collective-permute-start.6) | collective-permute-done | bytes 131104 | tf_op jit(solution)/shard_map/ppermute | solution.py:315
  46.7 1.6 %collective-permute-start.25 = (f32[2,256,128]{2,1,0:T(8,128)S(1)}, f32[2,256,128]{2,1,0:T(8,128)S(1)}, u32[]{:S(2)}, u32[]{:S(2)}) collective-permute-start(f32[2,256,128]{2,1,0:T(8,128)S(1)} %collective-permute-done.11.held), channel_id=1, source_target_pairs={{0,4},{4,0},{8,12},{12,8},{16,20},{20,16},{24,28},{28,24},{1,5},{5... | collective-permute-start | bytes 786440 | tf_op jit(solution)/shard_map/ppermute | solution.py:311
  48.3 3.6 %first_panel.1.x_ref = f32[128,1024]{1,0:T(8,128)S(1)} custom-call(s32[2]{0:T(128)S(1)} %pad_add_fusion.place_ref, f32[2,32,1024]{2,1,0:T(8,128)S(1)} %pad_maximum_fusion.1.pair, f32[2,32,1024]{2,1,0:T(8,128)S(1)} %collective-permute-done.12.other_pair, f32[2,264,128]{2,1,0:T(8,128)S(1)} %pad_maximum_fusion.refs_0_, ...), custom_call_target="tpu_custom_call" | custom-call | flops 200000000 | bytes 2097152 | tf_op jit(solution)/shard_map/first_panel/pallas_call | solution.py:402
  51.9 0.9 %near_update.1.near = f32[128,256]{1,0:T(8,128)S(1)} custom-call(s32[2]{0:T(128)S(1)} %pad_add_fusion.place_ref, f32[128,1024]{1,0:T(8,128)S(1)} %first_panel.1.x_ref, f32[2,256,128]{2,1,0:T(8,128)S(1)} %pad_maximum_fusion.2.held, f32[2,256,128]{2,1,0:T(8,128)S(1)} %collective-permute-done.13.got), custom_call_target="tpu_custom_call" | custom-call | flops 10000000 | bytes 2097152 | tf_op jit(solution)/shard_map/near_update/pallas_call | solution.py:413
  52.8 2.3 %collective-permute-done.25.got = f32[2,256,128]{2,1,0:T(8,128)S(1)} collective-permute-done((f32[2,256,128]{2,1,0:T(8,128)S(1)}, f32[2,256,128]{2,1,0:T(8,128)S(1)}, u32[]{:S(2)}, u32[]{:S(2)}) %collective-permute-start.25) | collective-permute-done | bytes 262176 | tf_op jit(solution)/shard_map/ppermute | solution.py:311
  55.0 0.9 %update.1 = (f32[32,256]{1,0:T(8,128)S(1)}, f32[32,256]{1,0:T(8,128)S(1)}, f32[32,256]{1,0:T(8,128)S(1)}, f32[32,256]{1,0:T(8,128)S(1)}) custom-call(s32[2]{0:T(128)S(1)} %pad_add_fusion.place_ref, f32[128,1024]{1,0:T(8,128)S(1)} %first_panel.1.x_ref, f32[128,256]{1,0:T(8,128)S(1)} %near_update.1.near, f32[2,256,128]{2,1,0:T(8,128)S(1)} %collective-permute-done.11.held, ...), custom_call_target="tpu_custom_call" | custom-call | flops 2000000000 | bytes 2097152 | tf_op jit(solution)/shard_map/update/pallas_call | solution.py:416
  55.9 1.4 %collective-permute-start.26 = (f32[32,256]{1,0:T(8,128)S(1)}, f32[32,256]{1,0:T(8,128)S(1)}, u32[]{:S(2)}, u32[]{:S(2)}) collective-permute-start(f32[32,256]{1,0:T(8,128)S(1)} %get-tuple-element.66), channel_id=1, source_target_pairs={{0,2},{1,3},{2,0},{3,1},{4,6},{5,7},{6,4},{7,5},{8,10},{9,11},{10,... | collective-permute-start | bytes 98312 | tf_op jit(solution)/shard_map/ppermute | solution.py:315
  58.1 2.9 %second_factor.1 = (bf16[1024,1024]{1,0:T(8,128)(2,1)S(1)}, bf16[1024,1024]{1,0:T(8,128)(2,1)S(1)}) custom-call(s32[2]{0:T(128)S(1)} %pad_add_fusion.place_ref, f32[2,264,128]{2,1,0:T(8,128)S(1)} %pad_maximum_fusion.refs_0_, f32[2,264,128]{2,1,0:T(8,128)S(1)} %collective-permute-done.8.refs_1_, f32[2,264,128]{2,1,0:T(8,128)S(1)} %collective-permute-done.9.refs_2_, ...), custom_call_target="tpu_custom_call" | custom-call | flops 3000000000 | bytes 2097152 | tf_op jit(solution)/shard_map/second_factor/pallas_call | solution.py:428
  61.0 2.1 %second_panel.1 = f32[32,2048]{1,0:T(8,128)} custom-call(s32[2]{0:T(128)S(1)} %pad_add_fusion.place_ref, f32[128,1024]{1,0:T(8,128)S(1)} %first_panel.1.x_ref, f32[2,32,1024]{2,1,0:T(8,128)S(1)} %get-tuple-element.61.both_ref, bf16[1024,1024]{1,0:T(8,128)(2,1)S(1)} %get-tuple-element.64.uh_ref, bf16[1024,1024]{1,0:T(8,128)(2,1)S(1)} %get-tuple-element.65.ul_ref, ...), custom_call_target="tpu_custom_call" | custom-call | flops 2500000000 | bytes 2097152 | tf_op jit(solution)/shard_map/second_panel/pallas_call | solution.py:432
  (55 shorter events, 9.4 us)
Async XLA Ops:
  4.2 8.9 %collective-permute-start.1 = (f32[264,128]{1,0:T(8,128)S(1)}, f32[264,128]{1,0:T(8,128)S(1)}, u32[]{:S(2)}, u32[]{:S(2)}) collective-permute-start(f32[264,128]{1,0:T(8,128)S(1)} %invert.1), channel_id=1, source_target_pairs={{0,16},{4,20},{8,24},{12,28},{16,0},{20,4},{24,8},{28,12},{1,17},{... | collective-permute-start | bytes 405512 | tf_op jit(solution)/shard_map/ppermute | solution.py:307
  13.1 7.4 %collective-permute-start.8 = (f32[2,264,128]{2,1,0:T(8,128)S(1)}, f32[2,264,128]{2,1,0:T(8,128)S(1)}, u32[]{:S(2)}, u32[]{:S(2)}) collective-permute-start(f32[2,264,128]{2,1,0:T(8,128)S(1)} %pad_maximum_fusion.refs_0_), channel_id=1, source_target_pairs={{0,4},{4,0},{8,12},{12,8},{16,20},{20,16},{24,28},{28,24},{1,5},{5... | collective-permute-start | bytes 811016 | tf_op jit(solution)/shard_map/ppermute | solution.py:311
  15.2 9.8 %collective-permute-start.9 = (f32[2,264,128]{2,1,0:T(8,128)S(1)}, f32[2,264,128]{2,1,0:T(8,128)S(1)}, u32[]{:S(2)}, u32[]{:S(2)}) collective-permute-start(f32[2,264,128]{2,1,0:T(8,128)S(1)} %pad_maximum_fusion.refs_0_), channel_id=1, source_target_pairs={{0,2},{1,3},{2,0},{3,1},{4,6},{5,7},{6,4},{7,5},{8,10},{9,11},{10,... | collective-permute-start | bytes 811016 | tf_op jit(solution)/shard_map/ppermute | solution.py:315
  16.7 9.0 %collective-permute-start.2 = (f32[2,264,128]{2,1,0:T(8,128)S(1)}, f32[2,264,128]{2,1,0:T(8,128)S(1)}, u32[]{:S(2)}, u32[]{:S(2)}) collective-permute-start(f32[2,264,128]{2,1,0:T(8,128)S(1)} %pad_maximum_fusion.refs_0_), channel_id=1, source_target_pairs={{0,8},{4,12},{8,0},{12,4},{16,24},{20,28},{24,16},{28,20},{1,9},{5... | collective-permute-start | bytes 811016 | tf_op jit(solution)/shard_map/ppermute | solution.py:307
  16.7 8.2 %collective-permute-start.7 = (f32[256,128]{1,0:T(8,128)S(1)}, f32[256,128]{1,0:T(8,128)S(1)}, u32[]{:S(2)}, u32[]{:S(2)}) collective-permute-start(f32[256,128]{1,0:T(8,128)S(1)} %copy-done.3), channel_id=1, source_target_pairs={{0,16},{4,20},{8,24},{12,28},{16,0},{20,4},{24,8},{28,12},{1,17},{... | collective-permute-start | bytes 393224 | tf_op jit(solution)/shard_map/ppermute | solution.py:307
  19.9 5.0 %collective-permute-start = (f32[4,32,256]{2,1,0:T(8,128)S(1)}, f32[4,32,256]{2,1,0:T(8,128)S(1)}, u32[]{:S(2)}, u32[]{:S(2)}) collective-permute-start(f32[4,32,256]{2,1,0:T(8,128)S(1)} %leave.1), channel_id=1, source_target_pairs={{0,4},{4,0},{8,12},{12,8},{16,20},{20,16},{24,28},{28,24},{1,5},{5... | collective-permute-start | bytes 393224 | tf_op jit(solution)/shard_map/ppermute | solution.py:311
  20.5 11.8 %collective-permute-start.14 = (f32[2,264,128]{2,1,0:T(8,128)S(1)}, f32[2,264,128]{2,1,0:T(8,128)S(1)}, u32[]{:S(2)}, u32[]{:S(2)}) collective-permute-start(f32[2,264,128]{2,1,0:T(8,128)S(1)} %collective-permute-done.8.refs_1_), channel_id=1, source_target_pairs={{0,2},{1,3},{2,0},{3,1},{4,6},{5,7},{6,4},{7,5},{8,10},{9,11},{10,... | collective-permute-start | bytes 811016 | tf_op jit(solution)/shard_map/ppermute | solution.py:315
  25.6 8.1 %collective-permute-start.10 = (f32[2,264,128]{2,1,0:T(8,128)S(1)}, f32[2,264,128]{2,1,0:T(8,128)S(1)}, u32[]{:S(2)}, u32[]{:S(2)}) collective-permute-start(f32[2,264,128]{2,1,0:T(8,128)S(1)} %collective-permute-done.2.refs_4_), channel_id=1, source_target_pairs={{0,2},{4,6},{8,10},{12,14},{16,18},{20,22},{24,26},{28,30},{1,5},{... | collective-permute-start | bytes 811016 | tf_op jit(solution)/shard_map/ppermute | solution.py:324
  26.3 9.0 %collective-permute-start.15 = (f32[2,264,128]{2,1,0:T(8,128)S(1)}, f32[2,264,128]{2,1,0:T(8,128)S(1)}, u32[]{:S(2)}, u32[]{:S(2)}) collective-permute-start(f32[2,264,128]{2,1,0:T(8,128)S(1)} %collective-permute-done.2.refs_4_), channel_id=1, source_target_pairs={{0,4},{4,0},{8,12},{12,8},{16,20},{20,16},{24,28},{28,24},{1,3},{5... | collective-permute-start | bytes 811016 | tf_op jit(solution)/shard_map/ppermute | solution.py:324
  27.2 11.0 %collective-permute-start.3 = (f32[2,32,256]{2,1,0:T(8,128)S(1)}, f32[2,32,256]{2,1,0:T(8,128)S(1)}, u32[]{:S(2)}, u32[]{:S(2)}) collective-permute-start(f32[2,32,256]{2,1,0:T(8,128)S(1)} %get-tuple-element.39), channel_id=1, source_target_pairs={{0,8},{4,12},{8,0},{12,4},{16,24},{20,28},{24,16},{28,20},{1,9},{5... | collective-permute-start | bytes 196616 | tf_op jit(solution)/shard_map/ppermute | solution.py:307
  30.7 8.0 %collective-permute-start.4 = (f32[2,32,256]{2,1,0:T(8,128)S(1)}, f32[2,32,256]{2,1,0:T(8,128)S(1)}, u32[]{:S(2)}, u32[]{:S(2)}) collective-permute-start(f32[2,32,256]{2,1,0:T(8,128)S(1)} %get-tuple-element.41), channel_id=1, source_target_pairs={{0,16},{4,20},{8,24},{12,28},{16,0},{20,4},{24,8},{28,12},{1,17},{... | collective-permute-start | bytes 196616 | tf_op jit(solution)/shard_map/ppermute | solution.py:307
  32.3 6.4 %collective-permute-start.5 = (f32[2,32,256]{2,1,0:T(8,128)S(1)}, f32[2,32,256]{2,1,0:T(8,128)S(1)}, u32[]{:S(2)}, u32[]{:S(2)}) collective-permute-start(f32[2,32,256]{2,1,0:T(8,128)S(1)} %get-tuple-element.43), channel_id=1, source_target_pairs={{0,24},{4,28},{8,16},{12,20},{16,8},{20,12},{24,0},{28,4},{1,25},{... | collective-permute-start | bytes 196616 | tf_op jit(solution)/shard_map/ppermute | solution.py:307
  33.8 7.0 %collective-permute-start.13 = (f32[2,256,128]{2,1,0:T(8,128)S(1)}, f32[2,256,128]{2,1,0:T(8,128)S(1)}, u32[]{:S(2)}, u32[]{:S(2)}) collective-permute-start(f32[2,256,128]{2,1,0:T(8,128)S(1)} %pad_maximum_fusion.2.held), channel_id=1, source_target_pairs={{0,4},{4,0},{8,12},{12,8},{16,20},{20,16},{24,28},{28,24},{1,5},{5... | collective-permute-start | bytes 786440 | tf_op jit(solution)/shard_map/ppermute | solution.py:311
  35.3 9.1 %collective-permute-start.11 = (f32[2,256,128]{2,1,0:T(8,128)S(1)}, f32[2,256,128]{2,1,0:T(8,128)S(1)}, u32[]{:S(2)}, u32[]{:S(2)}) collective-permute-start(f32[2,256,128]{2,1,0:T(8,128)S(1)} %pad_maximum_fusion.2.held), channel_id=1, source_target_pairs={{0,8},{4,12},{8,0},{12,4},{16,24},{20,28},{24,16},{28,20},{1,9},{5... | collective-permute-start | bytes 786440 | tf_op jit(solution)/shard_map/ppermute | solution.py:307
  38.2 6.7 %collective-permute-start.16 = (f32[2,264,128]{2,1,0:T(8,128)S(1)}, f32[2,264,128]{2,1,0:T(8,128)S(1)}, u32[]{:S(2)}, u32[]{:S(2)}) collective-permute-start(f32[2,264,128]{2,1,0:T(8,128)S(1)} %collective-permute-done.10.refs_5_), channel_id=1, source_target_pairs={{0,4},{4,0},{8,12},{12,8},{16,20},{20,16},{24,28},{28,24},{1,3},{5... | collective-permute-start | bytes 811016 | tf_op jit(solution)/shard_map/ppermute | solution.py:324
  39.3 5.0 %collective-permute-start.6 = (f32[32,1024]{1,0:T(8,128)S(1)}, f32[32,1024]{1,0:T(8,128)S(1)}, u32[]{:S(2)}, u32[]{:S(2)}) collective-permute-start(f32[32,1024]{1,0:T(8,128)S(1)} %get-tuple-element.45), channel_id=1, source_target_pairs={{0,2},{1,3},{2,0},{3,1},{4,6},{5,7},{6,4},{7,5},{8,10},{9,11},{10,... | collective-permute-start | bytes 393224 | tf_op jit(solution)/shard_map/ppermute | solution.py:315
  40.7 4.3 %collective-permute-start.17 = (f32[2,264,128]{2,1,0:T(8,128)S(1)}, f32[2,264,128]{2,1,0:T(8,128)S(1)}, u32[]{:S(2)}, u32[]{:S(2)}) collective-permute-start(f32[2,264,128]{2,1,0:T(8,128)S(1)} %pad_maximum_fusion.refs_0_), channel_id=1, source_target_pairs={{0,1},{1,0},{2,3},{3,2},{4,5},{5,4},{6,7},{7,6},{8,9},{9,8},{10,11... | collective-permute-start | bytes 811016 | tf_op jit(solution)/shard_map/ppermute | solution.py:315
  40.7 4.8 %collective-permute-start.18 = (f32[2,264,128]{2,1,0:T(8,128)S(1)}, f32[2,264,128]{2,1,0:T(8,128)S(1)}, u32[]{:S(2)}, u32[]{:S(2)}) collective-permute-start(f32[2,264,128]{2,1,0:T(8,128)S(1)} %collective-permute-done.8.refs_1_), channel_id=1, source_target_pairs={{0,1},{1,0},{2,3},{3,2},{4,5},{5,4},{6,7},{7,6},{8,9},{9,8},{10,11... | collective-permute-start | bytes 811016 | tf_op jit(solution)/shard_map/ppermute | solution.py:315
  45.0 3.3 %collective-permute-start.21 = (f32[2,264,128]{2,1,0:T(8,128)S(1)}, f32[2,264,128]{2,1,0:T(8,128)S(1)}, u32[]{:S(2)}, u32[]{:S(2)}) collective-permute-start(f32[2,264,128]{2,1,0:T(8,128)S(1)} %collective-permute-done.2.refs_4_), channel_id=1, source_target_pairs={{0,1},{1,0},{2,3},{3,2},{4,5},{5,4},{6,7},{7,6},{8,9},{9,8},{10,11... | collective-permute-start | bytes 811016 | tf_op jit(solution)/shard_map/ppermute | solution.py:315
  45.5 2.8 %collective-permute-start.22 = (f32[2,264,128]{2,1,0:T(8,128)S(1)}, f32[2,264,128]{2,1,0:T(8,128)S(1)}, u32[]{:S(2)}, u32[]{:S(2)}) collective-permute-start(f32[2,264,128]{2,1,0:T(8,128)S(1)} %collective-permute-done.10.refs_5_), channel_id=1, source_target_pairs={{0,1},{1,0},{2,3},{3,2},{4,5},{5,4},{6,7},{7,6},{8,9},{9,8},{10,11... | collective-permute-start | bytes 811016 | tf_op jit(solution)/shard_map/ppermute | solution.py:315
  46.7 8.4 %collective-permute-start.25 = (f32[2,256,128]{2,1,0:T(8,128)S(1)}, f32[2,256,128]{2,1,0:T(8,128)S(1)}, u32[]{:S(2)}, u32[]{:S(2)}) collective-permute-start(f32[2,256,128]{2,1,0:T(8,128)S(1)} %collective-permute-done.11.held), channel_id=1, source_target_pairs={{0,4},{4,0},{8,12},{12,8},{16,20},{20,16},{24,28},{28,24},{1,5},{5... | collective-permute-start | bytes 786440 | tf_op jit(solution)/shard_map/ppermute | solution.py:311
  55.9 5.1 %collective-permute-start.26 = (f32[32,256]{1,0:T(8,128)S(1)}, f32[32,256]{1,0:T(8,128)S(1)}, u32[]{:S(2)}, u32[]{:S(2)}) collective-permute-start(f32[32,256]{1,0:T(8,128)S(1)} %get-tuple-element.66), channel_id=1, source_target_pairs={{0,2},{1,3},{2,0},{3,1},{4,6},{5,7},{6,4},{7,5},{8,10},{9,11},{10,... | collective-permute-start | bytes 98312 | tf_op jit(solution)/shard_map/ppermute | solution.py:315
  57.3 3.7 %collective-permute-start.27 = (f32[32,256]{1,0:T(8,128)S(1)}, f32[32,256]{1,0:T(8,128)S(1)}, u32[]{:S(2)}, u32[]{:S(2)}) collective-permute-start(f32[32,256]{1,0:T(8,128)S(1)} %get-tuple-element.67), channel_id=1, source_target_pairs={{0,1},{1,0},{2,3},{3,2},{4,5},{5,4},{6,7},{7,6},{8,9},{9,8},{10,11... | collective-permute-start | bytes 98312 | tf_op jit(solution)/shard_map/ppermute | solution.py:315
  57.3 3.7 %collective-permute-start.28 = (f32[32,256]{1,0:T(8,128)S(1)}, f32[32,256]{1,0:T(8,128)S(1)}, u32[]{:S(2)}, u32[]{:S(2)}) collective-permute-start(f32[32,256]{1,0:T(8,128)S(1)} %get-tuple-element.68), channel_id=1, source_target_pairs={{0,3},{1,2},{2,1},{3,0},{4,7},{5,6},{6,5},{7,4},{8,11},{9,10},{10,... | collective-permute-start | bytes 98312 | tf_op jit(solution)/shard_map/ppermute | solution.py:315
  (9 other events, 43.9 us)

commit v10 on v9

--- a/solution.py
+++ b/solution.py
@@ -273,9 +273,12 @@
         put(at + 256, at, (jnp.zeros((256, 256), BF16),) * 2)
 
 
-def second_kernel(place_ref, x_ref, both_ref, uh_ref, ul_ref, mine, from_x, from_core, from_both, out_ref):
-    x = x_ref[0:32, :]
-    out_ref[:, 0:1024] = x
+def second_kernel(place_ref, x_ref, both_ref, uh_ref, ul_ref, mine, from_x, from_core, from_both, out_ref, buf, sem):
+    first = pltpu.make_async_copy(x_ref.at[pl.ds(0, 32)], out_ref.at[:, pl.ds(0, 1024)], sem.at[0])
+    first.start()
+    halves = [
+        pltpu.make_async_copy(buf.at[k], out_ref.at[:, pl.ds(1024 + 512 * k, 512)], sem.at[1 + k]) for k in range(2)
+    ]
     parts = []
     for k in range(4):
         way = place_ref[0] ^ k
@@ -293,9 +296,13 @@
         return uh_ref[rows, cols], ul_ref[rows, cols]
 
     xa = mul(ra, u(0, 0))
+    buf[0] = xa
+    halves[0].start()
     xb = mul(rb - mul(xa, u(0, 1)), u(1, 1))
-    out_ref[:, 1024:1536] = xa
-    out_ref[:, 1536:2048] = xb
+    buf[1] = xb
+    halves[1].start()
+    for copy in [first] + halves:
+        copy.wait()
 
 
 BOTH = ("bulk", "rep")
@@ -344,6 +351,9 @@
         cost_estimate=pl.CostEstimate(flops=flops, bytes_accessed=2 << 20, transcendentals=0),
         name=name,
     )
+
+
+OUT_SCRATCH = [pltpu.VMEM((2, 32, 512), F32), pltpu.SemaphoreType.DMA((3,))]
 
 
 def shape(*dims, dtype=F32):
@@ -429,7 +439,7 @@
         second_factor_kernel, halves, [SMEM] + [VMEM] * 16, [VMEM] * 2, scratch, SECOND, 24, "second_factor"
     )(after(place, mine), *bufs)
 
-    return call(second_kernel, shape(32, 2048), [SMEM] + [VMEM] * 8, VMEM, [], 2_500_000_000, 24, "second_panel")(
+    return call(second_kernel, shape(32, 2048), [SMEM] + [VMEM] * 8, ANY, OUT_SCRATCH, 2_500_000_000, 24, "second_panel")(
         place, x, both, uh, ul, mine, *back
     )
 

time: 63.2 us -> 63.2 us (level)
  no operation moved by 1% of the time
where the time goes in v10:
time: 63.2 us; the launch traced here: 63 us
  starting transfers between devices  29.3 us (46%)
  waiting for transfers between devices  17.4 us (28%)
  Pallas kernels  14.4 us (23%)
  local copies, waits for them, and re-layouts  1.59 us (3%)
    ppermute x7, starting transfers between devices, swap_z(): return lax.ppermute(x, 'bulk', [(k, k ^ 2 * m) for k in range(8)])  13.9 us
    ppermute x7, waiting for transfers between devices, swap_z(): return lax.ppermute(x, 'bulk', [(k, k ^ 2 * m) for k in range(8)])  10.7 us
    ppermute x15, starting transfers between devices, swap_rep(): return lax.ppermute(x, 'rep', [(k, k ^ bits) for k in range(4)])  8.21 us
    ppermute x4, starting transfers between devices, swap_y(): return lax.ppermute(x, 'bulk', [(k, k ^ 1) for k in range(8)])  5.72 us
    ppermute x15, waiting for transfers between devices, swap_rep(): return lax.ppermute(x, 'rep', [(k, k ^ bits) for k in range(4)])  3.97 us
    pallas_call x1, Pallas kernels, per_device(): call(first_kernel, shape(128, 1024), [SMEM] + [VMEM] * 18, VMEM, [pltpu.V...  3.59 us
    pallas_call x1, Pallas kernels, per_device(): call(second_factor_kernel, halves, [SMEM] + [VMEM] * 16, [VMEM] * 2, scra...  2.87 us
    pallas_call x1, Pallas kernels, per_device(): call(invert_kernel, shape(264, 128), [SMEM, VMEM, VMEM], VMEM, [], INVERT...  2.55 us
  transfers between devices with their start and end apart: 29, of which 9 were waited for; matrix products, arithmetic and copies ran while one was open for 0% of the time, Pallas kernels for 14%

profile of v10, /device:TPU:0, one launch (start us, length us, event | category | flops | bytes accessed | tf_op | source)
XLA Modules:
  0.0 63.0 jit_solution(16684142181195503688)
XLA Ops:
  0.1 0.9 %copy-done.1 = f32[256,128]{1,0:T(8,128)S(1)} copy-done((f32[256,128]{1,0:T(8,128)S(1)}, f32[256,128]{1,0:T(8,128)}, u32[]{:S(2)}) %copy-start.1) | copy-done | bytes 131096
  1.7 2.6 %invert.1 = f32[264,128]{1,0:T(8,128)S(1)} custom-call(s32[2]{0:T(128)S(1)} %pad_add_fusion.place_ref, f32[256,128]{1,0:T(8,128)S(1)} %copy-done.1, f32[2,128]{1,0:T(2,128)S(1)} %copy-done.2), custom_call_target="tpu_custom_call" | custom-call | flops 3500000000 | bytes 2097152 | tf_op jit(solution)/shard_map/invert/pallas_call | solution.py:368
  4.2 2.1 %collective-permute-start.1 = (f32[264,128]{1,0:T(8,128)S(1)}, f32[264,128]{1,0:T(8,128)S(1)}, u32[]{:S(2)}, u32[]{:S(2)}) collective-permute-start(f32[264,128]{1,0:T(8,128)S(1)} %invert.1), channel_id=1, source_target_pairs={{0,16},{4,20},{8,24},{12,28},{16,0},{20,4},{24,8},{28,12},{1,17},{... | collective-permute-start | bytes 405512 | tf_op jit(solution)/shard_map/ppermute | solution.py:314
  6.3 6.8 %collective-permute-done.1 = f32[264,128]{1,0:T(8,128)S(1)} collective-permute-done((f32[264,128]{1,0:T(8,128)S(1)}, f32[264,128]{1,0:T(8,128)S(1)}, u32[]{:S(2)}, u32[]{:S(2)}) %collective-permute-start.1) | collective-permute-done | bytes 135200 | tf_op jit(solution)/shard_map/ppermute | solution.py:314
  13.1 2.0 %collective-permute-start.8 = (f32[2,264,128]{2,1,0:T(8,128)S(1)}, f32[2,264,128]{2,1,0:T(8,128)S(1)}, u32[]{:S(2)}, u32[]{:S(2)}) collective-permute-start(f32[2,264,128]{2,1,0:T(8,128)S(1)} %pad_maximum_fusion.refs_0_), channel_id=1, source_target_pairs={{0,4},{4,0},{8,12},{12,8},{16,20},{20,16},{24,28},{28,24},{1,5},{5... | collective-permute-start | bytes 811016 | tf_op jit(solution)/shard_map/ppermute | solution.py:318
  15.2 1.5 %collective-permute-start.9 = (f32[2,264,128]{2,1,0:T(8,128)S(1)}, f32[2,264,128]{2,1,0:T(8,128)S(1)}, u32[]{:S(2)}, u32[]{:S(2)}) collective-permute-start(f32[2,264,128]{2,1,0:T(8,128)S(1)} %pad_maximum_fusion.refs_0_), channel_id=1, source_target_pairs={{0,2},{1,3},{2,0},{3,1},{4,6},{5,7},{6,4},{7,5},{8,10},{9,11},{10,... | collective-permute-start | bytes 811016 | tf_op jit(solution)/shard_map/ppermute | solution.py:322
  16.7 2.7 %collective-permute-start.7 = (f32[256,128]{1,0:T(8,128)S(1)}, f32[256,128]{1,0:T(8,128)S(1)}, u32[]{:S(2)}, u32[]{:S(2)}) collective-permute-start(f32[256,128]{1,0:T(8,128)S(1)} %copy-done.3), channel_id=1, source_target_pairs={{0,16},{4,20},{8,24},{12,28},{16,0},{20,4},{24,8},{28,12},{1,17},{... | collective-permute-start | bytes 393224 | tf_op jit(solution)/shard_map/ppermute | solution.py:314
  20.5 1.2 %collective-permute-start.14 = (f32[2,264,128]{2,1,0:T(8,128)S(1)}, f32[2,264,128]{2,1,0:T(8,128)S(1)}, u32[]{:S(2)}, u32[]{:S(2)}) collective-permute-start(f32[2,264,128]{2,1,0:T(8,128)S(1)} %collective-permute-done.8.refs_1_), channel_id=1, source_target_pairs={{0,2},{1,3},{2,0},{3,1},{4,6},{5,7},{6,4},{7,5},{8,10},{9,11},{10,... | collective-permute-start | bytes 811016 | tf_op jit(solution)/shard_map/ppermute | solution.py:322
  21.7 3.2 %collective-permute-done.7 = f32[256,128]{1,0:T(8,128)S(1)} collective-permute-done((f32[256,128]{1,0:T(8,128)S(1)}, f32[256,128]{1,0:T(8,128)S(1)}, u32[]{:S(2)}, u32[]{:S(2)}) %collective-permute-start.7) | collective-permute-done | bytes 131104 | tf_op jit(solution)/shard_map/ppermute | solution.py:314
  27.2 3.5 %collective-permute-start.3 = (f32[2,32,256]{2,1,0:T(8,128)S(1)}, f32[2,32,256]{2,1,0:T(8,128)S(1)}, u32[]{:S(2)}, u32[]{:S(2)}) collective-permute-start(f32[2,32,256]{2,1,0:T(8,128)S(1)} %get-tuple-element.39), channel_id=1, source_target_pairs={{0,8},{4,12},{8,0},{12,4},{16,24},{20,28},{24,16},{28,20},{1,9},{5... | collective-permute-start | bytes 196616 | tf_op jit(solution)/shard_map/ppermute | solution.py:314
  30.7 1.6 %collective-permute-start.4 = (f32[2,32,256]{2,1,0:T(8,128)S(1)}, f32[2,32,256]{2,1,0:T(8,128)S(1)}, u32[]{:S(2)}, u32[]{:S(2)}) collective-permute-start(f32[2,32,256]{2,1,0:T(8,128)S(1)} %get-tuple-element.41), channel_id=1, source_target_pairs={{0,16},{4,20},{8,24},{12,28},{16,0},{20,4},{24,8},{28,12},{1,17},{... | collective-permute-start | bytes 196616 | tf_op jit(solution)/shard_map/ppermute | solution.py:314
  32.3 1.0 %collective-permute-start.5 = (f32[2,32,256]{2,1,0:T(8,128)S(1)}, f32[2,32,256]{2,1,0:T(8,128)S(1)}, u32[]{:S(2)}, u32[]{:S(2)}) collective-permute-start(f32[2,32,256]{2,1,0:T(8,128)S(1)} %get-tuple-element.43), channel_id=1, source_target_pairs={{0,24},{4,28},{8,16},{12,20},{16,8},{20,12},{24,0},{28,4},{1,25},{... | collective-permute-start | bytes 196616 | tf_op jit(solution)/shard_map/ppermute | solution.py:314
  33.8 1.5 %collective-permute-start.13 = (f32[2,256,128]{2,1,0:T(8,128)S(1)}, f32[2,256,128]{2,1,0:T(8,128)S(1)}, u32[]{:S(2)}, u32[]{:S(2)}) collective-permute-start(f32[2,256,128]{2,1,0:T(8,128)S(1)} %pad_maximum_fusion.2.held), channel_id=1, source_target_pairs={{0,4},{4,0},{8,12},{12,8},{16,20},{20,16},{24,28},{28,24},{1,5},{5... | collective-permute-start | bytes 786440 | tf_op jit(solution)/shard_map/ppermute | solution.py:318
  35.3 3.0 %collective-permute-start.11 = (f32[2,256,128]{2,1,0:T(8,128)S(1)}, f32[2,256,128]{2,1,0:T(8,128)S(1)}, u32[]{:S(2)}, u32[]{:S(2)}) collective-permute-start(f32[2,256,128]{2,1,0:T(8,128)S(1)} %pad_maximum_fusion.2.held), channel_id=1, source_target_pairs={{0,8},{4,12},{8,0},{12,4},{16,24},{20,28},{24,16},{28,20},{1,9},{5... | collective-permute-start | bytes 786440 | tf_op jit(solution)/shard_map/ppermute | solution.py:314
  39.3 1.4 %collective-permute-start.6 = (f32[32,1024]{1,0:T(8,128)S(1)}, f32[32,1024]{1,0:T(8,128)S(1)}, u32[]{:S(2)}, u32[]{:S(2)}) collective-permute-start(f32[32,1024]{1,0:T(8,128)S(1)} %get-tuple-element.45), channel_id=1, source_target_pairs={{0,2},{1,3},{2,0},{3,1},{4,6},{5,7},{6,4},{7,5},{8,10},{9,11},{10,... | collective-permute-start | bytes 393224 | tf_op jit(solution)/shard_map/ppermute | solution.py:322
  41.3 3.1 %collective-permute-done.6 = f32[32,1024]{1,0:T(8,128)S(1)} collective-permute-done((f32[32,1024]{1,0:T(8,128)S(1)}, f32[32,1024]{1,0:T(8,128)S(1)}, u32[]{:S(2)}, u32[]{:S(2)}) %collective-permute-start.6) | collective-permute-done | bytes 131104 | tf_op jit(solution)/shard_map/ppermute | solution.py:322
  46.7 1.6 %collective-permute-start.25 = (f32[2,256,128]{2,1,0:T(8,128)S(1)}, f32[2,256,128]{2,1,0:T(8,128)S(1)}, u32[]{:S(2)}, u32[]{:S(2)}) collective-permute-start(f32[2,256,128]{2,1,0:T(8,128)S(1)} %collective-permute-done.11.held), channel_id=1, source_target_pairs={{0,4},{4,0},{8,12},{12,8},{16,20},{20,16},{24,28},{28,24},{1,5},{5... | collective-permute-start | bytes 786440 | tf_op jit(solution)/shard_map/ppermute | solution.py:318
  48.3 3.6 %first_panel.1.x_ref = f32[128,1024]{1,0:T(8,128)S(1)} custom-call(s32[2]{0:T(128)S(1)} %pad_add_fusion.place_ref, f32[2,32,1024]{2,1,0:T(8,128)S(1)} %pad_maximum_fusion.1.pair, f32[2,32,1024]{2,1,0:T(8,128)S(1)} %collective-permute-done.12.other_pair, f32[2,264,128]{2,1,0:T(8,128)S(1)} %pad_maximum_fusion.refs_0_, ...), custom_call_target="tpu_custom_call" | custom-call | flops 200000000 | bytes 2097152 | tf_op jit(solution)/shard_map/first_panel/pallas_call | solution.py:412
  51.9 0.9 %near_update.1.near = f32[128,256]{1,0:T(8,128)S(1)} custom-call(s32[2]{0:T(128)S(1)} %pad_add_fusion.place_ref, f32[128,1024]{1,0:T(8,128)S(1)} %first_panel.1.x_ref, f32[2,256,128]{2,1,0:T(8,128)S(1)} %pad_maximum_fusion.2.held, f32[2,256,128]{2,1,0:T(8,128)S(1)} %collective-permute-done.13.got), custom_call_target="tpu_custom_call" | custom-call | flops 10000000 | bytes 2097152 | tf_op jit(solution)/shard_map/near_update/pallas_call | solution.py:423
  52.8 2.3 %collective-permute-done.25.got = f32[2,256,128]{2,1,0:T(8,128)S(1)} collective-permute-done((f32[2,256,128]{2,1,0:T(8,128)S(1)}, f32[2,256,128]{2,1,0:T(8,128)S(1)}, u32[]{:S(2)}, u32[]{:S(2)}) %collective-permute-start.25) | collective-permute-done | bytes 262176 | tf_op jit(solution)/shard_map/ppermute | solution.py:318
  55.0 0.9 %update.1 = (f32[32,256]{1,0:T(8,128)S(1)}, f32[32,256]{1,0:T(8,128)S(1)}, f32[32,256]{1,0:T(8,128)S(1)}, f32[32,256]{1,0:T(8,128)S(1)}) custom-call(s32[2]{0:T(128)S(1)} %pad_add_fusion.place_ref, f32[128,1024]{1,0:T(8,128)S(1)} %first_panel.1.x_ref, f32[128,256]{1,0:T(8,128)S(1)} %near_update.1.near, f32[2,256,128]{2,1,0:T(8,128)S(1)} %collective-permute-done.11.held, ...), custom_call_target="tpu_custom_call" | custom-call | flops 2000000000 | bytes 2097152 | tf_op jit(solution)/shard_map/update/pallas_call | solution.py:426
  55.9 1.4 %collective-permute-start.26 = (f32[32,256]{1,0:T(8,128)S(1)}, f32[32,256]{1,0:T(8,128)S(1)}, u32[]{:S(2)}, u32[]{:S(2)}) collective-permute-start(f32[32,256]{1,0:T(8,128)S(1)} %get-tuple-element.66), channel_id=1, source_target_pairs={{0,2},{1,3},{2,0},{3,1},{4,6},{5,7},{6,4},{7,5},{8,10},{9,11},{10,... | collective-permute-start | bytes 98312 | tf_op jit(solution)/shard_map/ppermute | solution.py:322
  58.1 2.9 %second_factor.1 = (bf16[1024,1024]{1,0:T(8,128)(2,1)S(1)}, bf16[1024,1024]{1,0:T(8,128)(2,1)S(1)}) custom-call(s32[2]{0:T(128)S(1)} %pad_add_fusion.place_ref, f32[2,264,128]{2,1,0:T(8,128)S(1)} %pad_maximum_fusion.refs_0_, f32[2,264,128]{2,1,0:T(8,128)S(1)} %collective-permute-done.8.refs_1_, f32[2,264,128]{2,1,0:T(8,128)S(1)} %collective-permute-done.9.refs_2_, ...), custom_call_target="tpu_custom_call" | custom-call | flops 3000000000 | bytes 2097152 | tf_op jit(solution)/shard_map/second_factor/pallas_call | solution.py:438
  61.0 2.0 %second_panel.1 = f32[32,2048]{1,0:T(8,128)} custom-call(s32[2]{0:T(128)S(1)} %pad_add_fusion.place_ref, f32[128,1024]{1,0:T(8,128)S(1)} %first_panel.1.x_ref, f32[2,32,1024]{2,1,0:T(8,128)S(1)} %get-tuple-element.61.both_ref, bf16[1024,1024]{1,0:T(8,128)(2,1)S(1)} %get-tuple-element.64.uh_ref, bf16[1024,1024]{1,0:T(8,128)(2,1)S(1)} %get-tuple-element.65.ul_ref, ...), custom_call_target="tpu_custom_call" | custom-call | flops 2500000000 | bytes 2097152 | tf_op jit(solution)/shard_map/second_panel/pallas_call | solution.py:442
  (55 shorter events, 9.4 us)
Async XLA Ops:
  4.2 8.9 %collective-permute-start.1 = (f32[264,128]{1,0:T(8,128)S(1)}, f32[264,128]{1,0:T(8,128)S(1)}, u32[]{:S(2)}, u32[]{:S(2)}) collective-permute-start(f32[264,128]{1,0:T(8,128)S(1)} %invert.1), channel_id=1, source_target_pairs={{0,16},{4,20},{8,24},{12,28},{16,0},{20,4},{24,8},{28,12},{1,17},{... | collective-permute-start | bytes 405512 | tf_op jit(solution)/shard_map/ppermute | solution.py:314
  13.1 7.4 %collective-permute-start.8 = (f32[2,264,128]{2,1,0:T(8,128)S(1)}, f32[2,264,128]{2,1,0:T(8,128)S(1)}, u32[]{:S(2)}, u32[]{:S(2)}) collective-permute-start(f32[2,264,128]{2,1,0:T(8,128)S(1)} %pad_maximum_fusion.refs_0_), channel_id=1, source_target_pairs={{0,4},{4,0},{8,12},{12,8},{16,20},{20,16},{24,28},{28,24},{1,5},{5... | collective-permute-start | bytes 811016 | tf_op jit(solution)/shard_map/ppermute | solution.py:318
  15.2 9.8 %collective-permute-start.9 = (f32[2,264,128]{2,1,0:T(8,128)S(1)}, f32[2,264,128]{2,1,0:T(8,128)S(1)}, u32[]{:S(2)}, u32[]{:S(2)}) collective-permute-start(f32[2,264,128]{2,1,0:T(8,128)S(1)} %pad_maximum_fusion.refs_0_), channel_id=1, source_target_pairs={{0,2},{1,3},{2,0},{3,1},{4,6},{5,7},{6,4},{7,5},{8,10},{9,11},{10,... | collective-permute-start | bytes 811016 | tf_op jit(solution)/shard_map/ppermute | solution.py:322
  16.7 9.0 %collective-permute-start.2 = (f32[2,264,128]{2,1,0:T(8,128)S(1)}, f32[2,264,128]{2,1,0:T(8,128)S(1)}, u32[]{:S(2)}, u32[]{:S(2)}) collective-permute-start(f32[2,264,128]{2,1,0:T(8,128)S(1)} %pad_maximum_fusion.refs_0_), channel_id=1, source_target_pairs={{0,8},{4,12},{8,0},{12,4},{16,24},{20,28},{24,16},{28,20},{1,9},{5... | collective-permute-start | bytes 811016 | tf_op jit(solution)/shard_map/ppermute | solution.py:314
  16.7 8.2 %collective-permute-start.7 = (f32[256,128]{1,0:T(8,128)S(1)}, f32[256,128]{1,0:T(8,128)S(1)}, u32[]{:S(2)}, u32[]{:S(2)}) collective-permute-start(f32[256,128]{1,0:T(8,128)S(1)} %copy-done.3), channel_id=1, source_target_pairs={{0,16},{4,20},{8,24},{12,28},{16,0},{20,4},{24,8},{28,12},{1,17},{... | collective-permute-start | bytes 393224 | tf_op jit(solution)/shard_map/ppermute | solution.py:314
  19.9 5.0 %collective-permute-start = (f32[4,32,256]{2,1,0:T(8,128)S(1)}, f32[4,32,256]{2,1,0:T(8,128)S(1)}, u32[]{:S(2)}, u32[]{:S(2)}) collective-permute-start(f32[4,32,256]{2,1,0:T(8,128)S(1)} %leave.1), channel_id=1, source_target_pairs={{0,4},{4,0},{8,12},{12,8},{16,20},{20,16},{24,28},{28,24},{1,5},{5... | collective-permute-start | bytes 393224 | tf_op jit(solution)/shard_map/ppermute | solution.py:318
  20.5 11.8 %collective-permute-start.14 = (f32[2,264,128]{2,1,0:T(8,128)S(1)}, f32[2,264,128]{2,1,0:T(8,128)S(1)}, u32[]{:S(2)}, u32[]{:S(2)}) collective-permute-start(f32[2,264,128]{2,1,0:T(8,128)S(1)} %collective-permute-done.8.refs_1_), channel_id=1, source_target_pairs={{0,2},{1,3},{2,0},{3,1},{4,6},{5,7},{6,4},{7,5},{8,10},{9,11},{10,... | collective-permute-start | bytes 811016 | tf_op jit(solution)/shard_map/ppermute | solution.py:322
  25.6 8.1 %collective-permute-start.10 = (f32[2,264,128]{2,1,0:T(8,128)S(1)}, f32[2,264,128]{2,1,0:T(8,128)S(1)}, u32[]{:S(2)}, u32[]{:S(2)}) collective-permute-start(f32[2,264,128]{2,1,0:T(8,128)S(1)} %collective-permute-done.2.refs_4_), channel_id=1, source_target_pairs={{0,2},{4,6},{8,10},{12,14},{16,18},{20,22},{24,26},{28,30},{1,5},{... | collective-permute-start | bytes 811016 | tf_op jit(solution)/shard_map/ppermute | solution.py:331
  26.3 9.0 %collective-permute-start.15 = (f32[2,264,128]{2,1,0:T(8,128)S(1)}, f32[2,264,128]{2,1,0:T(8,128)S(1)}, u32[]{:S(2)}, u32[]{:S(2)}) collective-permute-start(f32[2,264,128]{2,1,0:T(8,128)S(1)} %collective-permute-done.2.refs_4_), channel_id=1, source_target_pairs={{0,4},{4,0},{8,12},{12,8},{16,20},{20,16},{24,28},{28,24},{1,3},{5... | collective-permute-start | bytes 811016 | tf_op jit(solution)/shard_map/ppermute | solution.py:331
  27.2 11.0 %collective-permute-start.3 = (f32[2,32,256]{2,1,0:T(8,128)S(1)}, f32[2,32,256]{2,1,0:T(8,128)S(1)}, u32[]{:S(2)}, u32[]{:S(2)}) collective-permute-start(f32[2,32,256]{2,1,0:T(8,128)S(1)} %get-tuple-element.39), channel_id=1, source_target_pairs={{0,8},{4,12},{8,0},{12,4},{16,24},{20,28},{24,16},{28,20},{1,9},{5... | collective-permute-start | bytes 196616 | tf_op jit(solution)/shard_map/ppermute | solution.py:314
  30.7 8.0 %collective-permute-start.4 = (f32[2,32,256]{2,1,0:T(8,128)S(1)}, f32[2,32,256]{2,1,0:T(8,128)S(1)}, u32[]{:S(2)}, u32[]{:S(2)}) collective-permute-start(f32[2,32,256]{2,1,0:T(8,128)S(1)} %get-tuple-element.41), channel_id=1, source_target_pairs={{0,16},{4,20},{8,24},{12,28},{16,0},{20,4},{24,8},{28,12},{1,17},{... | collective-permute-start | bytes 196616 | tf_op jit(solution)/shard_map/ppermute | solution.py:314
  32.3 6.4 %collective-permute-start.5 = (f32[2,32,256]{2,1,0:T(8,128)S(1)}, f32[2,32,256]{2,1,0:T(8,128)S(1)}, u32[]{:S(2)}, u32[]{:S(2)}) collective-permute-start(f32[2,32,256]{2,1,0:T(8,128)S(1)} %get-tuple-element.43), channel_id=1, source_target_pairs={{0,24},{4,28},{8,16},{12,20},{16,8},{20,12},{24,0},{28,4},{1,25},{... | collective-permute-start | bytes 196616 | tf_op jit(solution)/shard_map/ppermute | solution.py:314
  33.8 7.0 %collective-permute-start.13 = (f32[2,256,128]{2,1,0:T(8,128)S(1)}, f32[2,256,128]{2,1,0:T(8,128)S(1)}, u32[]{:S(2)}, u32[]{:S(2)}) collective-permute-start(f32[2,256,128]{2,1,0:T(8,128)S(1)} %pad_maximum_fusion.2.held), channel_id=1, source_target_pairs={{0,4},{4,0},{8,12},{12,8},{16,20},{20,16},{24,28},{28,24},{1,5},{5... | collective-permute-start | bytes 786440 | tf_op jit(solution)/shard_map/ppermute | solution.py:318
  35.3 9.1 %collective-permute-start.11 = (f32[2,256,128]{2,1,0:T(8,128)S(1)}, f32[2,256,128]{2,1,0:T(8,128)S(1)}, u32[]{:S(2)}, u32[]{:S(2)}) collective-permute-start(f32[2,256,128]{2,1,0:T(8,128)S(1)} %pad_maximum_fusion.2.held), channel_id=1, source_target_pairs={{0,8},{4,12},{8,0},{12,4},{16,24},{20,28},{24,16},{28,20},{1,9},{5... | collective-permute-start | bytes 786440 | tf_op jit(solution)/shard_map/ppermute | solution.py:314
  38.2 6.7 %collective-permute-start.16 = (f32[2,264,128]{2,1,0:T(8,128)S(1)}, f32[2,264,128]{2,1,0:T(8,128)S(1)}, u32[]{:S(2)}, u32[]{:S(2)}) collective-permute-start(f32[2,264,128]{2,1,0:T(8,128)S(1)} %collective-permute-done.10.refs_5_), channel_id=1, source_target_pairs={{0,4},{4,0},{8,12},{12,8},{16,20},{20,16},{24,28},{28,24},{1,3},{5... | collective-permute-start | bytes 811016 | tf_op jit(solution)/shard_map/ppermute | solution.py:331
  39.3 5.0 %collective-permute-start.6 = (f32[32,1024]{1,0:T(8,128)S(1)}, f32[32,1024]{1,0:T(8,128)S(1)}, u32[]{:S(2)}, u32[]{:S(2)}) collective-permute-start(f32[32,1024]{1,0:T(8,128)S(1)} %get-tuple-element.45), channel_id=1, source_target_pairs={{0,2},{1,3},{2,0},{3,1},{4,6},{5,7},{6,4},{7,5},{8,10},{9,11},{10,... | collective-permute-start | bytes 393224 | tf_op jit(solution)/shard_map/ppermute | solution.py:322
  40.7 4.3 %collective-permute-start.17 = (f32[2,264,128]{2,1,0:T(8,128)S(1)}, f32[2,264,128]{2,1,0:T(8,128)S(1)}, u32[]{:S(2)}, u32[]{:S(2)}) collective-permute-start(f32[2,264,128]{2,1,0:T(8,128)S(1)} %pad_maximum_fusion.refs_0_), channel_id=1, source_target_pairs={{0,1},{1,0},{2,3},{3,2},{4,5},{5,4},{6,7},{7,6},{8,9},{9,8},{10,11... | collective-permute-start | bytes 811016 | tf_op jit(solution)/shard_map/ppermute | solution.py:322
  40.7 4.8 %collective-permute-start.18 = (f32[2,264,128]{2,1,0:T(8,128)S(1)}, f32[2,264,128]{2,1,0:T(8,128)S(1)}, u32[]{:S(2)}, u32[]{:S(2)}) collective-permute-start(f32[2,264,128]{2,1,0:T(8,128)S(1)} %collective-permute-done.8.refs_1_), channel_id=1, source_target_pairs={{0,1},{1,0},{2,3},{3,2},{4,5},{5,4},{6,7},{7,6},{8,9},{9,8},{10,11... | collective-permute-start | bytes 811016 | tf_op jit(solution)/shard_map/ppermute | solution.py:322
  45.0 3.3 %collective-permute-start.21 = (f32[2,264,128]{2,1,0:T(8,128)S(1)}, f32[2,264,128]{2,1,0:T(8,128)S(1)}, u32[]{:S(2)}, u32[]{:S(2)}) collective-permute-start(f32[2,264,128]{2,1,0:T(8,128)S(1)} %collective-permute-done.2.refs_4_), channel_id=1, source_target_pairs={{0,1},{1,0},{2,3},{3,2},{4,5},{5,4},{6,7},{7,6},{8,9},{9,8},{10,11... | collective-permute-start | bytes 811016 | tf_op jit(solution)/shard_map/ppermute | solution.py:322
  45.5 2.8 %collective-permute-start.22 = (f32[2,264,128]{2,1,0:T(8,128)S(1)}, f32[2,264,128]{2,1,0:T(8,128)S(1)}, u32[]{:S(2)}, u32[]{:S(2)}) collective-permute-start(f32[2,264,128]{2,1,0:T(8,128)S(1)} %collective-permute-done.10.refs_5_), channel_id=1, source_target_pairs={{0,1},{1,0},{2,3},{3,2},{4,5},{5,4},{6,7},{7,6},{8,9},{9,8},{10,11... | collective-permute-start | bytes 811016 | tf_op jit(solution)/shard_map/ppermute | solution.py:322
  46.7 8.4 %collective-permute-start.25 = (f32[2,256,128]{2,1,0:T(8,128)S(1)}, f32[2,256,128]{2,1,0:T(8,128)S(1)}, u32[]{:S(2)}, u32[]{:S(2)}) collective-permute-start(f32[2,256,128]{2,1,0:T(8,128)S(1)} %collective-permute-done.11.held), channel_id=1, source_target_pairs={{0,4},{4,0},{8,12},{12,8},{16,20},{20,16},{24,28},{28,24},{1,5},{5... | collective-permute-start | bytes 786440 | tf_op jit(solution)/shard_map/ppermute | solution.py:318
  55.9 5.1 %collective-permute-start.26 = (f32[32,256]{1,0:T(8,128)S(1)}, f32[32,256]{1,0:T(8,128)S(1)}, u32[]{:S(2)}, u32[]{:S(2)}) collective-permute-start(f32[32,256]{1,0:T(8,128)S(1)} %get-tuple-element.66), channel_id=1, source_target_pairs={{0,2},{1,3},{2,0},{3,1},{4,6},{5,7},{6,4},{7,5},{8,10},{9,11},{10,... | collective-permute-start | bytes 98312 | tf_op jit(solution)/shard_map/ppermute | solution.py:322
  57.3 3.7 %collective-permute-start.27 = (f32[32,256]{1,0:T(8,128)S(1)}, f32[32,256]{1,0:T(8,128)S(1)}, u32[]{:S(2)}, u32[]{:S(2)}) collective-permute-start(f32[32,256]{1,0:T(8,128)S(1)} %get-tuple-element.67), channel_id=1, source_target_pairs={{0,1},{1,0},{2,3},{3,2},{4,5},{5,4},{6,7},{7,6},{8,9},{9,8},{10,11... | collective-permute-start | bytes 98312 | tf_op jit(solution)/shard_map/ppermute | solution.py:322
  57.3 3.7 %collective-permute-start.28 = (f32[32,256]{1,0:T(8,128)S(1)}, f32[32,256]{1,0:T(8,128)S(1)}, u32[]{:S(2)}, u32[]{:S(2)}) collective-permute-start(f32[32,256]{1,0:T(8,128)S(1)} %get-tuple-element.68), channel_id=1, source_target_pairs={{0,3},{1,2},{2,1},{3,0},{4,7},{5,6},{6,5},{7,4},{8,11},{9,10},{10,... | collective-permute-start | bytes 98312 | tf_op jit(solution)/shard_map/ppermute | solution.py:322
  (9 other events, 43.9 us)
